TPU v7x, 128 devices: a whole 4x4x4 slice. The times are simulated.
128 devices in a mesh: dp: 16 (over z, y), tensor: 8 (over x, core).
Axes of the slice: x: 4, y: 4, z: 4, core: 2. Of those that a mesh axis runs over, the one named last changes fastest.
Arguments:
- query: bfloat16 [8192, 8192], P('dp', 'tensor'), may hold values from -80 to 80
- new_key: bfloat16 [8192, 1024], P('dp', 'tensor'), may hold values from -4 to 4
- new_value: bfloat16 [8192, 1024], P('dp', 'tensor'), may hold values from -8 to 8
- cache_keys: bfloat16 [8192, 16, 1024], P('dp', None, 'tensor'), may hold values from -4 to 4
- cache_values: bfloat16 [8192, 16, 1024], P('dp', None, 'tensor'), may hold values from -6 to 6
- lengths: int32 [8192], P('dp'), may hold values from 2 to 16
- adapter_ids: int32 [8192, 1], P('dp'), may hold values from 0 to 255; in each aligned block of 512 rows (0 to 511, 512 to 1023, ...) at most 8 rows name the same one
- out_weight: bfloat16 [8192, 8192], P('tensor'), may hold values from -0.0625 to 0.0625
- adapter_a: bfloat16 [256, 8192, 64], P('dp', 'tensor'), may hold values from -0.0625 to 0.0625
- adapter_b: bfloat16 [256, 64, 8192], P('dp', None, 'tensor'), may hold values from -0.75 to 0.75
Outputs:
- projected: bfloat16 [8192, 8192], P('dp', 'tensor')
Inputs may be any that keep to these rules, and one draw needn't show every extreme that they name: `adapter_ids`: in each aligned block of 512 rows no adapter is named by more than 8 rows, a bound that some block reaches.
All inputs are finite; a program needn't handle non-finite values.
Results may differ from a plain program's by a relative error of at most 0.015.
Values may be sent and summed in bfloat16 or wider, within the bound.
No kernel may reach another device: no remote copies, remote signals or barrier semaphores. Data moves between devices by JAX's collectives and lax.ppermute only.
A program may use at most 128 MiB of HBM per device.

v0:
```python
import jax
import jax.numpy as jnp
from jax import lax
from jax.sharding import PartitionSpec as P

HEADS = 64
KVH = 8
HD = 128
MOST = 8


def attend(query, new_key, new_value, cache_keys, cache_values, lengths):
    rows = query.shape[0]
    slots = cache_keys.shape[1]
    kv_local = new_key.shape[1] // HD
    group = HEADS // KVH
    scale = 1.0 / HD**0.5
    queries = query.reshape(rows, kv_local, group, HD)
    keys = cache_keys.reshape(rows, slots, kv_local, HD)
    values = cache_values.reshape(rows, slots, kv_local, HD)
    own_key = new_key.reshape(rows, kv_local, HD)
    own_value = new_value.reshape(rows, kv_local, HD)
    scores = (
        jnp.einsum("rkgd,rlkd->rkgl", queries, keys, preferred_element_type=jnp.float32) * scale
    )
    own = jnp.einsum("rkgd,rkd->rkg", queries, own_key, preferred_element_type=jnp.float32) * scale
    live = jnp.arange(slots)[None, :] < lengths[:, None]
    live4 = live[:, None, None, :]
    scores = jnp.where(live4, scores, jnp.float32(-1e30))
    top = jnp.maximum(jnp.max(scores, axis=-1), own)
    expo = jnp.where(live4, jnp.exp(scores - top[..., None]), jnp.float32(0.0))
    expo_own = jnp.exp(own - top)
    total = jnp.sum(expo, axis=-1) + expo_own
    weights = (expo / total[..., None]).astype(jnp.bfloat16)
    weight_own = (expo_own / total).astype(jnp.bfloat16)
    mixed = jnp.einsum("rkgl,rlkd->rkgd", weights, values, preferred_element_type=jnp.float32)
    mixed = (
        mixed
        + weight_own.astype(jnp.float32)[..., None] * own_value.astype(jnp.float32)[:, :, None, :]
    )
    return mixed.astype(jnp.bfloat16).reshape(rows, kv_local * group * HD)


def per_device(
    query,
    new_key,
    new_value,
    cache_keys,
    cache_values,
    lengths,
    adapter_ids,
    out_weight,
    adapter_a,
    adapter_b,
):
    attended = attend(query, new_key, new_value, cache_keys, cache_values, lengths)
    rows, width = attended.shape
    adp_dev = adapter_a.shape[0]
    groups = lax.axis_size("dp")
    all_adapters = adp_dev * groups
    ids = adapter_ids[:, 0]
    onehot = (ids[:, None] == jnp.arange(all_adapters, dtype=jnp.int32)[None, :]).astype(jnp.int32)
    place = jnp.sum((jnp.cumsum(onehot, axis=0) - 1) * onehot, axis=1)
    target = ids * MOST + place
    outgoing = jnp.zeros((all_adapters * MOST, width), jnp.bfloat16).at[target].set(attended)
    outgoing = outgoing.reshape(groups, adp_dev, MOST, width)
    partial_rank = jnp.einsum(
        "samf,afk->samk",
        lax.all_to_all(outgoing, "dp", split_axis=0, concat_axis=0, tiled=True),
        adapter_a,
        preferred_element_type=jnp.float32,
    )
    summed = lax.psum(partial_rank, "tensor").astype(jnp.bfloat16)
    adapted = jnp.einsum(
        "samk,akf->samf", summed, adapter_b, preferred_element_type=jnp.float32
    ).astype(jnp.bfloat16)
    returned = lax.all_to_all(adapted, "dp", split_axis=0, concat_axis=0, tiled=True)
    returned = returned.reshape(all_adapters * MOST, returned.shape[-1])
    delta = returned[target]
    base = lax.psum_scatter(
        lax.dot_general(
            out_weight, attended, (((0,), (1,)), ((), ())), preferred_element_type=jnp.float32
        ),
        "tensor",
        scatter_dimension=0,
        tiled=True,
    ).T
    return (base + delta.astype(jnp.float32)).astype(jnp.bfloat16)


def solution(mesh):
    return jax.shard_map(
        per_device,
        mesh=mesh,
        in_specs=(
            P("dp", "tensor"),
            P("dp", "tensor"),
            P("dp", "tensor"),
            P("dp", None, "tensor"),
            P("dp", None, "tensor"),
            P("dp"),
            P("dp", None),
            P("tensor", None),
            P("dp", "tensor", None),
            P("dp", None, "tensor"),
        ),
        out_specs=P("dp", "tensor"),
        check_vma=False,
    )
```

profile of v0, /device:TPU:0, one launch (start us, length us, event | category | flops | bytes accessed | tf_op | source)
XLA Modules:
  0.0 246.3 jit_solution(6659540058262637577)
XLA Ops:
  6.5 0.0 copy-start
  6.5 0.0 reduce-scatter.2.cloned.1.call-start
  6.5 0.0 copy-start.6
  6.5 1.0 iota_compare_fusion.3
  7.5 1.6 convert_element_type.43
  9.1 1.5 copy.46
  10.6 0.0 copy-done.6
  10.6 0.7 fusion.29
  11.4 0.1 copy.43
  11.5 4.2 %fusion.7 = (f32[512,8]{1,0:T(8,128)S(1)}, f32[512,8,16]{2,1,0:T(8,128)}) fusion(pred[512,16]{1,0:T(8,128)(4,1)S(1)} %iota_compare_fusion.3, bf16[512,8,128]{2,1,0:T(8,128)(2,1)S(1)} %bitcast.70, bf16[512,16,128]{2,1,0:T(8,128)(2,1)} %param.13), kind=kOutput, calls=%fused_computation.16 | convolution fusion | flops 16969728 | bytes 3432448 | tf_op jit(solution)/shard_map/rkgd,rlkd->rkgl/dot_general | solution.py:24
  15.6 0.0 copy-start.3
  15.6 0.1 copy.33
  15.7 0.1 copy.34
  15.9 3.0 %fusion.8 = f32[512,8]{1,0:T(8,128)S(1)} fusion(f32[512,8,16]{2,1,0:T(8,128)} %get-tuple-element.8, f32[512,8]{1,0:T(8,128)S(1)} %copy.34, pred[512,16]{1,0:T(8,128)(4,1)S(1)} %iota_compare_fusion.3), kind=kLoop, calls=%fused_computation.17 | loop fusion | flops 323584 | bytes 303104 | tf_op jit(solution)/shard_map/reduce_sum | solution.py:33
  18.9 0.1 copy.35
  19.0 0.1 copy.36
  19.2 0.1 copy.37
  19.3 0.0 copy-done.3
  19.3 3.4 %add_convert_fusion = bf16[512,8,128]{2,1,0:T(8,128)(2,1)S(1)} fusion(bf16[512,16,128]{2,1,0:T(8,128)(2,1)} %param.14, f32[512,8,16]{2,1,0:T(8,128)} %get-tuple-element.8, f32[512,128]{1,0:T(8,128)S(1)} %copy-done.3, f32[512,8]{1,0:T(8,128)S(1)} %copy.37, f32[512,8]{1,0:T(8,128)S(1)} %copy.36, f32[512,8]{1,0:T(8,128)S(1)} %copy.34, ...), kind=kOutput, calls=%fused_computation.12 | convolution fusion | flops 18743296 | bytes 3727360 | tf_op jit(solution)/shard_map/rkgl,rlkd->rkgd/dot_general | solution.py:36
  22.7 0.0 copy-start.1
  22.7 1.0 copy-done.1
  23.7 15.6 %convolution_bitcast_fusion = f32[8192,512]{0,1:T(8,128)} fusion(bf16[1024,8192]{1,0:T(8,128)(2,1)} %param.17, bf16[64,8,8,128]{3,2,1,0:T(8,128)(2,1)S(1)} %bitcast.72), kind=kOutput, calls=%fused_computation.2 | convolution fusion | flops 8589934592 | bytes 34603008 | tf_op jit(solution)/shard_map/dot_general | solution.py:81
  39.3 0.0 copy-start.4
  39.3 0.0 reduce-scatter.2.cloned.1.call-update
  39.3 0.7 copy-done.4
  39.9 0.1 copy.38
  40.1 0.2 fusion.26
  40.3 0.1 add_add_fusion
  40.4 0.0 copy-start.2
  40.5 0.1 copy.39
  40.6 0.2 fusion.24
  40.8 0.9 copy-done.2
  41.7 5.2 %scatter_custom_fusion = bf16[2048,1024]{1,0:T(8,128)(2,1)} fusion(s32[512]{0:T(512)S(1)} %bitcast.77, bf16[]{:T(256)} %constant.5.clone.1, bf16[64,8,8,128]{3,2,1,0:T(8,128)(2,1)S(1)} %bitcast.73), kind=kCustom, calls=%fused_computation.10 | custom fusion | bytes 5242882 | tf_op jit(solution)/shard_map/scatter | solution.py:65
  46.9 0.0 copy-start.5
  46.9 59.1 %all_to_all.10 = bf16[16,16,8,1024]{3,2,1,0:T(8,128)(2,1)S(1)} all-to-all(bf16[16,16,8,1024]{3,2,1,0:T(8,128)(2,1)} %bitcast.68), channel_id=1, replica_groups=mesh['dp'=16,'tensor'=8] {'dp'}, dimensions={0} | all-to-all | bytes 8388608 | tf_op jit(solution)/shard_map/all_to_all | solution.py:69
  106.0 0.0 copy-done.5
  106.0 2.2 fusion.9
  108.2 56.1 %all-reduce.1 = bf16[16,16,8,64]{3,2,0,1:T(8,128)(2,1)S(1)} all-reduce(f32[16,16,8,64]{3,2,0,1:T(8,128)} %fusion.9), channel_id=1, replica_groups=mesh['dp'=16,'tensor'=8] {'tensor'}, use_global_device_ids=true, to_apply=%region_7.8 | all-reduce | flops 131072 | bytes 786432 | tf_op jit(solution)/shard_map/psum | solution.py:73
  164.3 0.0 copy-done
  164.3 1.2 convert_bitcast_fusion
  165.5 2.4 copy.41
  168.0 4.5 %all-to-all-start.1 = ((bf16[16,16,8,1024]{3,2,1,0:T(8,128)(2,1)}), bf16[16,16,8,1024]{3,2,1,0:T(8,128)(2,1)}, u32[]{:S(2)}, u32[]{:S(2)}) async-start(bf16[16,16,8,1024]{3,2,1,0:T(8,128)(2,1)} %copy.41), calls=%async_computation.2 | async-start | bytes 8388608 | tf_op jit(solution)/shard_map/all_to_all | solution.py:77
  172.5 58.6 %all-to-all-done.1 = bf16[16,16,8,1024]{3,2,1,0:T(8,128)(2,1)} async-done(((bf16[16,16,8,1024]{3,2,1,0:T(8,128)(2,1)}), bf16[16,16,8,1024]{3,2,1,0:T(8,128)(2,1)}, u32[]{:S(2)}, u32[]{:S(2)}) %all-to-all-start.1) | async-done | bytes 4194336 | tf_op jit(solution)/shard_map/all_to_all | solution.py:77
  231.1 5.5 %gather_fusion = bf16[512,1024]{1,0:T(8,128)(2,1)S(1)} fusion(bf16[2048,1024]{1,0:T(8,128)(2,1)} %bitcast.18, s32[1024]{0:T(1024)S(1)} %pad_clamp_fusion), kind=kCustom, calls=%fused_computation | custom fusion | bytes 2099200 | tf_op jit(solution)/shard_map/gather | solution.py:79
  236.6 0.0 reduce-scatter.2.cloned.1.call-done
  236.6 2.9 %fusion.4 = bf16[512,1024]{1,0:T(8,128)(2,1)} fusion(f32[1024,512]{0,1:T(8,128)} %reduce-scatter.2.cloned.1.call-done, bf16[512,1024]{1,0:T(8,128)(2,1)S(1)} %gather_fusion), kind=kLoop, calls=%fused_computation.9 | loop fusion | flops 1572864 | bytes 4194304 | tf_op jit(solution)/shard_map/convert_element_type | solution.py:88
  (7 shorter events, 0.1 us)
Async XLA Ops:
  6.5 157.8 %copy-start = (bf16[16,64,1024]{2,1,0:T(8,128)(2,1)S(1)}, bf16[16,64,1024]{2,1,0:T(8,128)(2,1)}, u32[]{:S(2)}) copy-start(bf16[16,64,1024]{2,1,0:T(8,128)(2,1)} %param.19) | copy-start | bytes 6291460
  6.5 230.0 %reduce-scatter.2.cloned.1.call-start = ((), (), s32[]{:S(2)}) async-start(), calls=%async_computation.3 | async-start | bytes 18874368 | tf_op jit(solution)/shard_map/reduce_scatter | solution.py:80
  6.5 4.1 %copy-start.6 = (bf16[512,128]{1,0:T(8,128)(2,1)S(1)}, bf16[512,128]{1,0:T(8,128)(2,1)}, u32[]{:S(2)}) copy-start(bf16[512,128]{1,0:T(8,128)(2,1)} %param.11) | copy-start | bytes 393220
  15.6 3.7 %copy-start.3 = (f32[512,128]{1,0:T(8,128)S(1)}, f32[512,128]{1,0:T(8,128)}, u32[]{:S(2)}) copy-start(f32[512,128]{1,0:T(8,128)} %convert_element_type.43) | copy-start | bytes 786436
  22.7 1.0 copy-start.1
  39.3 0.7 copy-start.4
  40.4 1.2 copy-start.2
  46.9 59.1 %copy-start.5 = (bf16[16,1024,64]{1,2,0:T(8,128)(2,1)S(1)}, bf16[16,1024,64]{1,2,0:T(8,128)(2,1)}, u32[]{:S(2)}) copy-start(bf16[16,1024,64]{1,2,0:T(8,128)(2,1)} %param.18) | copy-start | bytes 6291460
  168.0 63.1 %all-to-all-start.1 = ((bf16[16,16,8,1024]{3,2,1,0:T(8,128)(2,1)}), bf16[16,16,8,1024]{3,2,1,0:T(8,128)(2,1)}, u32[]{:S(2)}, u32[]{:S(2)}) async-start(bf16[16,16,8,1024]{3,2,1,0:T(8,128)(2,1)} %copy.41), calls=%async_computation.2 | async-start | bytes 8388608 | tf_op jit(solution)/shard_map/all_to_all | solution.py:77
Sparse Core Ops, SparseCore 0:
  39.4 98.0 reduce-scatter.1
where the time goes:
time: 248 us; the launch traced here: 246 us
  blocking collectives  115 us (46%)
  waiting for transfers between devices  58.6 us (24%)
  matrix products  27.3 us (11%)
  local copies, waits for them, and re-layouts  17.9 us (7%)
  between operations  13.6 us (5%)
  other arithmetic  9.17 us (4%)
  starting transfers between devices  4.54 us (2%)
    all_to_all x1, blocking collectives, per_device(): lax.all_to_all(outgoing, 'dp', split_axis=0, concat_axis=0, tiled=True)  59.1 us
    all_to_all x1, waiting for transfers between devices, per_device(): lax.all_to_all(adapted, 'dp', split_axis=0, concat_axis=0, tiled=True)  58.6 us
    psum x1, blocking collectives, per_device(): summed = lax.psum(partial_rank, 'tensor').astype(jnp.bfloat16)  56.1 us
    dot_general x1, matrix products, per_device(): lax.dot_general(out_weight, attended, (((0,), (1,)), ((), ())), preferred...  15.6 us
    gather x1, local copies, waits for them, and re-layouts, per_device(): delta = returned[target]  5.45 us
    scatter x1, local copies, waits for them, and re-layouts, per_device(): jnp.zeros((all_adapters * MOST, width), jnp.bfloat16).at[target]  5.2 us
  transfers between devices with their start and end apart: 2, of which 1 were waited for; matrix products, arithmetic and copies ran while one was open for 7% of the time, Pallas kernels for 0%

commit v1 on v0

v1 whole, which is shorter than its diff:
```python
import functools

import jax
import jax.numpy as jnp
from jax import lax
from jax.experimental import pallas as pl
from jax.experimental.pallas import tpu as pltpu
from jax.sharding import PartitionSpec as P

HD = 128
GROUP = 8
GROUPS = 16
ADP = 16
RANK = 64
SLOTS = 56
TAKES = SLOTS - 1
SENT = GROUPS * SLOTS
HALF = SENT // 2
SUB = 16
F32 = jnp.float32
BF16 = jnp.bfloat16
NT = (((1,), (1,)), ((), ()))
TN = (((0,), (0,)), ((), ()))
NEG = -1e30
VMEM_LIMIT = 50 * 1024 * 1024


def iota(shape, axis):
    return lax.broadcasted_iota(jnp.int32, shape, axis)


def params(**more):
    return pltpu.CompilerParams(vmem_limit_bytes=VMEM_LIMIT, **more)


def places(ids):
    rows = ids.shape[1]
    dst = lax.shift_right_logical(ids, 4)
    member = iota((GROUPS, rows), 0) == dst
    before = (iota((rows, rows), 0) < iota((rows, rows), 1)).astype(F32).astype(BF16)
    member = member.astype(F32)
    count = jnp.dot(member.astype(BF16), before, preferred_element_type=F32)
    place = jnp.sum(member * count, axis=0, keepdims=True)
    fullest = jnp.max(jnp.sum(member, axis=1, keepdims=True), axis=0, keepdims=True)
    return dst, place.astype(jnp.int32), fullest


def slot_of(dst, place, turn):
    at = place - turn * TAKES
    inside = (at >= 0) & (at < TAKES)
    return jnp.where(inside, dst * SLOTS + 1 + at, -1), at, inside


def fill(ids, att_ref, turn, out_ref):
    rows = ids.shape[1]
    dst, place, fullest = places(ids)
    slot, at, inside = slot_of(dst, place, turn)
    home = jnp.where(inside, dst * SLOTS, -1)
    local = (ids & (ADP - 1)).astype(F32)
    lanes = (iota((128, rows), 0) == at + 1).astype(F32).astype(BF16)
    for c in range(SENT // 128):
        row = iota((128, rows), 0) + c * 128
        pick = (row == slot).astype(F32).astype(BF16)
        moved = jnp.dot(pick, att_ref[...], preferred_element_type=F32)
        heads = jnp.where(row == home, local, 0.0).astype(BF16)
        names = lax.dot_general(heads, lanes, NT, preferred_element_type=F32)
        r1 = iota((128, 128), 0) + c * 128
        first = (lax.rem(r1, SLOTS) == 0) & (iota((128, 128), 1) == 0)
        names = names + jnp.where(first, fullest, 0.0)
        here = pl.ds(c * 128, 128)
        out_ref[here, 0:128] = (moved[:, 0:128] + names).astype(BF16)
        out_ref[here, 128:] = moved[:, 128:].astype(BF16)


def attend_kernel(q_ref, nk_ref, nv_ref, k_ref, v_ref, len_ref, ids_ref, att_ref, out_ref, live_ref, *, block):
    step = pl.program_id(0)
    rows = len_ref.shape[1]
    subs = rows // SUB
    wide = SUB * SUB
    scale = 1.0 / HD**0.5

    @pl.when(step == 0)
    def _():
        lens = len_ref[...].astype(F32)
        own = jnp.where(lax.shift_right_logical(iota((subs, rows), 1), 4) == iota((subs, rows), 0), lens, 0.0)
        spread = (iota((rows, wide), 0) & (SUB - 1)) == lax.shift_right_logical(iota((rows, wide), 1), 4)
        length = jnp.dot(own.astype(BF16), spread.astype(F32).astype(BF16), preferred_element_type=F32)
        slot = (iota((subs, wide), 1) & (SUB - 1)).astype(F32)
        live_ref[...] = jnp.where(slot < length, 0.0, NEG)

    across = iota((GROUP * SUB, wide), 0) & (SUB - 1)
    diagonal = jnp.where(across == lax.shift_right_logical(iota((GROUP * SUB, wide), 1), 4), 0.0, NEG)
    for sub in range(block // SUB):
        here = pl.ds(sub * SUB, SUB)
        there = pl.ds(pl.multiple_of(step * block + sub * SUB, SUB), SUB)
        q = jnp.concatenate([q_ref[here, h * HD : (h + 1) * HD] for h in range(GROUP)], axis=0)
        k = k_ref[here].reshape(wide, HD)
        v = v_ref[here].reshape(wide, HD)
        nk = nk_ref[here, :].astype(F32)
        nv = nv_ref[here, :].astype(F32)
        live = live_ref[pl.ds(step * (block // SUB) + sub, 1), :]
        s = lax.dot_general(q, k, NT, preferred_element_type=F32) + diagonal + live
        own = jnp.sum(q.astype(F32) * jnp.concatenate([nk] * GROUP, axis=0), axis=1, keepdims=True)
        top = jnp.maximum(jnp.max(s, axis=1, keepdims=True), own)
        e = jnp.exp((s - top) * scale)
        e_own = jnp.exp((own - top) * scale)
        total = jnp.sum(e, axis=1, keepdims=True) + e_own
        mixed = jnp.dot(e.astype(BF16), v, preferred_element_type=F32)
        mixed = (mixed + e_own * jnp.concatenate([nv] * GROUP, axis=0)) * (1.0 / total)
        mixed = mixed.astype(BF16)
        for h in range(GROUP):
            att_ref[there, h * HD : (h + 1) * HD] = mixed[h * SUB : (h + 1) * SUB, :]

    @pl.when(step == pl.num_programs(0) - 1)
    def _():
        fill(ids_ref[...], att_ref, 0, out_ref)


def attend(query, new_key, new_value, cache_keys, cache_values, lengths, ids):
    rows, width = query.shape
    slots = cache_keys.shape[1]
    block = 64
    whole = lambda i: (0, 0)
    return pl.pallas_call(
        functools.partial(attend_kernel, block=block),
        grid=(rows // block,),
        in_specs=[
            pl.BlockSpec((block, width), lambda i: (i, 0)),
            pl.BlockSpec((block, HD), lambda i: (i, 0)),
            pl.BlockSpec((block, HD), lambda i: (i, 0)),
            pl.BlockSpec((block, slots, HD), lambda i: (i, 0, 0)),
            pl.BlockSpec((block, slots, HD), lambda i: (i, 0, 0)),
            pl.BlockSpec((1, rows), whole),
            pl.BlockSpec((1, rows), whole),
        ],
        out_specs=[pl.BlockSpec((rows, width), whole), pl.BlockSpec((SENT, width), whole)],
        out_shape=[jax.ShapeDtypeStruct((rows, width), BF16), jax.ShapeDtypeStruct((SENT, width), BF16)],
        scratch_shapes=[pltpu.VMEM((rows // SUB, SUB * SUB), F32)],
        compiler_params=params(dimension_semantics=("arbitrary",)),
        name="attend",
    )(query, new_key, new_value, cache_keys, cache_values, lengths, ids)


def refill_kernel(turn_ref, ids_ref, att_ref, out_ref):
    fill(ids_ref[...], att_ref, turn_ref[0], out_ref)


def refill(turn, ids, attended):
    return pl.pallas_call(
        refill_kernel,
        in_specs=[pl.BlockSpec(memory_space=pltpu.SMEM)] + [pl.BlockSpec(memory_space=pltpu.VMEM)] * 2,
        out_specs=pl.BlockSpec(memory_space=pltpu.VMEM),
        out_shape=jax.ShapeDtypeStruct((SENT, attended.shape[1]), BF16),
        compiler_params=params(),
        name="refill",
    )(turn, ids, attended)


def both_halves(x):
    return pltpu.roll(x, RANK, 1)


def rank_kernel(x_ref, a_ref, part_ref, name_ref, acc_ref):
    first = iota((128, SENT), 1)
    for c in range(SENT // 128):
        here = pl.ds(c * 128, 128)
        row = iota((128, 1), 0) + c * 128
        block = lax.div(row, SLOTS)
        pick = (first == block * SLOTS).astype(F32).astype(BF16)
        heads = jnp.dot(pick, x_ref[:, 0:128], preferred_element_type=F32)
        at = iota((128, 128), 1) == row - block * SLOTS
        name = jnp.sum(jnp.where(at, heads, 0.0), axis=1, keepdims=True).astype(jnp.int32)
        name_ref[here, :] = jnp.broadcast_to(name, (128, 128))
    upper = (iota((SENT, 128), 1) >= RANK).astype(jnp.int32)
    for n in range(ADP * RANK // 256):
        full = lax.dot_general(x_ref[...], a_ref[n * 256 : (n + 1) * 256, :], NT, preferred_element_type=F32)
        name = name_ref[...]
        part = jnp.where(name == upper + 4 * n, full[:, 0:128], 0.0)
        part = part + jnp.where(name == upper + (4 * n + 2), full[:, 128:256], 0.0)
        if n == 0:
            acc_ref[...] = part
        else:
            acc_ref[...] += part
    total = acc_ref[...]
    total = total + both_halves(total)
    low = iota((HALF, 128), 1) < RANK
    part_ref[...] = jnp.where(low, total[0:HALF], total[HALF:]).astype(BF16)


def rank_parts(arrived, down):
    return pl.pallas_call(
        rank_kernel,
        in_specs=[pl.BlockSpec(memory_space=pltpu.VMEM)] * 2,
        out_specs=[pl.BlockSpec(memory_space=pltpu.VMEM)] * 2,
        out_shape=[jax.ShapeDtypeStruct((HALF, 128), BF16), jax.ShapeDtypeStruct((SENT, 128), jnp.int32)],
        scratch_shapes=[pltpu.VMEM((SENT, 128), F32)],
        compiler_params=params(),
        name="rank_parts",
    )(arrived, down)


def delta_kernel(p0_ref, p1_ref, p2_ref, p3_ref, name_ref, b_ref, out_ref, wide_ref):
    rank = (p0_ref[...].astype(F32) + p1_ref[...].astype(F32)) + (p2_ref[...].astype(F32) + p3_ref[...].astype(F32))
    rank = rank.astype(BF16).astype(F32)
    other = both_halves(rank)
    low = iota((HALF, 128), 1) < RANK
    for half in range(2):
        here = pl.ds(half * HALF, HALF)
        own = jnp.where(low, rank, other) if half == 0 else jnp.where(low, other, rank)
        name = name_ref[here, :]
        upper = (iota((HALF, 128), 1) >= RANK).astype(jnp.int32)
        for t in range(ADP * RANK // 128):
            wide_ref[here, t * 128 : (t + 1) * 128] = jnp.where(name == upper + 2 * t, own, 0.0).astype(BF16)
    for n in range(out_ref.shape[1] // 256):
        cols = slice(n * 256, (n + 1) * 256)
        out_ref[:, cols] = jnp.dot(wide_ref[...], b_ref[:, cols], preferred_element_type=F32).astype(BF16)


def deltas(parts, names, up):
    return pl.pallas_call(
        delta_kernel,
        in_specs=[pl.BlockSpec(memory_space=pltpu.VMEM)] * 6,
        out_specs=pl.BlockSpec(memory_space=pltpu.VMEM),
        out_shape=jax.ShapeDtypeStruct((SENT, up.shape[1]), BF16),
        scratch_shapes=[pltpu.VMEM((SENT, ADP * RANK), BF16)],
        compiler_params=params(),
        name="deltas",
    )(*parts, names, up)


def base_kernel(at_ref, att_ref, wt_ref, wm_ref, theirs_ref, mine_ref):
    theirs_ref[...] = jnp.dot(att_ref[...], wt_ref[...], preferred_element_type=F32).astype(BF16)
    mine_ref[...] = jnp.dot(att_ref[...], wm_ref[...], preferred_element_type=F32).astype(BF16)


def base_parts(attended, weight, theirs, mine, cols):
    rows, width = attended.shape
    piece = 512
    per = cols // piece
    at = jnp.stack([theirs, mine]).astype(jnp.int32)
    return pl.pallas_call(
        base_kernel,
        grid_spec=pltpu.PrefetchScalarGridSpec(
            num_scalar_prefetch=1,
            grid=(per,),
            in_specs=[
                pl.BlockSpec((rows, width), lambda j, at: (0, 0)),
                pl.BlockSpec((width, piece), lambda j, at: (0, at[0] * per + j)),
                pl.BlockSpec((width, piece), lambda j, at: (0, at[1] * per + j)),
            ],
            out_specs=[pl.BlockSpec((rows, piece), lambda j, at: (0, j))] * 2,
        ),
        out_shape=[jax.ShapeDtypeStruct((rows, cols), BF16)] * 2,
        compiler_params=params(dimension_semantics=("arbitrary",)),
        cost_estimate=pl.CostEstimate(
            flops=4 * rows * width * cols, bytes_accessed=4 * width * cols + 6 * rows * cols, transcendentals=0
        ),
        name="base_parts",
    )(at, attended, weight, weight)


def take(ids_ref, turn, back_ref):
    dst, place, _ = places(ids_ref[...])
    slot, _, inside = slot_of(dst, place, turn)
    pick = (iota((SENT, ids_ref.shape[1]), 0) == slot).astype(F32).astype(BF16)
    return lax.dot_general(pick, back_ref[...], TN, preferred_element_type=F32).astype(BF16).astype(F32)


def finish_kernel(ids_ref, back_ref, mine_ref, swapped_ref, ltop_ref, lbot_ref, rtop_ref, rbot_ref, out_ref):
    base = mine_ref[...].astype(F32) + swapped_ref[...].astype(F32)
    delta = take(ids_ref, 0, back_ref)
    half = ltop_ref.shape[0]
    top = base[0:half] + (ltop_ref[...].astype(F32) + rtop_ref[...].astype(F32))
    bot = base[half:] + (lbot_ref[...].astype(F32) + rbot_ref[...].astype(F32))
    out_ref[0:half, :] = (top + delta[0:half]).astype(BF16)
    out_ref[half:, :] = (bot + delta[half:]).astype(BF16)


def finish(ids, back, *parts):
    rows, cols = parts[0].shape
    return pl.pallas_call(
        finish_kernel,
        in_specs=[pl.BlockSpec(memory_space=pltpu.VMEM)] * (2 + len(parts)),
        out_specs=pl.BlockSpec(memory_space=pltpu.VMEM),
        out_shape=jax.ShapeDtypeStruct((rows, cols), BF16),
        compiler_params=params(),
        name="finish",
    )(ids, back, *parts)


def add_kernel(turn_ref, ids_ref, back_ref, so_far_ref, out_ref):
    delta = take(ids_ref, turn_ref[0], back_ref)
    out_ref[...] = (so_far_ref[...].astype(F32) + delta).astype(BF16)


def add_turn(turn, ids, back, so_far):
    return pl.pallas_call(
        add_kernel,
        in_specs=[pl.BlockSpec(memory_space=pltpu.SMEM)] + [pl.BlockSpec(memory_space=pltpu.VMEM)] * 3,
        out_specs=pl.BlockSpec(memory_space=pltpu.VMEM),
        out_shape=jax.ShapeDtypeStruct(so_far.shape, BF16),
        compiler_params=params(),
        name="add_turn",
    )(turn, ids, back, so_far)


def add16(a, b):
    return (a.astype(F32) + b.astype(F32)).astype(BF16)


def per_device(
    query, new_key, new_value, cache_keys, cache_values, lengths, adapter_ids, out_weight, adapter_a, adapter_b
):
    tensor = lax.axis_size("tensor")
    chips = tensor // 2
    cols = out_weight.shape[1] // tensor
    me = lax.axis_index("tensor")
    chip, core = me // 2, me % 2
    swap = [(i, i ^ 1) for i in range(tensor)]
    along = lambda by: [(i, (i + 2 * by) % tensor) for i in range(tensor)]
    right, left, across = along(1), along(-1), along(2)
    send = lambda x, perm: lax.ppermute(x, "tensor", perm)

    ids = adapter_ids.reshape(1, adapter_ids.shape[0])
    lens = lengths.reshape(1, lengths.shape[0])
    down = jnp.transpose(adapter_a, (0, 2, 1)).reshape(ADP * RANK, adapter_a.shape[1])
    up = adapter_b.reshape(ADP * RANK, adapter_b.shape[2])
    attended, outgoing = attend(query, new_key, new_value, cache_keys, cache_values, lens, ids)

    def exchange(x):
        x = x.reshape(GROUPS, SLOTS, x.shape[1])
        return lax.all_to_all(x, "dp", split_axis=0, concat_axis=0, tiled=True).reshape(SENT, x.shape[2])

    def adapt(arrived):
        part, names = rank_parts(arrived, down)
        pair = add16(part, send(part, swap))
        parts = [pair, send(pair, right), send(pair, left), send(pair, across)]
        return deltas(parts, names, up)

    arrived = exchange(outgoing)

    def chunk(by):
        to = (chip + by) % chips
        theirs, mine = base_parts(attended, out_weight, to * 2 + (1 - core), to * 2 + core, cols)
        return mine, send(theirs, swap)

    half = attended.shape[0] // 2
    far_mine, far_other = chunk(2)
    far_top = add16(far_mine[:half], far_other[:half])
    far_bot = add16(far_mine[half:], far_other[half:])
    from_left = send(far_top, right)
    from_right = send(far_bot, left)
    right_mine, right_other = chunk(1)
    left_mine, left_other = chunk(3)
    l_bot = send(add16(right_mine[half:], right_other[half:]), right)
    r_top = send(add16(left_mine[:half], left_other[:half]), left)
    own_mine, own_other = chunk(0)
    three = lambda a, b, c: (a.astype(F32) + b.astype(F32) + c.astype(F32)).astype(BF16)
    l_top = send(three(right_mine[:half], right_other[:half], from_left), right)
    r_bot = send(three(left_mine[half:], left_other[half:], from_right), left)

    back = exchange(adapt(arrived))
    out = finish(ids, back, own_mine, own_other, l_top, l_bot, r_top, r_bot)

    fullest = jnp.max(arrived.reshape(GROUPS, SLOTS, -1)[:, 0, 0]).astype(jnp.int32)

    def more(state):
        return state[0] * TAKES < fullest

    def another(state):
        turn, out = state
        number = turn.reshape(1)
        again = exchange(adapt(exchange(refill(number, ids, attended))))
        return turn + 1, add_turn(number, ids, again, out)

    return lax.while_loop(more, another, (jnp.int32(1), out))[1]


def solution(mesh):
    return jax.shard_map(
        per_device,
        mesh=mesh,
        in_specs=(
            P("dp", "tensor"),
            P("dp", "tensor"),
            P("dp", "tensor"),
            P("dp", None, "tensor"),
            P("dp", None, "tensor"),
            P("dp"),
            P("dp", None),
            P("tensor", None),
            P("dp", "tensor", None),
            P("dp", None, "tensor"),
        ),
        out_specs=P("dp", "tensor"),
        check_vma=False,
    )
```

time: 248 us -> 140 us (0.56)
  blocking collectives: 115 us -> 0 us
  Pallas kernels: 0 us -> 42.1 us
  matrix products: 27.3 us -> 0 us
  starting transfers between devices: 4.54 us -> 26.5 us
  between operations: 13.6 us -> 0.84 us
  local copies, waits for them, and re-layouts: 17.9 us -> 8.21 us
  waiting for transfers between devices: 58.6 us -> 51.3 us
    all_to_all x1 -> x0, blocking collectives: 59.1 us -> none  [per_device(): lax.all_to_all(outgoing, 'dp', split_axis=0, concat_axis=0, tiled=True)]
    psum x1 -> x0, blocking collectives: 56.1 us -> none  [per_device(): summed = lax.psum(partial_rank, 'tensor').astype(jnp.bfloat16)]
    pallas_call x0 -> x8, Pallas kernels: none -> 42.1 us  [the longest x4 20.4 us: base_parts(): pl.pallas_call(base_kernel, grid_spec=pltpu.PrefetchScalarGridSpec(num_sc...]
    all_to_all x1 -> x2, waiting for transfers between devices: 58.6 us -> 21.8 us  [exchange(): lax.all_to_all(x, 'dp', split_axis=0, concat_axis=0, tiled=True)]
    ppermute x0 -> x14, waiting for transfers between devices: none -> 29.5 us  [per_device(): send = lambda x, perm: lax.ppermute(x, 'tensor', perm)]
    dot_general x6 -> x0, matrix products: 27.3 us -> none  [the longest x1 15.6 us: per_device(): lax.dot_general(out_weight, attended, (((0,), (1,)), ((), ())), preferred...]
    ppermute x0 -> x14, starting transfers between devices: none -> 13.9 us  [per_device(): send = lambda x, perm: lax.ppermute(x, 'tensor', perm)]
    all_to_all x1 -> x2, starting transfers between devices: 4.54 us -> 12.6 us  [exchange(): lax.all_to_all(x, 'dp', split_axis=0, concat_axis=0, tiled=True)]
  transfers between devices with their start and end apart: 2 -> 16, of which waited for: 1 -> 5; matrix products, arithmetic and copies ran while one was open for 7% -> 7% of each run, Pallas kernels for 0% -> 20%
where the time goes in v1:
time: 140 us; the launch traced here: 139 us
  waiting for transfers between devices  51.3 us (37%)
  Pallas kernels  42.1 us (30%)
  starting transfers between devices  26.5 us (19%)
  other arithmetic  10.4 us (7%)
  local copies, waits for them, and re-layouts  8.21 us (6%)
    ppermute x14, waiting for transfers between devices, per_device(): send = lambda x, perm: lax.ppermute(x, 'tensor', perm)  29.5 us
    all_to_all x2, waiting for transfers between devices, exchange(): lax.all_to_all(x, 'dp', split_axis=0, concat_axis=0, tiled=True)  21.8 us
    pallas_call x4, Pallas kernels, base_parts(): pl.pallas_call(base_kernel, grid_spec=pltpu.PrefetchScalarGridSpec(num_sc...  20.4 us
    ppermute x14, starting transfers between devices, per_device(): send = lambda x, perm: lax.ppermute(x, 'tensor', perm)  13.9 us
    all_to_all x2, starting transfers between devices, exchange(): lax.all_to_all(x, 'dp', split_axis=0, concat_axis=0, tiled=True)  12.6 us
    pallas_call x1, Pallas kernels, attend(): pl.pallas_call(functools.partial(attend_kernel, block=block), grid=(rows...  9.62 us
    unnamed x30, local copies, waits for them, and re-layouts  8.21 us
    convert_element_type x3, other arithmetic, add16(): return (a.astype(F32) + b.astype(F32)).astype(BF16)  6.67 us
  transfers between devices with their start and end apart: 16, of which 5 were waited for; matrix products, arithmetic and copies ran while one was open for 7% of the time, Pallas kernels for 20%

profile of v1, /device:TPU:0, one launch (start us, length us, event | category | flops | bytes accessed | tf_op | source)
XLA Modules:
  0.0 139.3 jit_solution(6461630915499101057)
XLA Ops:
  0.0 1.2 copy-done.6
  1.2 0.9 copy-done.9
  2.1 0.9 copy-done.10
  3.0 0.7 copy-done.11
  3.7 9.6 %attend.1 = (bf16[512,1024]{1,0:T(8,128)(2,1)S(1)}, bf16[896,1024]{1,0:T(8,128)(2,1)S(1)}) custom-call(bf16[512,1024]{1,0:T(8,128)(2,1)S(1)} %copy-done.6, bf16[512,128]{1,0:T(8,128)(2,1)S(1)} %copy-done.9, bf16[512,128]{1,0:T(8,128)(2,1)S(1)} %copy-done.10, bf16[512,16,128]{2,1,0:T(8,128)(2,1)} %k_ref.1, bf16[512,16,128]{2,1,0:T(8,128)(2,1)} %v_ref.1, ...), custom_call_target="tpu_custom_call" | custom-call | tf_op jit(solution)/shard_map/attend/pallas_call | solution.py:124
  13.4 1.3 copy-done.2
  14.6 8.1 %all-to-all-start.2 = ((bf16[16,56,1024]{2,1,0:T(8,128)(2,1)}), bf16[16,56,1024]{2,1,0:T(8,128)(2,1)S(1)}, u32[]{:S(2)}, u32[]{:S(2)}) async-start(bf16[16,56,1024]{2,1,0:T(8,128)(2,1)} %bitcast.39), calls=%async_computation.2 | async-start | bytes 3670016 | tf_op jit(solution)/shard_map/all_to_all | solution.py:332
  22.8 0.1 pad_add_fusion.2.at_ref
  22.9 4.9 %base_parts.6 = (bf16[512,1024]{1,0:T(8,128)(2,1)}, bf16[512,1024]{1,0:T(8,128)(2,1)S(1)}) custom-call(s32[2]{0:T(128)S(1)} %pad_add_fusion.2.at_ref, bf16[512,1024]{1,0:T(8,128)(2,1)S(1)} %get-tuple-element.142.att_ref, bf16[1024,8192]{1,0:T(8,128)(2,1)} %wm_ref.7, bf16[1024,8192]{1,0:T(8,128)(2,1)} %wm_ref.7), custom_call_target="tpu_custom_call" | custom-call | flops 2147483648 | bytes 7340032 | tf_op jit(solution)/shard_map/base_parts/pallas_call | solution.py:241
  27.8 1.0 copy-done.3
  28.8 0.0 collective-permute-start.10
  28.8 0.1 pad_add_fusion.3.at_ref
  28.9 21.8 %all-to-all-done.2 = bf16[16,56,1024]{2,1,0:T(8,128)(2,1)S(1)} async-done(((bf16[16,56,1024]{2,1,0:T(8,128)(2,1)}), bf16[16,56,1024]{2,1,0:T(8,128)(2,1)S(1)}, u32[]{:S(2)}, u32[]{:S(2)}) %all-to-all-start.2) | async-done | bytes 1835040 | tf_op jit(solution)/shard_map/all_to_all | solution.py:332
  50.7 4.5 %rank_parts.2 = (bf16[448,128]{1,0:T(8,128)(2,1)S(1)}, s32[896,128]{1,0:T(8,128)S(1)}) custom-call(bf16[896,1024]{1,0:T(8,128)(2,1)S(1)} %bitcast.37, bf16[1024,1024]{1,0:T(8,128)(2,1)} %bitcast.43), custom_call_target="tpu_custom_call" | custom-call | tf_op jit(solution)/shard_map/rank_parts/pallas_call | solution.py:191
  55.2 0.1 collective-permute-start.4
  55.3 4.9 %base_parts.7 = (bf16[512,1024]{1,0:T(8,128)(2,1)}, bf16[512,1024]{1,0:T(8,128)(2,1)S(1)}) custom-call(s32[2]{0:T(128)S(1)} %pad_add_fusion.3.at_ref, bf16[512,1024]{1,0:T(8,128)(2,1)S(1)} %copy-done.13, bf16[1024,8192]{1,0:T(8,128)(2,1)} %wm_ref.7, bf16[1024,8192]{1,0:T(8,128)(2,1)} %wm_ref.7), custom_call_target="tpu_custom_call" | custom-call | flops 2147483648 | bytes 7340032 | tf_op jit(solution)/shard_map/base_parts/pallas_call | solution.py:241
  60.2 0.5 collective-permute-start.14
  60.7 0.1 pad_add_fusion.1.at_ref
  60.8 0.0 collective-permute-done.4
  60.8 0.9 add_convert_fusion.7.p0_ref
  61.7 0.0 copy-start.14
  61.8 3.1 %collective-permute-start.7 = (bf16[448,128]{1,0:T(8,128)(2,1)S(1)}, bf16[448,128]{1,0:T(8,128)(2,1)S(1)}, u32[]{:S(2)}, u32[]{:S(2)}) collective-permute-start(bf16[448,128]{1,0:T(8,128)(2,1)S(1)} %add_convert_fusion.7.p0_ref), channel_id=1, source_target_pairs={{0,4},{1,5},{2,6},{3,7},{4,0},{5,1},{6,2},{7,3},{8,12},{9,13},{10,... | collective-permute-start | bytes 344072 | tf_op jit(solution)/shard_map/ppermute | solution.py:322
  64.8 1.2 collective-permute-start.6
  66.0 0.9 collective-permute-start.5
  66.9 5.3 %base_parts.5 = (bf16[512,1024]{1,0:T(8,128)(2,1)}, bf16[512,1024]{1,0:T(8,128)(2,1)S(1)}) custom-call(s32[2]{0:T(128)S(1)} %pad_add_fusion.1.at_ref, bf16[512,1024]{1,0:T(8,128)(2,1)} %copy-done.12, bf16[1024,8192]{1,0:T(8,128)(2,1)} %wm_ref.7, bf16[1024,8192]{1,0:T(8,128)(2,1)} %wm_ref.7), custom_call_target="tpu_custom_call" | custom-call | flops 2147483648 | bytes 7340032 | tf_op jit(solution)/shard_map/base_parts/pallas_call | solution.py:241
  72.1 1.0 copy-done.4
  73.1 0.0 collective-permute-done.5.p1_ref
  73.2 2.6 %deltas.2 = bf16[896,1024]{1,0:T(8,128)(2,1)S(1)} custom-call(bf16[448,128]{1,0:T(8,128)(2,1)S(1)} %add_convert_fusion.7.p0_ref, bf16[448,128]{1,0:T(8,128)(2,1)S(1)} %collective-permute-done.5.p1_ref, bf16[448,128]{1,0:T(8,128)(2,1)S(1)} %collective-permute-done.6.p2_ref, bf16[448,128]{1,0:T(8,128)(2,1)S(1)} %collective-permute-done.7.p3_ref, ...), custom_call_target="tpu_custom_call" | custom-call | tf_op jit(solution)/shard_map/deltas/pallas_call | solution.py:220
  75.8 1.2 copy-done.1
  77.0 4.4 %all-to-all-start.3 = ((bf16[16,56,1024]{2,1,0:T(8,128)(2,1)}), bf16[16,56,1024]{2,1,0:T(8,128)(2,1)}, u32[]{:S(2)}, u32[]{:S(2)}) async-start(bf16[16,56,1024]{2,1,0:T(8,128)(2,1)} %bitcast.38), calls=%async_computation.3 | async-start | bytes 3670016 | tf_op jit(solution)/shard_map/all_to_all | solution.py:332
  81.4 3.0 %add_convert_fusion.2 = (bf16[256,1024]{1,0:T(8,128)(2,1)}, bf16[256,1024]{1,0:T(8,128)(2,1)}) fusion(bf16[512,1024]{1,0:T(8,128)(2,1)} %collective-permute-done.10, bf16[512,1024]{1,0:T(8,128)(2,1)} %copy-done.3), kind=kLoop, calls=%fused_computation.2 | loop fusion | flops 2097152 | bytes 3145728 | tf_op jit(solution)/shard_map/convert_element_type | solution.py:308
  84.4 2.4 %collective-permute-start.16 = (bf16[256,1024]{1,0:T(8,128)(2,1)}, bf16[256,1024]{1,0:T(8,128)(2,1)S(1)}, u32[]{:S(2)}, u32[]{:S(2)}) collective-permute-start(bf16[256,1024]{1,0:T(8,128)(2,1)} %get-tuple-element.86), channel_id=1, source_target_pairs={{0,6},{1,7},{2,0},{3,1},{4,2},{5,3},{6,4},{7,5},{8,14},{9,15},{10,... | collective-permute-start | bytes 1572872 | tf_op jit(solution)/shard_map/ppermute | solution.py:322
  86.8 0.1 pad_add_fusion.at_ref
  86.9 5.3 %base_parts.4 = (bf16[512,1024]{1,0:T(8,128)(2,1)}, bf16[512,1024]{1,0:T(8,128)(2,1)S(1)}) custom-call(s32[2]{0:T(128)S(1)} %pad_add_fusion.at_ref, bf16[512,1024]{1,0:T(8,128)(2,1)} %copy-done.12, bf16[1024,8192]{1,0:T(8,128)(2,1)} %wm_ref.7, bf16[1024,8192]{1,0:T(8,128)(2,1)} %wm_ref.7), custom_call_target="tpu_custom_call" | custom-call | flops 2147483648 | bytes 7340032 | tf_op jit(solution)/shard_map/base_parts/pallas_call | solution.py:241
  92.1 0.2 collective-permute-start.8
  92.3 6.6 %collective-permute-done.16 = bf16[256,1024]{1,0:T(8,128)(2,1)S(1)} collective-permute-done((bf16[256,1024]{1,0:T(8,128)(2,1)}, bf16[256,1024]{1,0:T(8,128)(2,1)S(1)}, u32[]{:S(2)}, u32[]{:S(2)}) %collective-permute-start.16) | collective-permute-done | bytes 524320 | tf_op jit(solution)/shard_map/ppermute | solution.py:322
  98.9 2.8 %add_convert_fusion.1 = (bf16[256,1024]{1,0:T(8,128)(2,1)}, bf16[256,1024]{1,0:T(8,128)(2,1)}) fusion(bf16[256,1024]{1,0:T(8,128)(2,1)S(1)} %collective-permute-done.16, bf16[512,1024]{1,0:T(8,128)(2,1)} %collective-permute-done.14, bf16[512,1024]{1,0:T(8,128)(2,1)S(1)} %get-tuple-element.67), kind=kLoop, calls=%fused_computation.1 | loop fusion | flops 2621440 | bytes 3670016 | tf_op jit(solution)/shard_map/convert_element_type | solution.py:358
  101.7 3.6 %collective-permute-start.17 = (bf16[256,1024]{1,0:T(8,128)(2,1)}, bf16[256,1024]{1,0:T(8,128)(2,1)S(1)}, u32[]{:S(2)}, u32[]{:S(2)}) collective-permute-start(bf16[256,1024]{1,0:T(8,128)(2,1)} %get-tuple-element.84), channel_id=1, source_target_pairs={{0,6},{1,7},{2,0},{3,1},{4,2},{5,3},{6,4},{7,5},{8,14},{9,15},{10,... | collective-permute-start | bytes 1572872 | tf_op jit(solution)/shard_map/ppermute | solution.py:322
  105.3 0.0 collective-permute-start.15
  105.4 0.0 copy-start.17
  105.4 2.8 %add_convert_fusion.4 = (bf16[256,1024]{1,0:T(8,128)(2,1)}, bf16[256,1024]{1,0:T(8,128)(2,1)}) fusion(bf16[512,1024]{1,0:T(8,128)(2,1)} %collective-permute-done.9, bf16[512,1024]{1,0:T(8,128)(2,1)S(1)} %copy-done.5, bf16[256,1024]{1,0:T(8,128)(2,1)S(1)} %collective-permute-done.11), kind=kLoop, calls=%fused_computation.4 | loop fusion | flops 2621440 | bytes 3670016 | tf_op jit(solution)/shard_map/convert_element_type | solution.py:308
  108.1 2.0 %collective-permute-start.13 = (bf16[256,1024]{1,0:T(8,128)(2,1)}, bf16[256,1024]{1,0:T(8,128)(2,1)}, u32[]{:S(2)}, u32[]{:S(2)}) collective-permute-start(bf16[256,1024]{1,0:T(8,128)(2,1)} %get-tuple-element.88), channel_id=1, source_target_pairs={{0,2},{1,3},{2,4},{3,5},{4,6},{5,7},{6,0},{7,1},{8,10},{9,11},{10,... | collective-permute-start | bytes 1572872 | tf_op jit(solution)/shard_map/ppermute | solution.py:322
  110.1 0.0 collective-permute-start.12
  110.2 0.6 slice_reduce_fusion
  111.4 6.5 %collective-permute-done.17.rbot_ref = bf16[256,1024]{1,0:T(8,128)(2,1)S(1)} collective-permute-done((bf16[256,1024]{1,0:T(8,128)(2,1)}, bf16[256,1024]{1,0:T(8,128)(2,1)S(1)}, u32[]{:S(2)}, u32[]{:S(2)}) %collective-permute-start.17) | collective-permute-done | bytes 524320 | tf_op jit(solution)/shard_map/ppermute | solution.py:322
  117.9 10.1 %collective-permute-done.15.rtop_ref = bf16[256,1024]{1,0:T(8,128)(2,1)} collective-permute-done((bf16[256,1024]{1,0:T(8,128)(2,1)}, bf16[256,1024]{1,0:T(8,128)(2,1)}, u32[]{:S(2)}, u32[]{:S(2)}) %collective-permute-start.15) | collective-permute-done | bytes 524320 | tf_op jit(solution)/shard_map/ppermute | solution.py:322
  128.0 6.3 %collective-permute-done.12.ltop_ref = bf16[256,1024]{1,0:T(8,128)(2,1)} collective-permute-done((bf16[256,1024]{1,0:T(8,128)(2,1)}, bf16[256,1024]{1,0:T(8,128)(2,1)}, u32[]{:S(2)}, u32[]{:S(2)}) %collective-permute-start.12) | collective-permute-done | bytes 524320 | tf_op jit(solution)/shard_map/ppermute | solution.py:322
  134.3 5.0 %finish.1 = bf16[512,1024]{1,0:T(8,128)(2,1)} custom-call(s32[1,512]{1,0:T(1,128)S(1)} %bitcast.46, bf16[896,1024]{1,0:T(8,128)(2,1)} %bitcast.13.back_ref, bf16[512,1024]{1,0:T(8,128)(2,1)S(1)} %copy-done.8, bf16[512,1024]{1,0:T(8,128)(2,1)} %collective-permute-done.8.swapped_ref, bf16[256,1024]{1,0:T(8,128)(2,1)} %collective-permute-done.12.ltop_ref, ...), custom_call_target="tpu_custom_call" | custom-call | tf_op jit(solution)/shard_map/finish/pallas_call | solution.py:281
  (32 shorter events, 0.1 us)
Async XLA Ops:
  0.0 1.2 copy-start.6
  1.2 0.9 copy-start.9
  2.1 0.9 copy-start.10
  3.0 0.7 copy-start.11
  13.3 1.3 copy-start.2
  14.6 8.3 %copy-start.12 = (bf16[512,1024]{1,0:T(8,128)(2,1)}, bf16[512,1024]{1,0:T(8,128)(2,1)S(1)}, u32[]{:S(2)}) copy-start(bf16[512,1024]{1,0:T(8,128)(2,1)S(1)} %get-tuple-element.142.att_ref) | copy-start | bytes 3145732
  14.6 36.0 %all-to-all-start.2 = ((bf16[16,56,1024]{2,1,0:T(8,128)(2,1)}), bf16[16,56,1024]{2,1,0:T(8,128)(2,1)S(1)}, u32[]{:S(2)}, u32[]{:S(2)}) async-start(bf16[16,56,1024]{2,1,0:T(8,128)(2,1)} %bitcast.39), calls=%async_computation.2 | async-start | bytes 3670016 | tf_op jit(solution)/shard_map/all_to_all | solution.py:332
  27.8 1.0 copy-start.3
  28.8 52.7 %collective-permute-start.10 = (bf16[512,1024]{1,0:T(8,128)(2,1)}, bf16[512,1024]{1,0:T(8,128)(2,1)}, u32[]{:S(2)}, u32[]{:S(2)}) collective-permute-start(bf16[512,1024]{1,0:T(8,128)(2,1)} %get-tuple-element.66), channel_id=1, source_target_pairs={{0,1},{1,0},{2,3},{3,2},{4,5},{5,4},{6,7},{7,6},{8,9},{9,8},{10,11... | collective-permute-start | bytes 3145736 | tf_op jit(solution)/shard_map/ppermute | solution.py:322
  50.7 4.6 %copy-start.13 = (bf16[512,1024]{1,0:T(8,128)(2,1)S(1)}, bf16[512,1024]{1,0:T(8,128)(2,1)}, u32[]{:S(2)}) copy-start(bf16[512,1024]{1,0:T(8,128)(2,1)} %copy-done.12) | copy-start | bytes 3145732
  55.2 5.6 %collective-permute-start.4 = (bf16[448,128]{1,0:T(8,128)(2,1)S(1)}, bf16[448,128]{1,0:T(8,128)(2,1)}, u32[]{:S(2)}, u32[]{:S(2)}) collective-permute-start(bf16[448,128]{1,0:T(8,128)(2,1)S(1)} %get-tuple-element.58), channel_id=1, source_target_pairs={{0,1},{1,0},{2,3},{3,2},{4,5},{5,4},{6,7},{7,6},{8,9},{9,8},{10,11... | collective-permute-start | bytes 344072 | tf_op jit(solution)/shard_map/ppermute | solution.py:322
  60.2 32.1 %collective-permute-start.14 = (bf16[512,1024]{1,0:T(8,128)(2,1)}, bf16[512,1024]{1,0:T(8,128)(2,1)}, u32[]{:S(2)}, u32[]{:S(2)}) collective-permute-start(bf16[512,1024]{1,0:T(8,128)(2,1)} %get-tuple-element.68), channel_id=1, source_target_pairs={{0,1},{1,0},{2,3},{3,2},{4,5},{5,4},{6,7},{7,6},{8,9},{9,8},{10,11... | collective-permute-start | bytes 3145736 | tf_op jit(solution)/shard_map/ppermute | solution.py:322
  61.7 11.4 %copy-start.14 = (bf16[16,64,1024]{2,1,0:T(8,128)(2,1)S(1)}, bf16[16,64,1024]{2,1,0:T(8,128)(2,1)}, u32[]{:S(2)}) copy-start(bf16[16,64,1024]{2,1,0:T(8,128)(2,1)} %param.21) | copy-start | bytes 6291460
  61.8 11.4 %collective-permute-start.7 = (bf16[448,128]{1,0:T(8,128)(2,1)S(1)}, bf16[448,128]{1,0:T(8,128)(2,1)S(1)}, u32[]{:S(2)}, u32[]{:S(2)}) collective-permute-start(bf16[448,128]{1,0:T(8,128)(2,1)S(1)} %add_convert_fusion.7.p0_ref), channel_id=1, source_target_pairs={{0,4},{1,5},{2,6},{3,7},{4,0},{5,1},{6,2},{7,3},{8,12},{9,13},{10,... | collective-permute-start | bytes 344072 | tf_op jit(solution)/shard_map/ppermute | solution.py:322
  64.8 8.3 %collective-permute-start.6 = (bf16[448,128]{1,0:T(8,128)(2,1)S(1)}, bf16[448,128]{1,0:T(8,128)(2,1)S(1)}, u32[]{:S(2)}, u32[]{:S(2)}) collective-permute-start(bf16[448,128]{1,0:T(8,128)(2,1)S(1)} %add_convert_fusion.7.p0_ref), channel_id=1, source_target_pairs={{0,6},{1,7},{2,0},{3,1},{4,2},{5,3},{6,4},{7,5},{8,14},{9,15},{10,... | collective-permute-start | bytes 344072 | tf_op jit(solution)/shard_map/ppermute | solution.py:322
  66.0 7.1 %collective-permute-start.5 = (bf16[448,128]{1,0:T(8,128)(2,1)S(1)}, bf16[448,128]{1,0:T(8,128)(2,1)S(1)}, u32[]{:S(2)}, u32[]{:S(2)}) collective-permute-start(bf16[448,128]{1,0:T(8,128)(2,1)S(1)} %add_convert_fusion.7.p0_ref), channel_id=1, source_target_pairs={{0,2},{1,3},{2,4},{3,5},{4,6},{5,7},{6,0},{7,1},{8,10},{9,11},{10,... | collective-permute-start | bytes 344072 | tf_op jit(solution)/shard_map/ppermute | solution.py:322
  72.1 1.0 copy-start.4
  73.1 32.2 %collective-permute-start.9 = (bf16[512,1024]{1,0:T(8,128)(2,1)}, bf16[512,1024]{1,0:T(8,128)(2,1)}, u32[]{:S(2)}, u32[]{:S(2)}) collective-permute-start(bf16[512,1024]{1,0:T(8,128)(2,1)} %get-tuple-element.64), channel_id=1, source_target_pairs={{0,1},{1,0},{2,3},{3,2},{4,5},{5,4},{6,7},{7,6},{8,9},{9,8},{10,11... | collective-permute-start | bytes 3145736 | tf_op jit(solution)/shard_map/ppermute | solution.py:322
  75.8 1.2 copy-start.1
  77.0 57.3 %all-to-all-start.3 = ((bf16[16,56,1024]{2,1,0:T(8,128)(2,1)}), bf16[16,56,1024]{2,1,0:T(8,128)(2,1)}, u32[]{:S(2)}, u32[]{:S(2)}) async-start(bf16[16,56,1024]{2,1,0:T(8,128)(2,1)} %bitcast.38), calls=%async_computation.3 | async-start | bytes 3670016 | tf_op jit(solution)/shard_map/all_to_all | solution.py:332
  84.4 14.5 %collective-permute-start.16 = (bf16[256,1024]{1,0:T(8,128)(2,1)}, bf16[256,1024]{1,0:T(8,128)(2,1)S(1)}, u32[]{:S(2)}, u32[]{:S(2)}) collective-permute-start(bf16[256,1024]{1,0:T(8,128)(2,1)} %get-tuple-element.86), channel_id=1, source_target_pairs={{0,6},{1,7},{2,0},{3,1},{4,2},{5,3},{6,4},{7,5},{8,14},{9,15},{10,... | collective-permute-start | bytes 1572872 | tf_op jit(solution)/shard_map/ppermute | solution.py:322
  86.8 18.6 %collective-permute-start.11 = (bf16[256,1024]{1,0:T(8,128)(2,1)}, bf16[256,1024]{1,0:T(8,128)(2,1)S(1)}, u32[]{:S(2)}, u32[]{:S(2)}) collective-permute-start(bf16[256,1024]{1,0:T(8,128)(2,1)} %get-tuple-element.87), channel_id=1, source_target_pairs={{0,2},{1,3},{2,4},{3,5},{4,6},{5,7},{6,0},{7,1},{8,10},{9,11},{10,... | collective-permute-start | bytes 1572872 | tf_op jit(solution)/shard_map/ppermute | solution.py:322
  92.1 9.6 %copy-start.7 = (bf16[512,1024]{1,0:T(8,128)(2,1)}, bf16[512,1024]{1,0:T(8,128)(2,1)S(1)}, u32[]{:S(2)}) copy-start(bf16[512,1024]{1,0:T(8,128)(2,1)S(1)} %get-tuple-element.61.mine_ref) | copy-start | bytes 3145732
  92.1 19.3 %collective-permute-start.8 = (bf16[512,1024]{1,0:T(8,128)(2,1)}, bf16[512,1024]{1,0:T(8,128)(2,1)}, u32[]{:S(2)}, u32[]{:S(2)}) collective-permute-start(bf16[512,1024]{1,0:T(8,128)(2,1)} %get-tuple-element.62), channel_id=1, source_target_pairs={{0,1},{1,0},{2,3},{3,2},{4,5},{5,4},{6,7},{7,6},{8,9},{9,8},{10,11... | collective-permute-start | bytes 3145736 | tf_op jit(solution)/shard_map/ppermute | solution.py:322
  98.9 6.4 %copy-start.5 = (bf16[512,1024]{1,0:T(8,128)(2,1)S(1)}, bf16[512,1024]{1,0:T(8,128)(2,1)}, u32[]{:S(2)}) copy-start(bf16[512,1024]{1,0:T(8,128)(2,1)} %copy-done.4) | copy-start | bytes 3145732
  101.7 16.2 %collective-permute-start.17 = (bf16[256,1024]{1,0:T(8,128)(2,1)}, bf16[256,1024]{1,0:T(8,128)(2,1)S(1)}, u32[]{:S(2)}, u32[]{:S(2)}) collective-permute-start(bf16[256,1024]{1,0:T(8,128)(2,1)} %get-tuple-element.84), channel_id=1, source_target_pairs={{0,6},{1,7},{2,0},{3,1},{4,2},{5,3},{6,4},{7,5},{8,14},{9,15},{10,... | collective-permute-start | bytes 1572872 | tf_op jit(solution)/shard_map/ppermute | solution.py:322
  105.3 22.7 %collective-permute-start.15 = (bf16[256,1024]{1,0:T(8,128)(2,1)}, bf16[256,1024]{1,0:T(8,128)(2,1)}, u32[]{:S(2)}, u32[]{:S(2)}) collective-permute-start(bf16[256,1024]{1,0:T(8,128)(2,1)} %get-tuple-element.85), channel_id=1, source_target_pairs={{0,6},{1,7},{2,0},{3,1},{4,2},{5,3},{6,4},{7,5},{8,14},{9,15},{10,... | collective-permute-start | bytes 1572872 | tf_op jit(solution)/shard_map/ppermute | solution.py:322
  105.3 28.9 %copy-start.8 = (bf16[512,1024]{1,0:T(8,128)(2,1)S(1)}, bf16[512,1024]{1,0:T(8,128)(2,1)}, u32[]{:S(2)}) copy-start(bf16[512,1024]{1,0:T(8,128)(2,1)} %copy-done.7) | copy-start | bytes 3145732
  105.4 28.9 %copy-start.17 = (s32[512,1]{0,1:T(1,128)S(1)}, s32[512,1]{0,1:T(1,128)}, u32[]{:S(2)}) copy-start(s32[512,1]{0,1:T(1,128)} %param.18) | copy-start | bytes 6148
  108.1 19.9 %collective-permute-start.13 = (bf16[256,1024]{1,0:T(8,128)(2,1)}, bf16[256,1024]{1,0:T(8,128)(2,1)}, u32[]{:S(2)}, u32[]{:S(2)}) collective-permute-start(bf16[256,1024]{1,0:T(8,128)(2,1)} %get-tuple-element.88), channel_id=1, source_target_pairs={{0,2},{1,3},{2,4},{3,5},{4,6},{5,7},{6,0},{7,1},{8,10},{9,11},{10,... | collective-permute-start | bytes 1572872 | tf_op jit(solution)/shard_map/ppermute | solution.py:322
  110.1 24.1 %collective-permute-start.12 = (bf16[256,1024]{1,0:T(8,128)(2,1)}, bf16[256,1024]{1,0:T(8,128)(2,1)}, u32[]{:S(2)}, u32[]{:S(2)}) collective-permute-start(bf16[256,1024]{1,0:T(8,128)(2,1)} %get-tuple-element.89), channel_id=1, source_target_pairs={{0,2},{1,3},{2,4},{3,5},{4,6},{5,7},{6,0},{7,1},{8,10},{9,11},{10,... | collective-permute-start | bytes 1572872 | tf_op jit(solution)/shard_map/ppermute | solution.py:322

commit v2 on v0

v2 whole, which is shorter than its diff:
```python
import functools

import jax
import jax.numpy as jnp
from jax import lax
from jax.experimental import pallas as pl
from jax.experimental.pallas import tpu as pltpu
from jax.sharding import PartitionSpec as P

HD = 128
GROUP = 8
GROUPS = 16
ADP = 16
RANK = 64
SLOTS = 56
TAKES = SLOTS - 1
SENT = GROUPS * SLOTS
HALF = SENT // 2
SUB = 16
WIDE = SUB * SUB
PACK = 448
PIECE = 256
BLOCK = 256
STEP = 512
F32 = jnp.float32
BF16 = jnp.bfloat16
NT = (((1,), (1,)), ((), ()))
TN = (((0,), (0,)), ((), ()))
NEG = -1e30
VMEM_LIMIT = 64 * 1024 * 1024 - 64 * 1024
COST = 1024
HBM = pl.BlockSpec(memory_space=pltpu.HBM)
VMEM = pl.BlockSpec(memory_space=pltpu.VMEM)
SMEM = pl.BlockSpec(memory_space=pltpu.SMEM)


def iota(shape, axis):
    return lax.broadcasted_iota(jnp.int32, shape, axis)


def mask16(cond):
    return cond.astype(F32).astype(BF16)


def call(kernel, name, in_specs, out_shape, scratch, cost=None):
    single = not isinstance(out_shape, list)
    return pl.pallas_call(
        kernel,
        in_specs=in_specs,
        out_specs=HBM if single else [HBM] * len(out_shape),
        out_shape=out_shape,
        scratch_shapes=scratch,
        compiler_params=pltpu.CompilerParams(vmem_limit_bytes=VMEM_LIMIT),
        cost_estimate=pl.CostEstimate(flops=COST, bytes_accessed=COST, transcendentals=0),
        name=name,
    )


def start(source, target, sem):
    copy = pltpu.make_async_copy(source, target, sem)
    copy.start()
    return copy


def wait(copies):
    for copy in copies:
        copy.wait()


def shape(rows, cols, dtype=BF16):
    return jax.ShapeDtypeStruct((rows, cols), dtype)


def dots(left, right_ref, columns):
    return jnp.dot(left, right_ref[:, columns], preferred_element_type=F32)


def places(ids):
    rows = ids.shape[1]
    dst = lax.shift_right_logical(ids, 4)
    member = (iota((GROUPS, rows), 0) == dst).astype(F32)
    before = mask16(iota((rows, rows), 0) < iota((rows, rows), 1))
    count = jnp.dot(member.astype(BF16), before, preferred_element_type=F32)
    place = jnp.sum(member * count, axis=0, keepdims=True)
    fullest = jnp.max(jnp.sum(member, axis=1, keepdims=True), axis=0, keepdims=True)
    return dst, place.astype(jnp.int32), fullest


def plan(ids, turn, plan_ref):
    dst, place, fullest = places(ids)
    at = place - turn * TAKES
    inside = (at >= 0) & (at < TAKES)
    plan_ref[0:1, :] = jnp.where(inside, dst * SLOTS + 1 + at, -1)
    plan_ref[1:2, :] = jnp.where(inside, dst * SLOTS, -1)
    plan_ref[2:3, :] = at + 1
    plan_ref[3:4, :] = ids & (ADP - 1)
    plan_ref[4:5, :] = jnp.broadcast_to(fullest, at.shape).astype(jnp.int32)


def pack(chunk, plan_ref, att_ref, out_ref):
    rows = plan_ref.shape[1]
    here = pl.ds(chunk * PACK, PACK)
    row = iota((PACK, rows), 0) + chunk * PACK
    pick = mask16(row == plan_ref[0:1, :])
    moved = jnp.dot(pick, att_ref[...], preferred_element_type=F32)
    heads = jnp.where(row == plan_ref[1:2, :], plan_ref[3:4, :].astype(F32), 0.0).astype(BF16)
    lanes = mask16(iota((128, rows), 0) == plan_ref[2:3, :])
    names = lax.dot_general(heads, lanes, NT, preferred_element_type=F32)
    slot = iota((PACK, 128), 0) + chunk * PACK
    first = (lax.rem(slot, SLOTS) == 0) & (iota((PACK, 128), 1) == 0)
    names = names + jnp.where(first, plan_ref[4:5, 0:128].astype(F32), 0.0)
    out_ref[here, 0:128] = (moved[:, 0:128] + names).astype(BF16)
    out_ref[here, 128:] = moved[:, 128:].astype(BF16)


def pack_all(plan_ref, att_ref, out_ref, out_hbm, sems):
    copies = []
    for chunk in range(SENT // PACK):
        pack(chunk, plan_ref, att_ref, out_ref)
        here = pl.ds(chunk * PACK, PACK)
        copies.append(start(out_ref.at[here], out_hbm.at[here], sems.at[chunk]))
    return copies


def attend_kernel(
    q_hbm, nk_hbm, nv_hbm, k_hbm, v_hbm, w_hbm, len_ref, ids_ref,
    att_hbm, out_hbm, far_hbm,
    q_ref, nk_ref, nv_ref, k_ref, v_ref, w_ref, live_ref, plan_ref, att_ref, out_ref, far_ref,
    in_sems, new_sems, w_sems, att_sems, out_sems, far_sems,
):
    rows = len_ref.shape[1]
    subs = rows // SUB
    blocks = rows // BLOCK
    scale = 1.4426950408889634 / HD**0.5
    new = [start(nk_hbm, nk_ref, new_sems.at[0]), start(nv_hbm, nv_ref, new_sems.at[1])]
    loads = []
    for b in range(blocks):
        here = pl.ds(b * BLOCK, BLOCK)
        pairs = ((q_hbm, q_ref), (k_hbm, k_ref), (v_hbm, v_ref))
        loads.append([start(a.at[here], z.at[here], in_sems.at[b, i]) for i, (a, z) in enumerate(pairs)])

    cols = far_ref.shape[1]
    weights = []
    for side in range(2):
        source = column_block(w_hbm, 2, 1, cols, side)
        weights.append(start(source, w_ref.at[:, side_of(side, cols)], w_sems.at[side]))

    lens = len_ref[...].astype(F32)
    own = jnp.where(lax.shift_right_logical(iota((subs, rows), 1), 4) == iota((subs, rows), 0), lens, 0.0)
    spread = (iota((rows, WIDE), 0) & (SUB - 1)) == lax.shift_right_logical(iota((rows, WIDE), 1), 4)
    length = jnp.dot(own.astype(BF16), mask16(spread), preferred_element_type=F32)
    live_ref[...] = jnp.where((iota((subs, WIDE), 1) & (SUB - 1)).astype(F32) < length, 0.0, NEG)
    plan(ids_ref[...], 0, plan_ref)

    across = iota((GROUP * SUB, WIDE), 0) & (SUB - 1)
    diagonal = jnp.where(across == lax.shift_right_logical(iota((GROUP * SUB, WIDE), 1), 4), 0.0, NEG)
    ones = jnp.ones((WIDE, 128), BF16)
    wait(new)
    stores = []
    for b in range(blocks):
        wait(loads[b])
        for sub in range(BLOCK // SUB):
            here = pl.ds(b * BLOCK + sub * SUB, SUB)
            q = jnp.concatenate([q_ref[here, h * HD : (h + 1) * HD] for h in range(GROUP)], axis=0)
            k = k_ref[here].reshape(WIDE, HD)
            v = v_ref[here].reshape(WIDE, HD)
            nk = nk_ref[here, :].astype(F32)
            nv = nv_ref[here, :].astype(F32)
            live = live_ref[pl.ds(b * (BLOCK // SUB) + sub, 1), :]
            s = lax.dot_general(q, k, NT, preferred_element_type=F32) + diagonal + live
            own = jnp.sum(q.astype(F32) * jnp.concatenate([nk] * GROUP, axis=0), axis=1, keepdims=True)
            top = jnp.maximum(jnp.max(s, axis=1, keepdims=True), own)
            e = jnp.exp2((s - top) * scale).astype(BF16)
            e_own = jnp.exp2((own - top) * scale)
            both = jnp.dot(e, jnp.concatenate([v, ones], axis=1), preferred_element_type=F32)
            mixed = both[:, 0:HD] + e_own * jnp.concatenate([nv] * GROUP, axis=0)
            mixed = (mixed * (1.0 / (both[:, HD:] + e_own))).astype(BF16)
            for h in range(GROUP):
                att_ref[here, h * HD : (h + 1) * HD] = mixed[h * SUB : (h + 1) * SUB, :]
        here = pl.ds(b * BLOCK, BLOCK)
        stores.append(start(att_ref.at[here], att_hbm.at[here], att_sems.at[b]))
    stores += pack_all(plan_ref, att_ref, out_ref, out_hbm, out_sems)
    for side in range(2):
        weights[side].wait()
        for n in range(side * (cols // 2), (side + 1) * (cols // 2), PIECE):
            these = slice(n, n + PIECE)
            far_ref[:, these] = dots(att_ref[...], w_ref, these).astype(BF16)
        these = side_of(side, cols)
        stores.append(start(far_ref.at[:, these], far_hbm.at[:, these], far_sems.at[side]))
    wait(stores)


def attend(query, new_key, new_value, cache_keys, cache_values, weight, lengths, ids, cols):
    rows, width = query.shape
    slots = cache_keys.shape[1]
    blocks = rows // BLOCK
    return call(
        attend_kernel,
        "attend",
        [HBM] * 6 + [VMEM] * 2,
        [shape(rows, width), shape(SENT, width), shape(rows, cols)],
        [
            pltpu.VMEM((rows, width), BF16),
            pltpu.VMEM((rows, HD), BF16),
            pltpu.VMEM((rows, HD), BF16),
            pltpu.VMEM((rows, slots, HD), BF16),
            pltpu.VMEM((rows, slots, HD), BF16),
            pltpu.VMEM((width, cols), BF16),
            pltpu.VMEM((rows // SUB, WIDE), F32),
            pltpu.VMEM((8, rows), jnp.int32),
            pltpu.VMEM((rows, width), BF16),
            pltpu.VMEM((SENT, width), BF16),
            pltpu.VMEM((rows, cols), BF16),
            pltpu.SemaphoreType.DMA((blocks, 3)),
            pltpu.SemaphoreType.DMA((2,)),
            pltpu.SemaphoreType.DMA((2,)),
            pltpu.SemaphoreType.DMA((blocks,)),
            pltpu.SemaphoreType.DMA((SENT // PACK,)),
            pltpu.SemaphoreType.DMA((2,)),
        ],
    )(query, new_key, new_value, cache_keys, cache_values, weight, lengths, ids)


def refill_kernel(turn_ref, ids_ref, att_ref, out_hbm, plan_ref, out_ref, sems):
    plan(ids_ref[...], turn_ref[0], plan_ref)
    wait(pack_all(plan_ref, att_ref, out_ref, out_hbm, sems))


def refill(turn, ids, attended):
    rows, width = attended.shape
    return call(
        refill_kernel,
        "refill",
        [SMEM, VMEM, VMEM],
        shape(SENT, width),
        [
            pltpu.VMEM((8, rows), jnp.int32),
            pltpu.VMEM((SENT, width), BF16),
            pltpu.SemaphoreType.DMA((SENT // PACK,)),
        ],
    )(turn, ids, attended)


def both_halves(x):
    return pltpu.roll(x, RANK, 1)


def turn_kernel(a_hbm, out_hbm, a_ref, out_ref, in_sems, out_sems):
    rows = a_ref.shape[0]
    starts = range(0, rows, PIECE)
    loads = [start(a_hbm.at[pl.ds(n, PIECE)], a_ref.at[pl.ds(n, PIECE)], in_sems.at[i]) for i, n in enumerate(starts)]
    stores = []
    for i, n in enumerate(starts):
        loads[i].wait()
        out_ref[:, n : n + PIECE] = jnp.transpose(a_ref[n : n + PIECE, :])
        stores.append(start(out_ref.at[:, pl.ds(n, PIECE)], out_hbm.at[:, pl.ds(n, PIECE)], out_sems.at[i]))
    wait(stores)


def turned(x):
    rows, cols = x.shape
    return call(
        turn_kernel,
        "turned",
        [HBM],
        shape(cols, rows),
        [
            pltpu.VMEM((rows, cols), BF16),
            pltpu.VMEM((cols, rows), BF16),
            pltpu.SemaphoreType.DMA((rows // PIECE,)),
            pltpu.SemaphoreType.DMA((rows // PIECE,)),
        ],
    )(x)


def rank_kernel(x_hbm, a_hbm, part_hbm, name_hbm, x_ref, a_ref, part_ref, name_ref, in_sems, out_sems):
    loads = []
    for half in range(2):
        here = pl.ds(half * HALF, HALF)
        loads.append(start(x_hbm.at[here], x_ref.at[here], in_sems.at[half]))
        if half == 0:
            downs = []
            for n in range(ADP * RANK // STEP):
                these = pl.ds(n * STEP, STEP)
                downs.append(start(a_hbm.at[:, these], a_ref.at[:, these], in_sems.at[2 + n]))
    upper = (iota((HALF, 128), 1) >= RANK).astype(jnp.int32)
    stores, totals = [], []
    for half in range(2):
        here = pl.ds(half * HALF, HALF)
        row = iota((HALF, 1), 0)
        block = lax.div(row, SLOTS)
        pick = mask16(iota((HALF, HALF), 1) == block * SLOTS)
        at = iota((HALF, 128), 1) == row - block * SLOTS
        loads[half].wait()
        heads = jnp.dot(pick, x_ref[here, 0:128], preferred_element_type=F32)
        name = jnp.sum(jnp.where(at, heads, 0.0), axis=1, keepdims=True).astype(jnp.int32)
        name = jnp.broadcast_to(name, (HALF, 128))
        name_ref[here, :] = name
        stores.append(start(name_ref.at[here], name_hbm.at[here], out_sems.at[half]))
        total = jnp.zeros((HALF, 128), F32)
        for n in range(ADP * RANK // STEP):
            if half == 0:
                downs[n].wait()
            full = dots(x_ref[here, :], a_ref, slice(n * STEP, (n + 1) * STEP))
            own = name - upper - n * (STEP // RANK)
            for t in range(STEP // 128):
                total = total + jnp.where(own == 2 * t, full[:, t * 128 : (t + 1) * 128], 0.0)
        totals.append(total + both_halves(total))
    low = iota((HALF, 128), 1) < RANK
    part_ref[...] = jnp.where(low, totals[0], totals[1]).astype(BF16)
    stores.append(start(part_ref, part_hbm, out_sems.at[2]))
    wait(stores)


def rank_parts(arrived, down):
    width = arrived.shape[1]
    return call(
        rank_kernel,
        "rank_parts",
        [HBM] * 2,
        [shape(HALF, 128), shape(SENT, 128, jnp.int32)],
        [
            pltpu.VMEM((SENT, width), BF16),
            pltpu.VMEM((width, ADP * RANK), BF16),
            pltpu.VMEM((HALF, 128), BF16),
            pltpu.VMEM((SENT, 128), jnp.int32),
            pltpu.SemaphoreType.DMA((2 + ADP * RANK // STEP,)),
            pltpu.SemaphoreType.DMA((3,)),
        ],
    )(arrived, down)


def delta_kernel(
    p0_hbm, p1_hbm, p2_hbm, p3_hbm, name_hbm, b_hbm, out_hbm, p_ref, name_ref, b_ref, wide_ref, out_ref, in_sems, out_sems
):
    parts = [start(p, p_ref.at[i], in_sems.at[i]) for i, p in enumerate((p0_hbm, p1_hbm, p2_hbm, p3_hbm))]
    parts.append(start(name_hbm, name_ref, in_sems.at[4]))
    up = start(b_hbm, b_ref, in_sems.at[5])
    wait(parts)
    rank = (p_ref[0].astype(F32) + p_ref[1].astype(F32)) + (p_ref[2].astype(F32) + p_ref[3].astype(F32))
    rank = rank.astype(BF16).astype(F32)
    other = both_halves(rank)
    low = iota((HALF, 128), 1) < RANK
    upper = (iota((HALF, 128), 1) >= RANK).astype(jnp.int32)
    stores = []
    for half in range(2):
        here = pl.ds(half * HALF, HALF)
        own = jnp.where(low, rank, other) if half == 0 else jnp.where(low, other, rank)
        name = name_ref[here, :] - upper
        for t in range(ADP * RANK // 128):
            wide_ref[here, t * 128 : (t + 1) * 128] = jnp.where(name == 2 * t, own, 0.0).astype(BF16)
        if half == 0:
            up.wait()
        for n in range(out_ref.shape[1] // PIECE):
            these = slice(n * PIECE, (n + 1) * PIECE)
            out_ref[here, these] = dots(wide_ref[here, :], b_ref, these).astype(BF16)
        stores.append(start(out_ref.at[here], out_hbm.at[here], out_sems.at[half]))
    wait(stores)


def deltas(parts, names, up):
    depth, cols = up.shape
    return call(
        delta_kernel,
        "deltas",
        [HBM] * 6,
        shape(SENT, cols),
        [
            pltpu.VMEM((4, HALF, 128), BF16),
            pltpu.VMEM((SENT, 128), jnp.int32),
            pltpu.VMEM((depth, cols), BF16),
            pltpu.VMEM((SENT, depth), BF16),
            pltpu.VMEM((SENT, cols), BF16),
            pltpu.SemaphoreType.DMA((6,)),
            pltpu.SemaphoreType.DMA((2,)),
        ],
    )(*parts, names, up)


def column_block(hbm, by, core_flip, cols, side):
    me = lax.axis_index("tensor")
    chips = hbm.shape[1] // cols // 2
    chip = lax.rem(lax.div(me, 2) + by, chips)
    core = lax.rem(me + core_flip, 2)
    half = cols // 2
    return hbm.at[:, pl.ds(pl.multiple_of((chip * 2 + core) * cols + side * half, half), half)]


def side_of(side, cols):
    return pl.ds(side * (cols // 2), cols // 2)


def theirs_kernel(att_hbm, w_hbm, *refs, offsets):
    outs, (att_ref, w_ref, out_ref, in_sems, out_sems) = refs[: len(offsets)], refs[len(offsets) :]
    cols = out_ref.shape[2]
    att = start(att_hbm, att_ref, in_sems.at[len(offsets), 0])
    loads = {}
    for i, by in enumerate(offsets):
        for side in range(2):
            source = column_block(w_hbm, by, 1, cols, side)
            loads[i, side] = start(source, w_ref.at[i, :, side_of(side, cols)], in_sems.at[i, side])
    att.wait()
    stores = []
    for i in range(len(offsets)):
        for side in range(2):
            loads[i, side].wait()
            for n in range(side * (cols // 2), (side + 1) * (cols // 2), PIECE):
                these = slice(n, n + PIECE)
                out_ref[i, :, these] = dots(att_ref[...], w_ref.at[i], these).astype(BF16)
            these = side_of(side, cols)
            stores.append(start(out_ref.at[i, :, these], outs[i].at[:, these], out_sems.at[i, side]))
    wait(stores)


def theirs(attended, weight, offsets, cols):
    rows, width = attended.shape
    n = len(offsets)
    return call(
        functools.partial(theirs_kernel, offsets=offsets),
        "theirs",
        [HBM] * 2,
        [shape(rows, cols)] * n,
        [
            pltpu.VMEM((rows, width), BF16),
            pltpu.VMEM((n, width, cols), BF16),
            pltpu.VMEM((n, rows, cols), BF16),
            pltpu.SemaphoreType.DMA((n + 1, 2)),
            pltpu.SemaphoreType.DMA((n, 2)),
        ],
    )(attended, weight)


def mine_kernel(att_hbm, w_hbm, *refs, offsets, parts):
    count = len(offsets)
    others, outs = refs[:count], refs[count : count + count * parts]
    att_ref, w_ref, other_ref, out_ref, in_sems, out_sems = refs[count + count * parts :]
    rows, cols = att_ref.shape[0], out_ref.shape[2]
    att = start(att_hbm, att_ref, in_sems.at[count, 0])
    loads = {}
    for i, by in enumerate(offsets):
        for side in range(2):
            these = side_of(side, cols)
            loads[i, side] = [
                start(column_block(w_hbm, by, 0, cols, side), w_ref.at[i, :, these], in_sems.at[i, side]),
                start(others[i].at[:, these], other_ref.at[i, :, these], in_sems.at[i, 2 + side]),
            ]
    att.wait()
    stores = []
    for i in range(count):
        for side in range(2):
            wait(loads[i, side])
            for n in range(side * (cols // 2), (side + 1) * (cols // 2), PIECE):
                these = slice(n, n + PIECE)
                full = dots(att_ref[...], w_ref.at[i], these) + other_ref[i, :, these].astype(F32)
                out_ref[i, :, these] = full.astype(BF16)
            these = side_of(side, cols)
            for part in range(parts):
                source = out_ref.at[i, pl.ds(part * (rows // parts), rows // parts), these]
                stores.append(start(source, outs[i * parts + part].at[:, these], out_sems.at[i, side, part]))
    wait(stores)


def mine(attended, weight, others, offsets, cols, parts=1):
    rows, width = attended.shape
    count = len(offsets)
    return call(
        functools.partial(mine_kernel, offsets=offsets, parts=parts),
        "mine",
        [HBM] * (2 + count),
        [shape(rows // parts, cols)] * (count * parts),
        [
            pltpu.VMEM((rows, width), BF16),
            pltpu.VMEM((count, width, cols), BF16),
            pltpu.VMEM((count, rows, cols), BF16),
            pltpu.VMEM((count, rows, cols), BF16),
            pltpu.SemaphoreType.DMA((count + 1, 4)),
            pltpu.SemaphoreType.DMA((count, 2, parts)),
        ],
    )(attended, weight, *others)


def merge_kernel(r_hbm, l_hbm, from_left, from_right, to_right, to_left, near_ref, far_ref, in_sems, out_sems):
    half = near_ref.shape[1]
    pairs = []
    for i, (near, far) in enumerate(((r_hbm, from_left), (l_hbm, from_right))):
        source = near.at[pl.ds(i * half, half)]
        pairs.append([start(source, near_ref.at[i], in_sems.at[i, 0]), start(far, far_ref.at[i], in_sems.at[i, 1])])
    stores = []
    for i, target in enumerate((to_right, to_left)):
        wait(pairs[i])
        near_ref[i] = (near_ref[i].astype(F32) + far_ref[i].astype(F32)).astype(BF16)
        stores.append(start(near_ref.at[i], target.at[pl.ds(i * half, half)], out_sems.at[i]))
    wait(stores)


def merge(to_right, to_left, from_left, from_right):
    half, cols = from_left.shape
    rows = to_right.shape[0]
    return pl.pallas_call(
        merge_kernel,
        in_specs=[HBM] * 4,
        out_specs=[HBM] * 2,
        out_shape=[shape(rows, cols)] * 2,
        scratch_shapes=[
            pltpu.VMEM((2, half, cols), BF16),
            pltpu.VMEM((2, half, cols), BF16),
            pltpu.SemaphoreType.DMA((2, 2)),
            pltpu.SemaphoreType.DMA((2,)),
        ],
        input_output_aliases={0: 0, 1: 1},
        compiler_params=pltpu.CompilerParams(vmem_limit_bytes=VMEM_LIMIT),
        cost_estimate=pl.CostEstimate(flops=COST, bytes_accessed=COST, transcendentals=0),
        name="merge",
    )(to_right, to_left, from_left, from_right)


def picks_kernel(turn_ref, ids_ref, pick_hbm, pick_ref, sem):
    dst, place, _ = places(ids_ref[...])
    at = place - turn_ref[0] * TAKES
    slot = jnp.where((at >= 0) & (at < TAKES), dst * SLOTS + 1 + at, -1).astype(F32)
    column = jnp.transpose(jnp.broadcast_to(slot, (8, slot.shape[1])))[:, 0:1].astype(jnp.int32)
    pick_ref[...] = mask16(iota(pick_ref.shape, 1) == column)
    start(pick_ref, pick_hbm, sem).wait()


def picks(turn, ids):
    rows = ids.shape[1]
    return call(
        picks_kernel,
        "picks",
        [SMEM, VMEM],
        shape(rows, SENT),
        [pltpu.VMEM((rows, SENT), BF16), pltpu.SemaphoreType.DMA],
    )(turn, ids)


def finish_kernel(pick_hbm, back_hbm, *refs, bases):
    base_hbms, refs = refs[:bases], refs[bases:]
    out_hbm, back_ref = refs[:2]
    base_refs, (out_ref, pick_ref, in_sems, pick_sem, out_sems) = refs[2 : 2 + bases], refs[2 + bases :]
    cols = out_ref.shape[1]
    loads = []
    for side in range(2):
        these = side_of(side, cols)
        pairs = [*zip(base_hbms, base_refs), (back_hbm, back_ref)]
        loads.append([start(a.at[:, these], z.at[:, these], in_sems.at[side, i]) for i, (a, z) in enumerate(pairs)])
    pick = start(pick_hbm, pick_ref, pick_sem)
    stores = []
    pick.wait()
    for side in range(2):
        wait(loads[side])
        for n in range(side * (cols // 2), (side + 1) * (cols // 2), PIECE):
            these = slice(n, n + PIECE)
            base = base_refs[0][:, these].astype(F32)
            for ref in base_refs[1:]:
                base = base + ref[:, these].astype(F32)
            delta = dots(pick_ref[...], back_ref, these).astype(BF16).astype(F32)
            out_ref[:, these] = (base + delta).astype(BF16)
        these = side_of(side, cols)
        stores.append(start(out_ref.at[:, these], out_hbm.at[:, these], out_sems.at[side]))
    wait(stores)


def finish(pick, back, *bases):
    rows, cols = bases[0].shape
    count = len(bases)
    return call(
        functools.partial(finish_kernel, bases=count),
        "finish",
        [HBM] * (2 + count),
        shape(rows, cols),
        [pltpu.VMEM((SENT, cols), BF16)]
        + [pltpu.VMEM((rows, cols), base.dtype) for base in bases]
        + [
            pltpu.VMEM((rows, cols), BF16),
            pltpu.VMEM((rows, SENT), BF16),
            pltpu.SemaphoreType.DMA((2, 1 + count)),
            pltpu.SemaphoreType.DMA,
            pltpu.SemaphoreType.DMA((2,)),
        ],
    )(pick, back, *bases)


def add16(a, b):
    return (a.astype(F32) + b.astype(F32)).astype(BF16)


def per_device(
    query, new_key, new_value, cache_keys, cache_values, lengths, adapter_ids, out_weight, adapter_a, adapter_b
):
    tensor = lax.axis_size("tensor")
    cols = out_weight.shape[1] // tensor
    swap = [(i, i ^ 1) for i in range(tensor)]
    along = lambda by: [(i, (i + 2 * by) % tensor) for i in range(tensor)]
    right, left, across = along(1), along(-1), along(2)
    send = lambda x, perm: lax.ppermute(x, "tensor", perm)

    ids = adapter_ids.reshape(1, adapter_ids.shape[0])
    lens = lengths.reshape(1, lengths.shape[0])
    down = turned(jnp.transpose(adapter_a, (0, 2, 1)).reshape(ADP * RANK, adapter_a.shape[1]))
    up = adapter_b.reshape(ADP * RANK, adapter_b.shape[2])
    attended, outgoing, far = attend(
        query, new_key, new_value, cache_keys, cache_values, out_weight, lens, ids, cols
    )

    def exchange(x):
        x = x.reshape(GROUPS, SLOTS, x.shape[1])
        return lax.all_to_all(x, "dp", split_axis=0, concat_axis=0, tiled=True).reshape(SENT, x.shape[2])

    def pair_rank(arrived):
        part, names = rank_parts(arrived, down)
        return add16(part, send(part, swap)), names

    def all_ranks(pair):
        return pair, send(pair, right), send(pair, left), send(pair, across)

    arrived = exchange(outgoing)

    tie = lax.optimization_barrier
    far = send(far, swap)
    far_top, far_bot = mine(attended, out_weight, (far,), (2,), cols, parts=2)
    from_left, from_right = send(far_top, right), send(far_bot, left)
    attended, _ = tie((attended, far_top))
    *near, home = [send(x, swap) for x in theirs(attended, out_weight, (1, 3, 0), cols)]
    near, down = tie((near, down))
    to_right, to_left = mine(attended, out_weight, near, (1, 3), cols)
    arrived, down, to_right, to_left = tie((arrived, down, to_right, to_left))
    pair, names = pair_rank(arrived)
    pair, to_right, to_left, from_left, from_right = tie((pair, to_right, to_left, from_left, from_right))
    parts, (to_right, to_left) = tie((all_ranks(pair), merge(to_right, to_left, from_left, from_right)))
    delta, attended, ids = tie((deltas(parts, names, up), attended, ids))
    back = exchange(delta)
    (own,) = mine(attended, out_weight, (home,), (0,), cols)
    pick = picks(jnp.zeros((1,), jnp.int32), ids)
    out = finish(pick, back, own, send(to_right, right), send(to_left, left))

    fullest = jnp.max(arrived.reshape(GROUPS, SLOTS, -1)[:, 0, 0]).astype(jnp.int32)

    def more(state):
        return state[0] * TAKES < fullest

    def another(state):
        turn, out = state
        number = turn.reshape(1)
        pair, names = pair_rank(exchange(refill(number, ids, attended)))
        parts = all_ranks(pair)
        again = exchange(deltas(parts, names, up))
        return turn + 1, finish(picks(number, ids), again, out)

    return lax.while_loop(more, another, (jnp.int32(1), out))[1]


def solution(mesh):
    return jax.shard_map(
        per_device,
        mesh=mesh,
        in_specs=(
            P("dp", "tensor"),
            P("dp", "tensor"),
            P("dp", "tensor"),
            P("dp", None, "tensor"),
            P("dp", None, "tensor"),
            P("dp"),
            P("dp", None),
            P("tensor", None),
            P("dp", "tensor", None),
            P("dp", None, "tensor"),
        ),
        out_specs=P("dp", "tensor"),
        check_vma=False,
    )
```

time: 248 us -> 111 us (0.45)
  blocking collectives: 115 us -> 0 us
  Pallas kernels: 0 us -> 52.4 us
  waiting for transfers between devices: 58.6 us -> 27.8 us
  matrix products: 27.3 us -> 0 us
  starting transfers between devices: 4.54 us -> 24.6 us
  local copies, waits for them, and re-layouts: 17.9 us -> 0 us
  between operations: 13.6 us -> 1.05 us
  other arithmetic: 9.17 us -> 3.04 us
    all_to_all x1 -> x0, blocking collectives: 59.1 us -> none  [per_device(): lax.all_to_all(outgoing, 'dp', split_axis=0, concat_axis=0, tiled=True)]
    psum x1 -> x0, blocking collectives: 56.1 us -> none  [per_device(): summed = lax.psum(partial_rank, 'tensor').astype(jnp.bfloat16)]
    pallas_call x0 -> x11, Pallas kernels: none -> 52.4 us  [the longest x3 13.7 us: mine(): call(functools.partial(mine_kernel, offsets=offsets, parts=parts), 'mine'...]
    all_to_all x1 -> x2, waiting for transfers between devices: 58.6 us -> 7.88 us  [exchange(): lax.all_to_all(x, 'dp', split_axis=0, concat_axis=0, tiled=True)]
    dot_general x6 -> x0, matrix products: 27.3 us -> none  [the longest x1 15.6 us: per_device(): lax.dot_general(out_weight, attended, (((0,), (1,)), ((), ())), preferred...]
    ppermute x0 -> x12, waiting for transfers between devices: none -> 19.9 us  [per_device(): send = lambda x, perm: lax.ppermute(x, 'tensor', perm)]
    ppermute x0 -> x12, starting transfers between devices: none -> 12 us  [per_device(): send = lambda x, perm: lax.ppermute(x, 'tensor', perm)]
    all_to_all x1 -> x2, starting transfers between devices: 4.54 us -> 12.6 us  [exchange(): lax.all_to_all(x, 'dp', split_axis=0, concat_axis=0, tiled=True)]
  transfers between devices with their start and end apart: 2 -> 14, of which waited for: 1 -> 5; matrix products, arithmetic and copies ran while one was open for 7% -> 3% of each run, Pallas kernels for 0% -> 30%
where the time goes in v2:
time: 111 us; the launch traced here: 109 us
  Pallas kernels  52.4 us (47%)
  waiting for transfers between devices  27.8 us (25%)
  starting transfers between devices  24.6 us (22%)
  other arithmetic  3.04 us (3%)
    ppermute x12, waiting for transfers between devices, per_device(): send = lambda x, perm: lax.ppermute(x, 'tensor', perm)  19.9 us
    pallas_call x3, Pallas kernels, mine(): call(functools.partial(mine_kernel, offsets=offsets, parts=parts), 'mine'...  13.7 us
    all_to_all x2, starting transfers between devices, exchange(): lax.all_to_all(x, 'dp', split_axis=0, concat_axis=0, tiled=True)  12.6 us
    ppermute x12, starting transfers between devices, per_device(): send = lambda x, perm: lax.ppermute(x, 'tensor', perm)  12 us
    pallas_call x1, Pallas kernels, attend(): call(attend_kernel, 'attend', [HBM] * 6 + [VMEM] * 2, [shape(rows, width)...  9.12 us
    all_to_all x2, waiting for transfers between devices, exchange(): lax.all_to_all(x, 'dp', split_axis=0, concat_axis=0, tiled=True)  7.88 us
    pallas_call x1, Pallas kernels, theirs(): call(functools.partial(theirs_kernel, offsets=offsets), 'theirs', [HBM] *...  6.81 us
    pallas_call x1, Pallas kernels, rank_parts(): call(rank_kernel, 'rank_parts', [HBM] * 2, [shape(HALF, 128), shape(SENT,...  5.16 us
  transfers between devices with their start and end apart: 14, of which 5 were waited for; matrix products, arithmetic and copies ran while one was open for 3% of the time, Pallas kernels for 30%

profile of v2, /device:TPU:0, one launch (start us, length us, event | category | flops | bytes accessed | tf_op | source)
XLA Modules:
  0.0 109.1 jit_solution(15460446419701467091)
XLA Ops:
  0.0 9.1 %attend.1 = (bf16[512,1024]{1,0:T(8,128)(2,1)}, bf16[896,1024]{1,0:T(8,128)(2,1)}, bf16[512,1024]{1,0:T(8,128)(2,1)}) custom-call(bf16[512,1024]{1,0:T(8,128)(2,1)} %q_hbm.1, bf16[512,128]{1,0:T(8,128)(2,1)} %nk_hbm.1, bf16[512,128]{1,0:T(8,128)(2,1)} %nv_hbm.1, bf16[512,16,128]{2,1,0:T(8,128)(2,1)} %k_hbm.1, bf16[512,16,128]{2,1,0:T(8,128)(2,1)} %v_hbm.1, ...), custom_call_target="tpu_custom_call" | custom-call | flops 1024 | bytes 1024 | tf_op jit(solution)/shard_map/attend/pallas_call | solution.py:197
  9.1 0.1 collective-permute-start.4
  9.2 8.2 %all-to-all-start.2 = ((bf16[16,56,1024]{2,1,0:T(8,128)(2,1)}), bf16[16,56,1024]{2,1,0:T(8,128)(2,1)}, u32[]{:S(2)}, u32[]{:S(2)}) async-start(bf16[16,56,1024]{2,1,0:T(8,128)(2,1)} %bitcast.33), calls=%async_computation.2 | async-start | bytes 3670016 | tf_op jit(solution)/shard_map/all_to_all | solution.py:608
  17.4 0.0 collective-permute-done.4.refs_0_
  17.4 4.1 %mine.3 = (bf16[256,1024]{1,0:T(8,128)(2,1)}, bf16[256,1024]{1,0:T(8,128)(2,1)}) custom-call(bf16[512,1024]{1,0:T(8,128)(2,1)} %get-tuple-element.184.att_hbm, bf16[1024,8192]{1,0:T(8,128)(2,1)} %w_hbm.9, bf16[512,1024]{1,0:T(8,128)(2,1)} %collective-permute-done.4.refs_0_), custom_call_target="tpu_custom_call" | custom-call | flops 1024 | bytes 1024 | tf_op jit(solution)/shard_map/mine/pallas_call | solution.py:466
  21.5 6.8 %theirs.1 = (bf16[512,1024]{1,0:T(8,128)(2,1)}, bf16[512,1024]{1,0:T(8,128)(2,1)}, bf16[512,1024]{1,0:T(8,128)(2,1)}) custom-call(bf16[512,1024]{1,0:T(8,128)(2,1)} %get-tuple-element.184.att_hbm, bf16[1024,8192]{1,0:T(8,128)(2,1)} %w_hbm.9), custom_call_target="tpu_custom_call" | custom-call | flops 1024 | bytes 1024 | tf_op jit(solution)/shard_map/theirs/pallas_call | solution.py:418
  28.4 0.3 collective-permute-start.5
  28.6 0.3 collective-permute-start.6
  28.9 2.8 %collective-permute-start.9 = (bf16[256,1024]{1,0:T(8,128)(2,1)}, bf16[256,1024]{1,0:T(8,128)(2,1)}, u32[]{:S(2)}, u32[]{:S(2)}) collective-permute-start(bf16[256,1024]{1,0:T(8,128)(2,1)} %get-tuple-element.98), channel_id=1, source_target_pairs={{0,6},{1,7},{2,0},{3,1},{4,2},{5,3},{6,4},{7,5},{8,14},{9,15},{10,... | collective-permute-start | bytes 1572872 | tf_op jit(solution)/shard_map/ppermute | solution.py:596
  31.7 0.0 collective-permute-start.8
  31.7 2.8 %turned.1.a_hbm = bf16[1024,1024]{1,0:T(8,128)(2,1)} custom-call(bf16[1024,1024]{1,0:T(8,128)(2,1)} %bitcast.32), custom_call_target="tpu_custom_call" | custom-call | flops 1024 | bytes 1024 | tf_op jit(solution)/shard_map/turned/pallas_call | solution.py:262
  34.5 0.0 collective-permute-done.5.refs_0_
  34.5 0.0 collective-permute-done.6.refs_1_
  34.5 5.5 %mine.4 = (bf16[512,1024]{1,0:T(8,128)(2,1)}, bf16[512,1024]{1,0:T(8,128)(2,1)}) custom-call(bf16[512,1024]{1,0:T(8,128)(2,1)} %get-tuple-element.184.att_hbm, bf16[1024,8192]{1,0:T(8,128)(2,1)} %w_hbm.9, bf16[512,1024]{1,0:T(8,128)(2,1)} %collective-permute-done.5.refs_0_, bf16[512,1024]{1,0:T(8,128)(2,1)} %collective-permute-done.6.refs_1_), custom_call_target="tpu_custom_call" | custom-call | flops 1024 | bytes 1024 | tf_op jit(solution)/shard_map/mine/pallas_call | solution.py:466
  40.1 7.9 %all-to-all-done.2 = bf16[16,56,1024]{2,1,0:T(8,128)(2,1)} async-done(((bf16[16,56,1024]{2,1,0:T(8,128)(2,1)}), bf16[16,56,1024]{2,1,0:T(8,128)(2,1)}, u32[]{:S(2)}, u32[]{:S(2)}) %all-to-all-start.2) | async-done | bytes 1835040 | tf_op jit(solution)/shard_map/all_to_all | solution.py:608
  47.9 5.2 %rank_parts.2 = (bf16[448,128]{1,0:T(8,128)(2,1)}, s32[896,128]{1,0:T(8,128)}) custom-call(bf16[896,1024]{1,0:T(8,128)(2,1)} %bitcast.8.x_hbm, bf16[1024,1024]{1,0:T(8,128)(2,1)} %turned.1.a_hbm), custom_call_target="tpu_custom_call" | custom-call | flops 1024 | bytes 1024 | tf_op jit(solution)/shard_map/rank_parts/pallas_call | solution.py:317
  53.1 0.1 collective-permute-start.7
  53.2 1.5 %collective-permute-done.7 = bf16[448,128]{1,0:T(8,128)(2,1)S(1)} collective-permute-done((bf16[448,128]{1,0:T(8,128)(2,1)}, bf16[448,128]{1,0:T(8,128)(2,1)S(1)}, u32[]{:S(2)}, u32[]{:S(2)}) %collective-permute-start.7) | collective-permute-done | bytes 114720 | tf_op jit(solution)/shard_map/ppermute | solution.py:596
  54.7 1.6 %add_convert_fusion.1.p0_hbm = bf16[448,128]{1,0:T(8,128)(2,1)} fusion(bf16[448,128]{1,0:T(8,128)(2,1)S(1)} %collective-permute-done.7, bf16[448,128]{1,0:T(8,128)(2,1)} %get-tuple-element.95), kind=kLoop, calls=%fused_computation.1 | loop fusion | flops 229376 | bytes 344064 | tf_op jit(solution)/shard_map/convert_element_type | solution.py:585
  56.3 0.0 collective-permute-done.9.from_right
  56.3 0.0 collective-permute-done.8.from_left
  56.3 3.0 %collective-permute-start.12 = (bf16[448,128]{1,0:T(8,128)(2,1)}, bf16[448,128]{1,0:T(8,128)(2,1)}, u32[]{:S(2)}, u32[]{:S(2)}) collective-permute-start(bf16[448,128]{1,0:T(8,128)(2,1)} %add_convert_fusion.1.p0_hbm), channel_id=1, source_target_pairs={{0,4},{1,5},{2,6},{3,7},{4,0},{5,1},{6,2},{7,3},{8,12},{9,13},{10,... | collective-permute-start | bytes 344072 | tf_op jit(solution)/shard_map/ppermute | solution.py:596
  59.3 1.1 %collective-permute-start.11 = (bf16[448,128]{1,0:T(8,128)(2,1)}, bf16[448,128]{1,0:T(8,128)(2,1)}, u32[]{:S(2)}, u32[]{:S(2)}) collective-permute-start(bf16[448,128]{1,0:T(8,128)(2,1)} %add_convert_fusion.1.p0_hbm), channel_id=1, source_target_pairs={{0,6},{1,7},{2,0},{3,1},{4,2},{5,3},{6,4},{7,5},{8,14},{9,15},{10,... | collective-permute-start | bytes 344072 | tf_op jit(solution)/shard_map/ppermute | solution.py:596
  60.5 0.9 collective-permute-start.10
  61.4 2.5 %merge.1 = (bf16[512,1024]{1,0:T(8,128)(2,1)}, bf16[512,1024]{1,0:T(8,128)(2,1)}) custom-call(bf16[512,1024]{1,0:T(8,128)(2,1)} %get-tuple-element.100.r_hbm, bf16[512,1024]{1,0:T(8,128)(2,1)} %get-tuple-element.101.l_hbm, bf16[256,1024]{1,0:T(8,128)(2,1)} %collective-permute-done.8.from_left, ...), custom_call_target="tpu_custom_call", output_to_operand_aliasing={{0}: (0, {}), {1}: (1, {})} | custom-call | flops 1024 | bytes 1024 | tf_op jit(solution)/shard_map/merge/pallas_call | solution.py:499
  63.8 0.0 collective-permute-done.12.p3_hbm
  63.9 2.0 %collective-permute-done.11.p2_hbm = bf16[448,128]{1,0:T(8,128)(2,1)} collective-permute-done((bf16[448,128]{1,0:T(8,128)(2,1)}, bf16[448,128]{1,0:T(8,128)(2,1)}, u32[]{:S(2)}, u32[]{:S(2)}) %collective-permute-start.11) | collective-permute-done | bytes 114720 | tf_op jit(solution)/shard_map/ppermute | solution.py:596
  65.9 0.9 collective-permute-done.10.p1_hbm
  66.8 5.1 %deltas.2 = bf16[896,1024]{1,0:T(8,128)(2,1)} custom-call(bf16[448,128]{1,0:T(8,128)(2,1)} %add_convert_fusion.1.p0_hbm, bf16[448,128]{1,0:T(8,128)(2,1)} %collective-permute-done.10.p1_hbm, bf16[448,128]{1,0:T(8,128)(2,1)} %collective-permute-done.11.p2_hbm, bf16[448,128]{1,0:T(8,128)(2,1)} %collective-permute-done.12.p3_hbm, ...), custom_call_target="tpu_custom_call" | custom-call | flops 1024 | bytes 1024 | tf_op jit(solution)/shard_map/deltas/pallas_call | solution.py:363
  71.9 4.4 %all-to-all-start.3 = ((bf16[16,56,1024]{2,1,0:T(8,128)(2,1)}), bf16[16,56,1024]{2,1,0:T(8,128)(2,1)}, u32[]{:S(2)}, u32[]{:S(2)}) async-start(bf16[16,56,1024]{2,1,0:T(8,128)(2,1)} %bitcast.31), calls=%async_computation.3 | async-start | bytes 3670016 | tf_op jit(solution)/shard_map/all_to_all | solution.py:608
  76.4 0.1 collective-permute-start.13
  76.5 0.6 collective-permute-start.14
  77.0 2.7 %collective-permute-start.15 = (bf16[512,1024]{1,0:T(8,128)(2,1)}, bf16[512,1024]{1,0:T(8,128)(2,1)}, u32[]{:S(2)}, u32[]{:S(2)}) collective-permute-start(bf16[512,1024]{1,0:T(8,128)(2,1)} %get-tuple-element.116), channel_id=1, source_target_pairs={{0,6},{1,7},{2,0},{3,1},{4,2},{5,3},{6,4},{7,5},{8,14},{9,15},{10,... | collective-permute-start | bytes 3145736 | tf_op jit(solution)/shard_map/ppermute | solution.py:596
  79.8 1.5 %slice_reduce_fusion = bf16[]{:T(256)} fusion(bf16[16,56,1024]{2,1,0:T(8,128)(2,1)} %bitcast.14), kind=kLoop, calls=%fused_computation.2 | loop fusion | flops 15 | bytes 34 | tf_op jit(solution)/shard_map/reduce_max | solution.py:637
  81.9 2.2 %picks.2.pick_hbm = bf16[512,896]{1,0:T(8,128)(2,1)} custom-call(s32[1]{0:T(128)} %constant.3.clone.1.turn_ref, s32[1,512]{1,0:T(1,128)} %bitcast.35), custom_call_target="tpu_custom_call" | custom-call | flops 1024 | bytes 1024 | tf_op jit(solution)/shard_map/picks/pallas_call | solution.py:528
  84.1 0.0 collective-permute-done.13.refs_0_
  84.1 4.0 %mine.5.refs_0_ = bf16[512,1024]{1,0:T(8,128)(2,1)} custom-call(bf16[512,1024]{1,0:T(8,128)(2,1)} %get-tuple-element.184.att_hbm, bf16[1024,8192]{1,0:T(8,128)(2,1)} %w_hbm.9, bf16[512,1024]{1,0:T(8,128)(2,1)} %collective-permute-done.13.refs_0_), custom_call_target="tpu_custom_call" | custom-call | flops 1024 | bytes 1024 | tf_op jit(solution)/shard_map/mine/pallas_call | solution.py:466
  88.1 15.4 %collective-permute-done.14.refs_1_ = bf16[512,1024]{1,0:T(8,128)(2,1)} collective-permute-done((bf16[512,1024]{1,0:T(8,128)(2,1)}, bf16[512,1024]{1,0:T(8,128)(2,1)}, u32[]{:S(2)}, u32[]{:S(2)}) %collective-permute-start.14) | collective-permute-done | bytes 1048608 | tf_op jit(solution)/shard_map/ppermute | solution.py:596
  103.6 0.0 collective-permute-done.15.refs_2_
  103.6 0.0 all-to-all-done.3
  103.6 5.1 %finish.2 = bf16[512,1024]{1,0:T(8,128)(2,1)} custom-call(bf16[512,896]{1,0:T(8,128)(2,1)} %picks.2.pick_hbm, bf16[896,1024]{1,0:T(8,128)(2,1)} %bitcast.13.back_hbm, bf16[512,1024]{1,0:T(8,128)(2,1)} %mine.5.refs_0_, bf16[512,1024]{1,0:T(8,128)(2,1)} %collective-permute-done.14.refs_1_, bf16[512,1024]{1,0:T(8,128)(2,1)} %collective-permute-done.15.refs_2_), custom_call_target="tpu_custom_call" | custom-call | flops 1024 | bytes 1024 | tf_op jit(solution)/shard_map/finish/pallas_call | solution.py:567
  108.7 0.2 while.10
Async XLA Ops:
  9.1 8.3 %collective-permute-start.4 = (bf16[512,1024]{1,0:T(8,128)(2,1)}, bf16[512,1024]{1,0:T(8,128)(2,1)}, u32[]{:S(2)}, u32[]{:S(2)}) collective-permute-start(bf16[512,1024]{1,0:T(8,128)(2,1)} %get-tuple-element.83), channel_id=1, source_target_pairs={{0,1},{1,0},{2,3},{3,2},{4,5},{5,4},{6,7},{7,6},{8,9},{9,8},{10,11... | collective-permute-start | bytes 3145736 | tf_op jit(solution)/shard_map/ppermute | solution.py:596
  9.2 38.7 %all-to-all-start.2 = ((bf16[16,56,1024]{2,1,0:T(8,128)(2,1)}), bf16[16,56,1024]{2,1,0:T(8,128)(2,1)}, u32[]{:S(2)}, u32[]{:S(2)}) async-start(bf16[16,56,1024]{2,1,0:T(8,128)(2,1)} %bitcast.33), calls=%async_computation.2 | async-start | bytes 3670016 | tf_op jit(solution)/shard_map/all_to_all | solution.py:608
  28.4 6.1 %collective-permute-start.5 = (bf16[512,1024]{1,0:T(8,128)(2,1)}, bf16[512,1024]{1,0:T(8,128)(2,1)}, u32[]{:S(2)}, u32[]{:S(2)}) collective-permute-start(bf16[512,1024]{1,0:T(8,128)(2,1)} %get-tuple-element.86), channel_id=1, source_target_pairs={{0,1},{1,0},{2,3},{3,2},{4,5},{5,4},{6,7},{7,6},{8,9},{9,8},{10,11... | collective-permute-start | bytes 3145736 | tf_op jit(solution)/shard_map/ppermute | solution.py:596
  28.6 5.9 %collective-permute-start.6 = (bf16[512,1024]{1,0:T(8,128)(2,1)}, bf16[512,1024]{1,0:T(8,128)(2,1)}, u32[]{:S(2)}, u32[]{:S(2)}) collective-permute-start(bf16[512,1024]{1,0:T(8,128)(2,1)} %get-tuple-element.87), channel_id=1, source_target_pairs={{0,1},{1,0},{2,3},{3,2},{4,5},{5,4},{6,7},{7,6},{8,9},{9,8},{10,11... | collective-permute-start | bytes 3145736 | tf_op jit(solution)/shard_map/ppermute | solution.py:596
  28.9 27.4 %collective-permute-start.9 = (bf16[256,1024]{1,0:T(8,128)(2,1)}, bf16[256,1024]{1,0:T(8,128)(2,1)}, u32[]{:S(2)}, u32[]{:S(2)}) collective-permute-start(bf16[256,1024]{1,0:T(8,128)(2,1)} %get-tuple-element.98), channel_id=1, source_target_pairs={{0,6},{1,7},{2,0},{3,1},{4,2},{5,3},{6,4},{7,5},{8,14},{9,15},{10,... | collective-permute-start | bytes 1572872 | tf_op jit(solution)/shard_map/ppermute | solution.py:596
  31.7 24.6 %collective-permute-start.8 = (bf16[256,1024]{1,0:T(8,128)(2,1)}, bf16[256,1024]{1,0:T(8,128)(2,1)}, u32[]{:S(2)}, u32[]{:S(2)}) collective-permute-start(bf16[256,1024]{1,0:T(8,128)(2,1)} %get-tuple-element.84), channel_id=1, source_target_pairs={{0,2},{1,3},{2,4},{3,5},{4,6},{5,7},{6,0},{7,1},{8,10},{9,11},{10,... | collective-permute-start | bytes 1572872 | tf_op jit(solution)/shard_map/ppermute | solution.py:596
  53.1 1.6 %collective-permute-start.7 = (bf16[448,128]{1,0:T(8,128)(2,1)}, bf16[448,128]{1,0:T(8,128)(2,1)S(1)}, u32[]{:S(2)}, u32[]{:S(2)}) collective-permute-start(bf16[448,128]{1,0:T(8,128)(2,1)} %get-tuple-element.95), channel_id=1, source_target_pairs={{0,1},{1,0},{2,3},{3,2},{4,5},{5,4},{6,7},{7,6},{8,9},{9,8},{10,11... | collective-permute-start | bytes 344072 | tf_op jit(solution)/shard_map/ppermute | solution.py:596
  56.3 7.6 %collective-permute-start.12 = (bf16[448,128]{1,0:T(8,128)(2,1)}, bf16[448,128]{1,0:T(8,128)(2,1)}, u32[]{:S(2)}, u32[]{:S(2)}) collective-permute-start(bf16[448,128]{1,0:T(8,128)(2,1)} %add_convert_fusion.1.p0_hbm), channel_id=1, source_target_pairs={{0,4},{1,5},{2,6},{3,7},{4,0},{5,1},{6,2},{7,3},{8,12},{9,13},{10,... | collective-permute-start | bytes 344072 | tf_op jit(solution)/shard_map/ppermute | solution.py:596
  59.3 6.5 %collective-permute-start.11 = (bf16[448,128]{1,0:T(8,128)(2,1)}, bf16[448,128]{1,0:T(8,128)(2,1)}, u32[]{:S(2)}, u32[]{:S(2)}) collective-permute-start(bf16[448,128]{1,0:T(8,128)(2,1)} %add_convert_fusion.1.p0_hbm), channel_id=1, source_target_pairs={{0,6},{1,7},{2,0},{3,1},{4,2},{5,3},{6,4},{7,5},{8,14},{9,15},{10,... | collective-permute-start | bytes 344072 | tf_op jit(solution)/shard_map/ppermute | solution.py:596
  60.5 6.3 %collective-permute-start.10 = (bf16[448,128]{1,0:T(8,128)(2,1)}, bf16[448,128]{1,0:T(8,128)(2,1)}, u32[]{:S(2)}, u32[]{:S(2)}) collective-permute-start(bf16[448,128]{1,0:T(8,128)(2,1)} %add_convert_fusion.1.p0_hbm), channel_id=1, source_target_pairs={{0,2},{1,3},{2,4},{3,5},{4,6},{5,7},{6,0},{7,1},{8,10},{9,11},{10,... | collective-permute-start | bytes 344072 | tf_op jit(solution)/shard_map/ppermute | solution.py:596
  71.9 31.6 %all-to-all-start.3 = ((bf16[16,56,1024]{2,1,0:T(8,128)(2,1)}), bf16[16,56,1024]{2,1,0:T(8,128)(2,1)}, u32[]{:S(2)}, u32[]{:S(2)}) async-start(bf16[16,56,1024]{2,1,0:T(8,128)(2,1)} %bitcast.31), calls=%async_computation.3 | async-start | bytes 3670016 | tf_op jit(solution)/shard_map/all_to_all | solution.py:608
  76.4 7.7 %collective-permute-start.13 = (bf16[512,1024]{1,0:T(8,128)(2,1)}, bf16[512,1024]{1,0:T(8,128)(2,1)}, u32[]{:S(2)}, u32[]{:S(2)}) collective-permute-start(bf16[512,1024]{1,0:T(8,128)(2,1)} %get-tuple-element.114), channel_id=1, source_target_pairs={{0,1},{1,0},{2,3},{3,2},{4,5},{5,4},{6,7},{7,6},{8,9},{9,8},{10,11... | collective-permute-start | bytes 3145736 | tf_op jit(solution)/shard_map/ppermute | solution.py:596
  76.5 27.1 %collective-permute-start.14 = (bf16[512,1024]{1,0:T(8,128)(2,1)}, bf16[512,1024]{1,0:T(8,128)(2,1)}, u32[]{:S(2)}, u32[]{:S(2)}) collective-permute-start(bf16[512,1024]{1,0:T(8,128)(2,1)} %get-tuple-element.115), channel_id=1, source_target_pairs={{0,2},{1,3},{2,4},{3,5},{4,6},{5,7},{6,0},{7,1},{8,10},{9,11},{10,... | collective-permute-start | bytes 3145736 | tf_op jit(solution)/shard_map/ppermute | solution.py:596
  77.0 26.5 %collective-permute-start.15 = (bf16[512,1024]{1,0:T(8,128)(2,1)}, bf16[512,1024]{1,0:T(8,128)(2,1)}, u32[]{:S(2)}, u32[]{:S(2)}) collective-permute-start(bf16[512,1024]{1,0:T(8,128)(2,1)} %get-tuple-element.116), channel_id=1, source_target_pairs={{0,6},{1,7},{2,0},{3,1},{4,2},{5,3},{6,4},{7,5},{8,14},{9,15},{10,... | collective-permute-start | bytes 3145736 | tf_op jit(solution)/shard_map/ppermute | solution.py:596

commit v3 on v2

--- a/solution.py
+++ b/solution.py
@@ -20,7 +20,7 @@
 WIDE = SUB * SUB
 PACK = 448
 PIECE = 256
-BLOCK = 256
+BLOCKS = (128, 384)
 STEP = 512
 F32 = jnp.float32
 BF16 = jnp.bfloat16
@@ -130,12 +130,11 @@
 ):
     rows = len_ref.shape[1]
     subs = rows // SUB
-    blocks = rows // BLOCK
+    blocks = [pl.ds(sum(BLOCKS[:b]), BLOCKS[b]) for b in range(len(BLOCKS))]
     scale = 1.4426950408889634 / HD**0.5
     new = [start(nk_hbm, nk_ref, new_sems.at[0]), start(nv_hbm, nv_ref, new_sems.at[1])]
     loads = []
-    for b in range(blocks):
-        here = pl.ds(b * BLOCK, BLOCK)
+    for b, here in enumerate(blocks):
         pairs = ((q_hbm, q_ref), (k_hbm, k_ref), (v_hbm, v_ref))
         loads.append([start(a.at[here], z.at[here], in_sems.at[b, i]) for i, (a, z) in enumerate(pairs)])
 
@@ -157,16 +156,16 @@
     ones = jnp.ones((WIDE, 128), BF16)
     wait(new)
     stores = []
-    for b in range(blocks):
+    for b, block in enumerate(blocks):
         wait(loads[b])
-        for sub in range(BLOCK // SUB):
-            here = pl.ds(b * BLOCK + sub * SUB, SUB)
+        for sub in range(block.start, block.start + block.size, SUB):
+            here = pl.ds(sub, SUB)
             q = jnp.concatenate([q_ref[here, h * HD : (h + 1) * HD] for h in range(GROUP)], axis=0)
             k = k_ref[here].reshape(WIDE, HD)
             v = v_ref[here].reshape(WIDE, HD)
             nk = nk_ref[here, :].astype(F32)
             nv = nv_ref[here, :].astype(F32)
-            live = live_ref[pl.ds(b * (BLOCK // SUB) + sub, 1), :]
+            live = live_ref[pl.ds(sub // SUB, 1), :]
             s = lax.dot_general(q, k, NT, preferred_element_type=F32) + diagonal + live
             own = jnp.sum(q.astype(F32) * jnp.concatenate([nk] * GROUP, axis=0), axis=1, keepdims=True)
             top = jnp.maximum(jnp.max(s, axis=1, keepdims=True), own)
@@ -177,8 +176,7 @@
             mixed = (mixed * (1.0 / (both[:, HD:] + e_own))).astype(BF16)
             for h in range(GROUP):
                 att_ref[here, h * HD : (h + 1) * HD] = mixed[h * SUB : (h + 1) * SUB, :]
-        here = pl.ds(b * BLOCK, BLOCK)
-        stores.append(start(att_ref.at[here], att_hbm.at[here], att_sems.at[b]))
+        stores.append(start(att_ref.at[block], att_hbm.at[block], att_sems.at[b]))
     stores += pack_all(plan_ref, att_ref, out_ref, out_hbm, out_sems)
     for side in range(2):
         weights[side].wait()
@@ -193,7 +191,7 @@
 def attend(query, new_key, new_value, cache_keys, cache_values, weight, lengths, ids, cols):
     rows, width = query.shape
     slots = cache_keys.shape[1]
-    blocks = rows // BLOCK
+    blocks = len(BLOCKS)
     return call(
         attend_kernel,
         "attend",
@@ -245,34 +243,6 @@
     return pltpu.roll(x, RANK, 1)
 
 
-def turn_kernel(a_hbm, out_hbm, a_ref, out_ref, in_sems, out_sems):
-    rows = a_ref.shape[0]
-    starts = range(0, rows, PIECE)
-    loads = [start(a_hbm.at[pl.ds(n, PIECE)], a_ref.at[pl.ds(n, PIECE)], in_sems.at[i]) for i, n in enumerate(starts)]
-    stores = []
-    for i, n in enumerate(starts):
-        loads[i].wait()
-        out_ref[:, n : n + PIECE] = jnp.transpose(a_ref[n : n + PIECE, :])
-        stores.append(start(out_ref.at[:, pl.ds(n, PIECE)], out_hbm.at[:, pl.ds(n, PIECE)], out_sems.at[i]))
-    wait(stores)
-
-
-def turned(x):
-    rows, cols = x.shape
-    return call(
-        turn_kernel,
-        "turned",
-        [HBM],
-        shape(cols, rows),
-        [
-            pltpu.VMEM((rows, cols), BF16),
-            pltpu.VMEM((cols, rows), BF16),
-            pltpu.SemaphoreType.DMA((rows // PIECE,)),
-            pltpu.SemaphoreType.DMA((rows // PIECE,)),
-        ],
-    )(x)
-
-
 def rank_kernel(x_hbm, a_hbm, part_hbm, name_hbm, x_ref, a_ref, part_ref, name_ref, in_sems, out_sems):
     loads = []
     for half in range(2):
@@ -282,7 +252,7 @@
             downs = []
             for n in range(ADP * RANK // STEP):
                 these = pl.ds(n * STEP, STEP)
-                downs.append(start(a_hbm.at[:, these], a_ref.at[:, these], in_sems.at[2 + n]))
+                downs.append(start(a_hbm.at[these], a_ref.at[these], in_sems.at[2 + n]))
     upper = (iota((HALF, 128), 1) >= RANK).astype(jnp.int32)
     stores, totals = [], []
     for half in range(2):
@@ -301,7 +271,7 @@
         for n in range(ADP * RANK // STEP):
             if half == 0:
                 downs[n].wait()
-            full = dots(x_ref[here, :], a_ref, slice(n * STEP, (n + 1) * STEP))
+            full = lax.dot_general(x_ref[here, :], a_ref[n * STEP : (n + 1) * STEP, :], NT, preferred_element_type=F32)
             own = name - upper - n * (STEP // RANK)
             for t in range(STEP // 128):
                 total = total + jnp.where(own == 2 * t, full[:, t * 128 : (t + 1) * 128], 0.0)
@@ -321,7 +291,7 @@
         [shape(HALF, 128), shape(SENT, 128, jnp.int32)],
         [
             pltpu.VMEM((SENT, width), BF16),
-            pltpu.VMEM((width, ADP * RANK), BF16),
+            pltpu.VMEM((ADP * RANK, width), BF16),
             pltpu.VMEM((HALF, 128), BF16),
             pltpu.VMEM((SENT, 128), jnp.int32),
             pltpu.SemaphoreType.DMA((2 + ADP * RANK // STEP,)),
@@ -333,6 +303,7 @@
 def delta_kernel(
     p0_hbm, p1_hbm, p2_hbm, p3_hbm, name_hbm, b_hbm, out_hbm, p_ref, name_ref, b_ref, wide_ref, out_ref, in_sems, out_sems
 ):
+    cols = out_ref.shape[1]
     parts = [start(p, p_ref.at[i], in_sems.at[i]) for i, p in enumerate((p0_hbm, p1_hbm, p2_hbm, p3_hbm))]
     parts.append(start(name_hbm, name_ref, in_sems.at[4]))
     up = start(b_hbm, b_ref, in_sems.at[5])
@@ -351,10 +322,12 @@
             wide_ref[here, t * 128 : (t + 1) * 128] = jnp.where(name == 2 * t, own, 0.0).astype(BF16)
         if half == 0:
             up.wait()
-        for n in range(out_ref.shape[1] // PIECE):
-            these = slice(n * PIECE, (n + 1) * PIECE)
-            out_ref[here, these] = dots(wide_ref[here, :], b_ref, these).astype(BF16)
-        stores.append(start(out_ref.at[here], out_hbm.at[here], out_sems.at[half]))
+        for side in range(2):
+            for n in range(side * (cols // 2), (side + 1) * (cols // 2), PIECE):
+                these = slice(n, n + PIECE)
+                out_ref[here, these] = dots(wide_ref[here, :], b_ref, these).astype(BF16)
+            these = side_of(side, cols)
+            stores.append(start(out_ref.at[here, these], out_hbm.at[here, these], out_sems.at[half, side]))
     wait(stores)
 
 
@@ -372,7 +345,7 @@
             pltpu.VMEM((SENT, depth), BF16),
             pltpu.VMEM((SENT, cols), BF16),
             pltpu.SemaphoreType.DMA((6,)),
-            pltpu.SemaphoreType.DMA((2,)),
+            pltpu.SemaphoreType.DMA((2, 2)),
         ],
     )(*parts, names, up)
 
@@ -430,10 +403,11 @@
     )(attended, weight)
 
 
-def mine_kernel(att_hbm, w_hbm, *refs, offsets, parts):
+def mine_kernel(att_hbm, w_hbm, *refs, offsets, parts, more):
     count = len(offsets)
-    others, outs = refs[:count], refs[count : count + count * parts]
-    att_ref, w_ref, other_ref, out_ref, in_sems, out_sems = refs[count + count * parts :]
+    others, halves, refs = refs[:count], refs[count : count + more], refs[count + more :]
+    outs = list(refs[: sum(parts)])
+    att_ref, w_ref, other_ref, half_ref, out_ref, in_sems, out_sems = refs[sum(parts) :]
     rows, cols = att_ref.shape[0], out_ref.shape[2]
     att = start(att_hbm, att_ref, in_sems.at[count, 0])
     loads = {}
@@ -444,74 +418,74 @@
                 start(column_block(w_hbm, by, 0, cols, side), w_ref.at[i, :, these], in_sems.at[i, side]),
                 start(others[i].at[:, these], other_ref.at[i, :, these], in_sems.at[i, 2 + side]),
             ]
+    added = [start(x, half_ref.at[i], in_sems.at[count, 1 + i]) for i, x in enumerate(halves)]
     att.wait()
     stores = []
     for i in range(count):
+        targets = [outs.pop(0) for _ in range(parts[i])]
+        tall = rows // parts[i]
         for side in range(2):
             wait(loads[i, side])
             for n in range(side * (cols // 2), (side + 1) * (cols // 2), PIECE):
                 these = slice(n, n + PIECE)
                 full = dots(att_ref[...], w_ref.at[i], these) + other_ref[i, :, these].astype(F32)
+                if more:
+                    wait(added)
+                    added = []
+                    full = full + half_ref[:, :, these].reshape(full.shape).astype(F32)
                 out_ref[i, :, these] = full.astype(BF16)
             these = side_of(side, cols)
-            for part in range(parts):
-                source = out_ref.at[i, pl.ds(part * (rows // parts), rows // parts), these]
-                stores.append(start(source, outs[i * parts + part].at[:, these], out_sems.at[i, side, part]))
+            for part, target in enumerate(targets):
+                source = out_ref.at[i, pl.ds(part * tall, tall), these]
+                stores.append(start(source, target.at[:, these], out_sems.at[i, side, part]))
     wait(stores)
 
 
-def mine(attended, weight, others, offsets, cols, parts=1):
+def mine(attended, weight, others, offsets, cols, parts, halves=()):
     rows, width = attended.shape
     count = len(offsets)
     return call(
-        functools.partial(mine_kernel, offsets=offsets, parts=parts),
+        functools.partial(mine_kernel, offsets=offsets, parts=parts, more=len(halves)),
         "mine",
-        [HBM] * (2 + count),
-        [shape(rows // parts, cols)] * (count * parts),
+        [HBM] * (2 + count + len(halves)),
+        [shape(rows // n, cols) for n in parts for _ in range(n)],
         [
             pltpu.VMEM((rows, width), BF16),
             pltpu.VMEM((count, width, cols), BF16),
             pltpu.VMEM((count, rows, cols), BF16),
+            pltpu.VMEM((2, rows // 2, cols), BF16),
             pltpu.VMEM((count, rows, cols), BF16),
             pltpu.SemaphoreType.DMA((count + 1, 4)),
-            pltpu.SemaphoreType.DMA((count, 2, parts)),
-        ],
-    )(attended, weight, *others)
-
-
-def merge_kernel(r_hbm, l_hbm, from_left, from_right, to_right, to_left, near_ref, far_ref, in_sems, out_sems):
-    half = near_ref.shape[1]
-    pairs = []
-    for i, (near, far) in enumerate(((r_hbm, from_left), (l_hbm, from_right))):
-        source = near.at[pl.ds(i * half, half)]
-        pairs.append([start(source, near_ref.at[i], in_sems.at[i, 0]), start(far, far_ref.at[i], in_sems.at[i, 1])])
+            pltpu.SemaphoreType.DMA((count, 2, max(parts))),
+        ],
+    )(attended, weight, *others, *halves)
+
+
+def merge_kernel(a_hbm, b_hbm, c_hbm, d_hbm, ab_hbm, cd_hbm, in_ref, out_ref, in_sems, out_sems):
+    sources = (a_hbm, b_hbm, c_hbm, d_hbm)
+    loads = [start(x, in_ref.at[i], in_sems.at[i]) for i, x in enumerate(sources)]
     stores = []
-    for i, target in enumerate((to_right, to_left)):
-        wait(pairs[i])
-        near_ref[i] = (near_ref[i].astype(F32) + far_ref[i].astype(F32)).astype(BF16)
-        stores.append(start(near_ref.at[i], target.at[pl.ds(i * half, half)], out_sems.at[i]))
+    for i, target in enumerate((ab_hbm, cd_hbm)):
+        wait(loads[2 * i : 2 * i + 2])
+        out_ref[i] = (in_ref[2 * i].astype(F32) + in_ref[2 * i + 1].astype(F32)).astype(BF16)
+        stores.append(start(out_ref.at[i], target, out_sems.at[i]))
     wait(stores)
 
 
-def merge(to_right, to_left, from_left, from_right):
-    half, cols = from_left.shape
-    rows = to_right.shape[0]
-    return pl.pallas_call(
+def merge(a, b, c, d):
+    rows, cols = a.shape
+    return call(
         merge_kernel,
-        in_specs=[HBM] * 4,
-        out_specs=[HBM] * 2,
-        out_shape=[shape(rows, cols)] * 2,
-        scratch_shapes=[
-            pltpu.VMEM((2, half, cols), BF16),
-            pltpu.VMEM((2, half, cols), BF16),
-            pltpu.SemaphoreType.DMA((2, 2)),
+        "merge",
+        [HBM] * 4,
+        [shape(rows, cols)] * 2,
+        [
+            pltpu.VMEM((4, rows, cols), BF16),
+            pltpu.VMEM((2, rows, cols), BF16),
+            pltpu.SemaphoreType.DMA((4,)),
             pltpu.SemaphoreType.DMA((2,)),
         ],
-        input_output_aliases={0: 0, 1: 1},
-        compiler_params=pltpu.CompilerParams(vmem_limit_bytes=VMEM_LIMIT),
-        cost_estimate=pl.CostEstimate(flops=COST, bytes_accessed=COST, transcendentals=0),
-        name="merge",
-    )(to_right, to_left, from_left, from_right)
+    )(a, b, c, d)
 
 
 def picks_kernel(turn_ref, ids_ref, pick_hbm, pick_ref, sem):
@@ -534,26 +508,25 @@
     )(turn, ids)
 
 
-def finish_kernel(pick_hbm, back_hbm, *refs, bases):
-    base_hbms, refs = refs[:bases], refs[bases:]
-    out_hbm, back_ref = refs[:2]
-    base_refs, (out_ref, pick_ref, in_sems, pick_sem, out_sems) = refs[2 : 2 + bases], refs[2 + bases :]
-    cols = out_ref.shape[1]
-    loads = []
+def finish_kernel(pick_hbm, back_hbm, base_hbm, *refs, more):
+    halves, refs = refs[:more], refs[more:]
+    out_hbm, back_ref, base_ref, half_ref, out_ref, pick_ref, in_sems, more_sems, out_sems = refs
+    rows, cols = out_ref.shape
+    loads = [[start(pick_hbm, pick_ref, in_sems.at[0, 0])], []]
     for side in range(2):
         these = side_of(side, cols)
-        pairs = [*zip(base_hbms, base_refs), (back_hbm, back_ref)]
-        loads.append([start(a.at[:, these], z.at[:, these], in_sems.at[side, i]) for i, (a, z) in enumerate(pairs)])
-    pick = start(pick_hbm, pick_ref, pick_sem)
+        loads[side].append(start(back_hbm.at[:, these], back_ref.at[:, these], in_sems.at[side, 1]))
+        loads[side].append(start(base_hbm.at[:, these], base_ref.at[:, these], in_sems.at[side, 2]))
+        for i, x in enumerate(halves):
+            loads[side].append(start(x.at[:, these], half_ref.at[i, :, these], more_sems.at[side, i]))
     stores = []
-    pick.wait()
     for side in range(2):
         wait(loads[side])
         for n in range(side * (cols // 2), (side + 1) * (cols // 2), PIECE):
             these = slice(n, n + PIECE)
-            base = base_refs[0][:, these].astype(F32)
-            for ref in base_refs[1:]:
-                base = base + ref[:, these].astype(F32)
+            base = base_ref[:, these].astype(F32)
+            if more:
+                base = base + half_ref[:, :, these].reshape(base.shape).astype(F32)
             delta = dots(pick_ref[...], back_ref, these).astype(BF16).astype(F32)
             out_ref[:, these] = (base + delta).astype(BF16)
         these = side_of(side, cols)
@@ -561,24 +534,24 @@
     wait(stores)
 
 
-def finish(pick, back, *bases):
-    rows, cols = bases[0].shape
-    count = len(bases)
-    return call(
-        functools.partial(finish_kernel, bases=count),
+def finish(pick, back, base, halves=()):
+    rows, cols = base.shape
+    return call(
+        functools.partial(finish_kernel, more=len(halves)),
         "finish",
-        [HBM] * (2 + count),
+        [HBM] * (3 + len(halves)),
         shape(rows, cols),
-        [pltpu.VMEM((SENT, cols), BF16)]
-        + [pltpu.VMEM((rows, cols), base.dtype) for base in bases]
-        + [
+        [
+            pltpu.VMEM((SENT, cols), BF16),
+            pltpu.VMEM((rows, cols), BF16),
+            pltpu.VMEM((2, rows // 2, cols), BF16),
             pltpu.VMEM((rows, cols), BF16),
             pltpu.VMEM((rows, SENT), BF16),
-            pltpu.SemaphoreType.DMA((2, 1 + count)),
-            pltpu.SemaphoreType.DMA,
+            pltpu.SemaphoreType.DMA((2, 3)),
+            pltpu.SemaphoreType.DMA((2, 2)),
             pltpu.SemaphoreType.DMA((2,)),
         ],
-    )(pick, back, *bases)
+    )(pick, back, base, *halves)
 
 
 def add16(a, b):
@@ -597,7 +570,7 @@
 
     ids = adapter_ids.reshape(1, adapter_ids.shape[0])
     lens = lengths.reshape(1, lengths.shape[0])
-    down = turned(jnp.transpose(adapter_a, (0, 2, 1)).reshape(ADP * RANK, adapter_a.shape[1]))
+    down = jnp.transpose(adapter_a, (0, 2, 1)).reshape(ADP * RANK, adapter_a.shape[1])
     up = adapter_b.reshape(ADP * RANK, adapter_b.shape[2])
     attended, outgoing, far = attend(
         query, new_key, new_value, cache_keys, cache_values, out_weight, lens, ids, cols
@@ -618,21 +591,24 @@
 
     tie = lax.optimization_barrier
     far = send(far, swap)
-    far_top, far_bot = mine(attended, out_weight, (far,), (2,), cols, parts=2)
+    near = [send(x, swap) for x in theirs(attended, out_weight, (1, 3), cols)]
+    far_top, far_bot = mine(attended, out_weight, (far,), (2,), cols, (2,))
     from_left, from_right = send(far_top, right), send(far_bot, left)
-    attended, _ = tie((attended, far_top))
-    *near, home = [send(x, swap) for x in theirs(attended, out_weight, (1, 3, 0), cols)]
-    near, down = tie((near, down))
-    to_right, to_left = mine(attended, out_weight, near, (1, 3), cols)
-    arrived, down, to_right, to_left = tie((arrived, down, to_right, to_left))
+    right_top, right_bot, left_top, left_bot = mine(attended, out_weight, near, (1, 3), cols, (2, 2))
+    l_bot, r_top = send(right_bot, right), send(left_top, left)
+    arrived, right_top, left_bot = tie((arrived, right_top, left_bot))
     pair, names = pair_rank(arrived)
-    pair, to_right, to_left, from_left, from_right = tie((pair, to_right, to_left, from_left, from_right))
-    parts, (to_right, to_left) = tie((all_ranks(pair), merge(to_right, to_left, from_left, from_right)))
+    pair, right_top, left_bot, from_left, from_right, l_bot, r_top = tie(
+        (pair, right_top, left_bot, from_left, from_right, l_bot, r_top)
+    )
+    parts, (right_top, left_bot) = tie((all_ranks(pair), merge(right_top, from_left, left_bot, from_right)))
     delta, attended, ids = tie((deltas(parts, names, up), attended, ids))
     back = exchange(delta)
-    (own,) = mine(attended, out_weight, (home,), (0,), cols)
+    l_top, r_bot = send(right_top, right), send(left_bot, left)
+    (home,) = theirs(attended, out_weight, (0,), cols)
+    (own,) = mine(attended, out_weight, (send(home, swap),), (0,), cols, (1,), halves=(r_top, l_bot))
     pick = picks(jnp.zeros((1,), jnp.int32), ids)
-    out = finish(pick, back, own, send(to_right, right), send(to_left, left))
+    out = finish(pick, back, own, halves=(l_top, r_bot))
 
     fullest = jnp.max(arrived.reshape(GROUPS, SLOTS, -1)[:, 0, 0]).astype(jnp.int32)
 

time: 111 us -> 107 us (0.964); the launches traced: 109 us -> 106 us
  waiting for transfers between devices: 27.8 us -> 19.7 us
  starting transfers between devices: 24.6 us -> 30.9 us
    ppermute x12 -> x14, waiting for transfers between devices: 19.9 us -> 9.17 us  [per_device(): send = lambda x, perm: lax.ppermute(x, 'tensor', perm)]
    ppermute x12 -> x14, starting transfers between devices: 12 us -> 15.6 us  [per_device(): send = lambda x, perm: lax.ppermute(x, 'tensor', perm)]
    pallas_call x6 -> x5, Pallas kernels: 24.1 us -> 21.2 us  [the longest x3 14.5 us: mine(): call(functools.partial(mine_kernel, offsets=offsets, parts=parts, more=le...]
    all_to_all x2, starting transfers between devices: 12.6 us -> 15.3 us  [exchange(): lax.all_to_all(x, 'dp', split_axis=0, concat_axis=0, tiled=True)]
    all_to_all x2, waiting for transfers between devices: 7.88 us -> 10.5 us  [exchange(): lax.all_to_all(x, 'dp', split_axis=0, concat_axis=0, tiled=True)]
    pallas_call x1 -> x2, Pallas kernels: 6.81 us -> 9.1 us  [theirs(): call(functools.partial(theirs_kernel, offsets=offsets), 'theirs', [HBM] *...]
  transfers between devices with their start and end apart: 14 -> 16, of which waited for: 5 -> 8; matrix products, arithmetic and copies ran while one was open for 3% -> 3% of each run, Pallas kernels for 30% -> 32%
where the time goes in v3:
time: 107 us; the launch traced here: 106 us
  Pallas kernels  51.6 us (48%)
  starting transfers between devices  30.9 us (29%)
  waiting for transfers between devices  19.7 us (18%)
  other arithmetic  2.94 us (3%)
    ppermute x14, starting transfers between devices, per_device(): send = lambda x, perm: lax.ppermute(x, 'tensor', perm)  15.6 us
    all_to_all x2, starting transfers between devices, exchange(): lax.all_to_all(x, 'dp', split_axis=0, concat_axis=0, tiled=True)  15.3 us
    pallas_call x3, Pallas kernels, mine(): call(functools.partial(mine_kernel, offsets=offsets, parts=parts, more=le...  14.5 us
    all_to_all x2, waiting for transfers between devices, exchange(): lax.all_to_all(x, 'dp', split_axis=0, concat_axis=0, tiled=True)  10.5 us
    ppermute x14, waiting for transfers between devices, per_device(): send = lambda x, perm: lax.ppermute(x, 'tensor', perm)  9.17 us
    pallas_call x2, Pallas kernels, theirs(): call(functools.partial(theirs_kernel, offsets=offsets), 'theirs', [HBM] *...  9.1 us
    pallas_call x1, Pallas kernels, attend(): call(attend_kernel, 'attend', [HBM] * 6 + [VMEM] * 2, [shape(rows, width)...  8.97 us
    pallas_call x1, Pallas kernels, rank_parts(): call(rank_kernel, 'rank_parts', [HBM] * 2, [shape(HALF, 128), shape(SENT,...  5.21 us
  transfers between devices with their start and end apart: 16, of which 8 were waited for; matrix products, arithmetic and copies ran while one was open for 3% of the time, Pallas kernels for 32%

profile of v3, /device:TPU:0, one launch (start us, length us, event | category | flops | bytes accessed | tf_op | source)
XLA Modules:
  0.0 106.3 jit_solution(17246547248348774034)
XLA Ops:
  0.0 9.0 %attend.1 = (bf16[512,1024]{1,0:T(8,128)(2,1)}, bf16[896,1024]{1,0:T(8,128)(2,1)}, bf16[512,1024]{1,0:T(8,128)(2,1)}) custom-call(bf16[512,1024]{1,0:T(8,128)(2,1)} %q_hbm.1, bf16[512,128]{1,0:T(8,128)(2,1)} %nk_hbm.1, bf16[512,128]{1,0:T(8,128)(2,1)} %nv_hbm.1, bf16[512,16,128]{2,1,0:T(8,128)(2,1)} %k_hbm.1, bf16[512,16,128]{2,1,0:T(8,128)(2,1)} %v_hbm.1, ...), custom_call_target="tpu_custom_call" | custom-call | flops 1024 | bytes 1024 | tf_op jit(solution)/shard_map/attend/pallas_call | solution.py:195
  9.0 8.2 %all-to-all-start.2 = ((bf16[16,56,1024]{2,1,0:T(8,128)(2,1)}), bf16[16,56,1024]{2,1,0:T(8,128)(2,1)}, u32[]{:S(2)}, u32[]{:S(2)}) async-start(bf16[16,56,1024]{2,1,0:T(8,128)(2,1)} %bitcast.34), calls=%async_computation.2 | async-start | bytes 3670016 | tf_op jit(solution)/shard_map/all_to_all | solution.py:581
  17.2 0.1 collective-permute-start.7
  17.3 5.3 %theirs.2 = (bf16[512,1024]{1,0:T(8,128)(2,1)}, bf16[512,1024]{1,0:T(8,128)(2,1)}) custom-call(bf16[512,1024]{1,0:T(8,128)(2,1)} %get-tuple-element.180.att_hbm, bf16[1024,8192]{1,0:T(8,128)(2,1)} %w_hbm.11), custom_call_target="tpu_custom_call" | custom-call | flops 1024 | bytes 1024 | tf_op jit(solution)/shard_map/theirs/pallas_call | solution.py:391
  22.6 0.6 collective-permute-start.4
  23.1 0.1 collective-permute-start.5
  23.2 0.0 collective-permute-done.7.refs_0_
  23.2 4.1 %mine.4 = (bf16[256,1024]{1,0:T(8,128)(2,1)}, bf16[256,1024]{1,0:T(8,128)(2,1)}) custom-call(bf16[512,1024]{1,0:T(8,128)(2,1)} %get-tuple-element.180.att_hbm, bf16[1024,8192]{1,0:T(8,128)(2,1)} %w_hbm.11, bf16[512,1024]{1,0:T(8,128)(2,1)} %collective-permute-done.7.refs_0_), custom_call_target="tpu_custom_call" | custom-call | flops 1024 | bytes 1024 | tf_op jit(solution)/shard_map/mine/pallas_call | solution.py:447
  27.4 1.6 %collective-permute-start.8 = (bf16[256,1024]{1,0:T(8,128)(2,1)}, bf16[256,1024]{1,0:T(8,128)(2,1)}, u32[]{:S(2)}, u32[]{:S(2)}) collective-permute-start(bf16[256,1024]{1,0:T(8,128)(2,1)} %get-tuple-element.90), channel_id=1, source_target_pairs={{0,2},{1,3},{2,4},{3,5},{4,6},{5,7},{6,0},{7,1},{8,10},{9,11},{10,... | collective-permute-start | bytes 1572872 | tf_op jit(solution)/shard_map/ppermute | solution.py:569
  28.9 1.7 %collective-permute-start.9 = (bf16[256,1024]{1,0:T(8,128)(2,1)}, bf16[256,1024]{1,0:T(8,128)(2,1)}, u32[]{:S(2)}, u32[]{:S(2)}) collective-permute-start(bf16[256,1024]{1,0:T(8,128)(2,1)} %get-tuple-element.91), channel_id=1, source_target_pairs={{0,6},{1,7},{2,0},{3,1},{4,2},{5,3},{6,4},{7,5},{8,14},{9,15},{10,... | collective-permute-start | bytes 1572872 | tf_op jit(solution)/shard_map/ppermute | solution.py:569
  30.7 0.0 collective-permute-done.4.refs_0_
  30.7 0.0 collective-permute-done.5.refs_1_
  30.7 5.5 %mine.3 = (bf16[256,1024]{1,0:T(8,128)(2,1)}, bf16[256,1024]{1,0:T(8,128)(2,1)}, bf16[256,1024]{1,0:T(8,128)(2,1)}, bf16[256,1024]{1,0:T(8,128)(2,1)}) custom-call(bf16[512,1024]{1,0:T(8,128)(2,1)} %get-tuple-element.180.att_hbm, bf16[1024,8192]{1,0:T(8,128)(2,1)} %w_hbm.11, bf16[512,1024]{1,0:T(8,128)(2,1)} %collective-permute-done.4.refs_0_, ...), custom_call_target="tpu_custom_call" | custom-call | flops 1024 | bytes 1024 | tf_op jit(solution)/shard_map/mine/pallas_call | solution.py:447
  36.2 0.3 collective-permute-start.10
  36.5 3.0 %collective-permute-start.11 = (bf16[256,1024]{1,0:T(8,128)(2,1)}, bf16[256,1024]{1,0:T(8,128)(2,1)}, u32[]{:S(2)}, u32[]{:S(2)}) collective-permute-start(bf16[256,1024]{1,0:T(8,128)(2,1)} %get-tuple-element.93), channel_id=1, source_target_pairs={{0,6},{1,7},{2,0},{3,1},{4,2},{5,3},{6,4},{7,5},{8,14},{9,15},{10,... | collective-permute-start | bytes 1572872 | tf_op jit(solution)/shard_map/ppermute | solution.py:569
  39.5 5.6 %all-to-all-done.2 = bf16[16,56,1024]{2,1,0:T(8,128)(2,1)} async-done(((bf16[16,56,1024]{2,1,0:T(8,128)(2,1)}), bf16[16,56,1024]{2,1,0:T(8,128)(2,1)}, u32[]{:S(2)}, u32[]{:S(2)}) %all-to-all-start.2) | async-done | bytes 1835040 | tf_op jit(solution)/shard_map/all_to_all | solution.py:581
  45.1 5.2 %rank_parts.2 = (bf16[448,128]{1,0:T(8,128)(2,1)}, s32[896,128]{1,0:T(8,128)}) custom-call(bf16[896,1024]{1,0:T(8,128)(2,1)} %bitcast.8.x_hbm, bf16[1024,1024]{1,0:T(8,128)(2,1)} %bitcast.31), custom_call_target="tpu_custom_call" | custom-call | flops 1024 | bytes 1024 | tf_op jit(solution)/shard_map/rank_parts/pallas_call | solution.py:287
  50.4 0.1 collective-permute-start.6
  50.5 1.5 %collective-permute-done.6 = bf16[448,128]{1,0:T(8,128)(2,1)S(1)} collective-permute-done((bf16[448,128]{1,0:T(8,128)(2,1)}, bf16[448,128]{1,0:T(8,128)(2,1)S(1)}, u32[]{:S(2)}, u32[]{:S(2)}) %collective-permute-start.6) | collective-permute-done | bytes 114720 | tf_op jit(solution)/shard_map/ppermute | solution.py:569
  52.0 1.6 %add_convert_fusion.1.p0_hbm = bf16[448,128]{1,0:T(8,128)(2,1)} fusion(bf16[448,128]{1,0:T(8,128)(2,1)S(1)} %collective-permute-done.6, bf16[448,128]{1,0:T(8,128)(2,1)} %get-tuple-element.86), kind=kLoop, calls=%fused_computation.1 | loop fusion | flops 229376 | bytes 344064 | tf_op jit(solution)/shard_map/convert_element_type | solution.py:558
  53.6 0.0 collective-permute-done.8.b_hbm
  53.6 0.0 collective-permute-done.9.d_hbm
  53.6 0.9 collective-permute-done.10.refs_2_
  54.4 0.0 collective-permute-done.11.refs_1_
  54.5 2.7 %collective-permute-start.14 = (bf16[448,128]{1,0:T(8,128)(2,1)}, bf16[448,128]{1,0:T(8,128)(2,1)}, u32[]{:S(2)}, u32[]{:S(2)}) collective-permute-start(bf16[448,128]{1,0:T(8,128)(2,1)} %add_convert_fusion.1.p0_hbm), channel_id=1, source_target_pairs={{0,4},{1,5},{2,6},{3,7},{4,0},{5,1},{6,2},{7,3},{8,12},{9,13},{10,... | collective-permute-start | bytes 344072 | tf_op jit(solution)/shard_map/ppermute | solution.py:569
  57.2 1.4 %collective-permute-start.13 = (bf16[448,128]{1,0:T(8,128)(2,1)}, bf16[448,128]{1,0:T(8,128)(2,1)}, u32[]{:S(2)}, u32[]{:S(2)}) collective-permute-start(bf16[448,128]{1,0:T(8,128)(2,1)} %add_convert_fusion.1.p0_hbm), channel_id=1, source_target_pairs={{0,6},{1,7},{2,0},{3,1},{4,2},{5,3},{6,4},{7,5},{8,14},{9,15},{10,... | collective-permute-start | bytes 344072 | tf_op jit(solution)/shard_map/ppermute | solution.py:569
  58.6 0.6 collective-permute-start.12
  59.2 2.5 %merge.1 = (bf16[256,1024]{1,0:T(8,128)(2,1)}, bf16[256,1024]{1,0:T(8,128)(2,1)}) custom-call(bf16[256,1024]{1,0:T(8,128)(2,1)} %get-tuple-element.95.a_hbm, bf16[256,1024]{1,0:T(8,128)(2,1)} %collective-permute-done.8.b_hbm, bf16[256,1024]{1,0:T(8,128)(2,1)} %get-tuple-element.97.c_hbm, bf16[256,1024]{1,0:T(8,128)(2,1)} %collective-permute-done.9.d_hbm), custom_call_target="tpu_custom_call" | custom-call | flops 1024 | bytes 1024 | tf_op jit(solution)/shard_map/merge/pallas_call | solution.py:477
  61.7 0.2 collective-permute-done.14.p3_hbm
  61.9 1.5 %collective-permute-done.13.p2_hbm = bf16[448,128]{1,0:T(8,128)(2,1)} collective-permute-done((bf16[448,128]{1,0:T(8,128)(2,1)}, bf16[448,128]{1,0:T(8,128)(2,1)}, u32[]{:S(2)}, u32[]{:S(2)}) %collective-permute-start.13) | collective-permute-done | bytes 114720 | tf_op jit(solution)/shard_map/ppermute | solution.py:569
  63.4 1.5 %collective-permute-done.12.p1_hbm = bf16[448,128]{1,0:T(8,128)(2,1)} collective-permute-done((bf16[448,128]{1,0:T(8,128)(2,1)}, bf16[448,128]{1,0:T(8,128)(2,1)}, u32[]{:S(2)}, u32[]{:S(2)}) %collective-permute-start.12) | collective-permute-done | bytes 114720 | tf_op jit(solution)/shard_map/ppermute | solution.py:569
  64.9 5.0 %deltas.2 = bf16[896,1024]{1,0:T(8,128)(2,1)} custom-call(bf16[448,128]{1,0:T(8,128)(2,1)} %add_convert_fusion.1.p0_hbm, bf16[448,128]{1,0:T(8,128)(2,1)} %collective-permute-done.12.p1_hbm, bf16[448,128]{1,0:T(8,128)(2,1)} %collective-permute-done.13.p2_hbm, bf16[448,128]{1,0:T(8,128)(2,1)} %collective-permute-done.14.p3_hbm, ...), custom_call_target="tpu_custom_call" | custom-call | flops 1024 | bytes 1024 | tf_op jit(solution)/shard_map/deltas/pallas_call | solution.py:336
  69.9 7.2 %all-to-all-start.3 = ((bf16[16,56,1024]{2,1,0:T(8,128)(2,1)}), bf16[16,56,1024]{2,1,0:T(8,128)(2,1)}, u32[]{:S(2)}, u32[]{:S(2)}) async-start(bf16[16,56,1024]{2,1,0:T(8,128)(2,1)} %bitcast.33), calls=%async_computation.3 | async-start | bytes 3670016 | tf_op jit(solution)/shard_map/all_to_all | solution.py:581
  77.1 3.8 %theirs.3 = bf16[512,1024]{1,0:T(8,128)(2,1)} custom-call(bf16[512,1024]{1,0:T(8,128)(2,1)} %get-tuple-element.180.att_hbm, bf16[1024,8192]{1,0:T(8,128)(2,1)} %w_hbm.11), custom_call_target="tpu_custom_call" | custom-call | flops 1024 | bytes 1024 | tf_op jit(solution)/shard_map/theirs/pallas_call | solution.py:391
  80.9 0.1 collective-permute-start.15
  81.0 0.1 collective-permute-start.16
  81.1 3.2 %collective-permute-start.17 = (bf16[256,1024]{1,0:T(8,128)(2,1)}, bf16[256,1024]{1,0:T(8,128)(2,1)}, u32[]{:S(2)}, u32[]{:S(2)}) collective-permute-start(bf16[256,1024]{1,0:T(8,128)(2,1)} %get-tuple-element.112), channel_id=1, source_target_pairs={{0,6},{1,7},{2,0},{3,1},{4,2},{5,3},{6,4},{7,5},{8,14},{9,15},{10,... | collective-permute-start | bytes 1572872 | tf_op jit(solution)/shard_map/ppermute | solution.py:569
  84.3 1.4 %slice_reduce_fusion = bf16[]{:T(256)} fusion(bf16[16,56,1024]{2,1,0:T(8,128)(2,1)} %bitcast.14), kind=kLoop, calls=%fused_computation.2 | loop fusion | flops 15 | bytes 34 | tf_op jit(solution)/shard_map/reduce_max | solution.py:613
  86.2 2.2 %picks.2.pick_hbm = bf16[512,896]{1,0:T(8,128)(2,1)} custom-call(s32[1]{0:T(128)} %constant.3.clone.1.turn_ref, s32[1,512]{1,0:T(1,128)} %bitcast.36), custom_call_target="tpu_custom_call" | custom-call | flops 1024 | bytes 1024 | tf_op jit(solution)/shard_map/picks/pallas_call | solution.py:502
  88.4 0.0 collective-permute-done.15.refs_0_
  88.4 4.9 %mine.5.base_hbm = bf16[512,1024]{1,0:T(8,128)(2,1)} custom-call(bf16[512,1024]{1,0:T(8,128)(2,1)} %get-tuple-element.180.att_hbm, bf16[1024,8192]{1,0:T(8,128)(2,1)} %w_hbm.11, bf16[512,1024]{1,0:T(8,128)(2,1)} %collective-permute-done.15.refs_0_, bf16[256,1024]{1,0:T(8,128)(2,1)} %collective-permute-done.11.refs_1_, ...), custom_call_target="tpu_custom_call" | custom-call | flops 1024 | bytes 1024 | tf_op jit(solution)/shard_map/mine/pallas_call | solution.py:447
  93.3 3.5 %collective-permute-done.16.refs_0_ = bf16[256,1024]{1,0:T(8,128)(2,1)} collective-permute-done((bf16[256,1024]{1,0:T(8,128)(2,1)}, bf16[256,1024]{1,0:T(8,128)(2,1)}, u32[]{:S(2)}, u32[]{:S(2)}) %collective-permute-start.16) | collective-permute-done | bytes 524320 | tf_op jit(solution)/shard_map/ppermute | solution.py:569
  96.8 0.0 collective-permute-done.17.refs_1_
  96.8 4.8 %all-to-all-done.3 = bf16[16,56,1024]{2,1,0:T(8,128)(2,1)} async-done(((bf16[16,56,1024]{2,1,0:T(8,128)(2,1)}), bf16[16,56,1024]{2,1,0:T(8,128)(2,1)}, u32[]{:S(2)}, u32[]{:S(2)}) %all-to-all-start.3) | async-done | bytes 1835040 | tf_op jit(solution)/shard_map/all_to_all | solution.py:581
  101.7 4.1 %finish.2 = bf16[512,1024]{1,0:T(8,128)(2,1)} custom-call(bf16[512,896]{1,0:T(8,128)(2,1)} %picks.2.pick_hbm, bf16[896,1024]{1,0:T(8,128)(2,1)} %bitcast.13.back_hbm, bf16[512,1024]{1,0:T(8,128)(2,1)} %mine.5.base_hbm, bf16[256,1024]{1,0:T(8,128)(2,1)} %collective-permute-done.16.refs_0_, bf16[256,1024]{1,0:T(8,128)(2,1)} %collective-permute-done.17.refs_1_), custom_call_target="tpu_custom_call" | custom-call | flops 1024 | bytes 1024 | tf_op jit(solution)/shard_map/finish/pallas_call | solution.py:539
  105.8 0.2 while.10
Async XLA Ops:
  9.0 36.2 %all-to-all-start.2 = ((bf16[16,56,1024]{2,1,0:T(8,128)(2,1)}), bf16[16,56,1024]{2,1,0:T(8,128)(2,1)}, u32[]{:S(2)}, u32[]{:S(2)}) async-start(bf16[16,56,1024]{2,1,0:T(8,128)(2,1)} %bitcast.34), calls=%async_computation.2 | async-start | bytes 3670016 | tf_op jit(solution)/shard_map/all_to_all | solution.py:581
  17.2 6.1 %collective-permute-start.7 = (bf16[512,1024]{1,0:T(8,128)(2,1)}, bf16[512,1024]{1,0:T(8,128)(2,1)}, u32[]{:S(2)}, u32[]{:S(2)}) collective-permute-start(bf16[512,1024]{1,0:T(8,128)(2,1)} %get-tuple-element.89), channel_id=1, source_target_pairs={{0,1},{1,0},{2,3},{3,2},{4,5},{5,4},{6,7},{7,6},{8,9},{9,8},{10,11... | collective-permute-start | bytes 3145736 | tf_op jit(solution)/shard_map/ppermute | solution.py:569
  22.6 8.1 %collective-permute-start.4 = (bf16[512,1024]{1,0:T(8,128)(2,1)}, bf16[512,1024]{1,0:T(8,128)(2,1)}, u32[]{:S(2)}, u32[]{:S(2)}) collective-permute-start(bf16[512,1024]{1,0:T(8,128)(2,1)} %get-tuple-element.81), channel_id=1, source_target_pairs={{0,1},{1,0},{2,3},{3,2},{4,5},{5,4},{6,7},{7,6},{8,9},{9,8},{10,11... | collective-permute-start | bytes 3145736 | tf_op jit(solution)/shard_map/ppermute | solution.py:569
  23.1 7.5 %collective-permute-start.5 = (bf16[512,1024]{1,0:T(8,128)(2,1)}, bf16[512,1024]{1,0:T(8,128)(2,1)}, u32[]{:S(2)}, u32[]{:S(2)}) collective-permute-start(bf16[512,1024]{1,0:T(8,128)(2,1)} %get-tuple-element.82), channel_id=1, source_target_pairs={{0,1},{1,0},{2,3},{3,2},{4,5},{5,4},{6,7},{7,6},{8,9},{9,8},{10,11... | collective-permute-start | bytes 3145736 | tf_op jit(solution)/shard_map/ppermute | solution.py:569
  27.4 26.2 %collective-permute-start.8 = (bf16[256,1024]{1,0:T(8,128)(2,1)}, bf16[256,1024]{1,0:T(8,128)(2,1)}, u32[]{:S(2)}, u32[]{:S(2)}) collective-permute-start(bf16[256,1024]{1,0:T(8,128)(2,1)} %get-tuple-element.90), channel_id=1, source_target_pairs={{0,2},{1,3},{2,4},{3,5},{4,6},{5,7},{6,0},{7,1},{8,10},{9,11},{10,... | collective-permute-start | bytes 1572872 | tf_op jit(solution)/shard_map/ppermute | solution.py:569
  28.9 24.6 %collective-permute-start.9 = (bf16[256,1024]{1,0:T(8,128)(2,1)}, bf16[256,1024]{1,0:T(8,128)(2,1)}, u32[]{:S(2)}, u32[]{:S(2)}) collective-permute-start(bf16[256,1024]{1,0:T(8,128)(2,1)} %get-tuple-element.91), channel_id=1, source_target_pairs={{0,6},{1,7},{2,0},{3,1},{4,2},{5,3},{6,4},{7,5},{8,14},{9,15},{10,... | collective-permute-start | bytes 1572872 | tf_op jit(solution)/shard_map/ppermute | solution.py:569
  36.2 18.3 %collective-permute-start.10 = (bf16[256,1024]{1,0:T(8,128)(2,1)}, bf16[256,1024]{1,0:T(8,128)(2,1)}, u32[]{:S(2)}, u32[]{:S(2)}) collective-permute-start(bf16[256,1024]{1,0:T(8,128)(2,1)} %get-tuple-element.92), channel_id=1, source_target_pairs={{0,2},{1,3},{2,4},{3,5},{4,6},{5,7},{6,0},{7,1},{8,10},{9,11},{10,... | collective-permute-start | bytes 1572872 | tf_op jit(solution)/shard_map/ppermute | solution.py:569
  36.5 17.9 %collective-permute-start.11 = (bf16[256,1024]{1,0:T(8,128)(2,1)}, bf16[256,1024]{1,0:T(8,128)(2,1)}, u32[]{:S(2)}, u32[]{:S(2)}) collective-permute-start(bf16[256,1024]{1,0:T(8,128)(2,1)} %get-tuple-element.93), channel_id=1, source_target_pairs={{0,6},{1,7},{2,0},{3,1},{4,2},{5,3},{6,4},{7,5},{8,14},{9,15},{10,... | collective-permute-start | bytes 1572872 | tf_op jit(solution)/shard_map/ppermute | solution.py:569
  50.4 1.6 %collective-permute-start.6 = (bf16[448,128]{1,0:T(8,128)(2,1)}, bf16[448,128]{1,0:T(8,128)(2,1)S(1)}, u32[]{:S(2)}, u32[]{:S(2)}) collective-permute-start(bf16[448,128]{1,0:T(8,128)(2,1)} %get-tuple-element.86), channel_id=1, source_target_pairs={{0,1},{1,0},{2,3},{3,2},{4,5},{5,4},{6,7},{7,6},{8,9},{9,8},{10,11... | collective-permute-start | bytes 344072 | tf_op jit(solution)/shard_map/ppermute | solution.py:569
  54.5 7.5 %collective-permute-start.14 = (bf16[448,128]{1,0:T(8,128)(2,1)}, bf16[448,128]{1,0:T(8,128)(2,1)}, u32[]{:S(2)}, u32[]{:S(2)}) collective-permute-start(bf16[448,128]{1,0:T(8,128)(2,1)} %add_convert_fusion.1.p0_hbm), channel_id=1, source_target_pairs={{0,4},{1,5},{2,6},{3,7},{4,0},{5,1},{6,2},{7,3},{8,12},{9,13},{10,... | collective-permute-start | bytes 344072 | tf_op jit(solution)/shard_map/ppermute | solution.py:569
  57.2 6.2 %collective-permute-start.13 = (bf16[448,128]{1,0:T(8,128)(2,1)}, bf16[448,128]{1,0:T(8,128)(2,1)}, u32[]{:S(2)}, u32[]{:S(2)}) collective-permute-start(bf16[448,128]{1,0:T(8,128)(2,1)} %add_convert_fusion.1.p0_hbm), channel_id=1, source_target_pairs={{0,6},{1,7},{2,0},{3,1},{4,2},{5,3},{6,4},{7,5},{8,14},{9,15},{10,... | collective-permute-start | bytes 344072 | tf_op jit(solution)/shard_map/ppermute | solution.py:569
  58.6 6.3 %collective-permute-start.12 = (bf16[448,128]{1,0:T(8,128)(2,1)}, bf16[448,128]{1,0:T(8,128)(2,1)}, u32[]{:S(2)}, u32[]{:S(2)}) collective-permute-start(bf16[448,128]{1,0:T(8,128)(2,1)} %add_convert_fusion.1.p0_hbm), channel_id=1, source_target_pairs={{0,2},{1,3},{2,4},{3,5},{4,6},{5,7},{6,0},{7,1},{8,10},{9,11},{10,... | collective-permute-start | bytes 344072 | tf_op jit(solution)/shard_map/ppermute | solution.py:569
  69.9 31.8 %all-to-all-start.3 = ((bf16[16,56,1024]{2,1,0:T(8,128)(2,1)}), bf16[16,56,1024]{2,1,0:T(8,128)(2,1)}, u32[]{:S(2)}, u32[]{:S(2)}) async-start(bf16[16,56,1024]{2,1,0:T(8,128)(2,1)} %bitcast.33), calls=%async_computation.3 | async-start | bytes 3670016 | tf_op jit(solution)/shard_map/all_to_all | solution.py:581
  80.9 7.5 %collective-permute-start.15 = (bf16[512,1024]{1,0:T(8,128)(2,1)}, bf16[512,1024]{1,0:T(8,128)(2,1)}, u32[]{:S(2)}, u32[]{:S(2)}) collective-permute-start(bf16[512,1024]{1,0:T(8,128)(2,1)} %theirs.3), channel_id=1, source_target_pairs={{0,1},{1,0},{2,3},{3,2},{4,5},{5,4},{6,7},{7,6},{8,9},{9,8},{10,11... | collective-permute-start | bytes 3145736 | tf_op jit(solution)/shard_map/ppermute | solution.py:569
  81.0 15.9 %collective-permute-start.16 = (bf16[256,1024]{1,0:T(8,128)(2,1)}, bf16[256,1024]{1,0:T(8,128)(2,1)}, u32[]{:S(2)}, u32[]{:S(2)}) collective-permute-start(bf16[256,1024]{1,0:T(8,128)(2,1)} %get-tuple-element.111), channel_id=1, source_target_pairs={{0,2},{1,3},{2,4},{3,5},{4,6},{5,7},{6,0},{7,1},{8,10},{9,11},{10,... | collective-permute-start | bytes 1572872 | tf_op jit(solution)/shard_map/ppermute | solution.py:569
  81.1 15.8 %collective-permute-start.17 = (bf16[256,1024]{1,0:T(8,128)(2,1)}, bf16[256,1024]{1,0:T(8,128)(2,1)}, u32[]{:S(2)}, u32[]{:S(2)}) collective-permute-start(bf16[256,1024]{1,0:T(8,128)(2,1)} %get-tuple-element.112), channel_id=1, source_target_pairs={{0,6},{1,7},{2,0},{3,1},{4,2},{5,3},{6,4},{7,5},{8,14},{9,15},{10,... | collective-permute-start | bytes 1572872 | tf_op jit(solution)/shard_map/ppermute | solution.py:569

commit v4 on v3

--- a/solution.py
+++ b/solution.py
@@ -20,7 +20,7 @@
 WIDE = SUB * SUB
 PACK = 448
 PIECE = 256
-BLOCKS = (128, 384)
+BLOCK = 256
 STEP = 512
 F32 = jnp.float32
 BF16 = jnp.bfloat16
@@ -29,6 +29,8 @@
 NEG = -1e30
 VMEM_LIMIT = 64 * 1024 * 1024 - 64 * 1024
 COST = 1024
+ROOM = 960 * 1024
+SIDES = 2
 HBM = pl.BlockSpec(memory_space=pltpu.HBM)
 VMEM = pl.BlockSpec(memory_space=pltpu.VMEM)
 SMEM = pl.BlockSpec(memory_space=pltpu.SMEM)
@@ -42,7 +44,7 @@
     return cond.astype(F32).astype(BF16)
 
 
-def call(kernel, name, in_specs, out_shape, scratch, cost=None):
+def call(kernel, name, in_specs, out_shape, scratch, room=0):
     single = not isinstance(out_shape, list)
     return pl.pallas_call(
         kernel,
@@ -50,7 +52,7 @@
         out_specs=HBM if single else [HBM] * len(out_shape),
         out_shape=out_shape,
         scratch_shapes=scratch,
-        compiler_params=pltpu.CompilerParams(vmem_limit_bytes=VMEM_LIMIT),
+        compiler_params=pltpu.CompilerParams(vmem_limit_bytes=VMEM_LIMIT - room),
         cost_estimate=pl.CostEstimate(flops=COST, bytes_accessed=COST, transcendentals=0),
         name=name,
     )
@@ -123,26 +125,20 @@
 
 
 def attend_kernel(
-    q_hbm, nk_hbm, nv_hbm, k_hbm, v_hbm, w_hbm, len_ref, ids_ref,
-    att_hbm, out_hbm, far_hbm,
-    q_ref, nk_ref, nv_ref, k_ref, v_ref, w_ref, live_ref, plan_ref, att_ref, out_ref, far_ref,
-    in_sems, new_sems, w_sems, att_sems, out_sems, far_sems,
+    q_hbm, nk_hbm, nv_hbm, k_hbm, v_hbm, len_ref, ids_ref,
+    att_hbm, out_hbm,
+    q_ref, nk_ref, nv_ref, k_ref, v_ref, live_ref, plan_ref, att_ref, out_ref, in_sems, new_sems, att_sems, out_sems,
 ):
     rows = len_ref.shape[1]
     subs = rows // SUB
-    blocks = [pl.ds(sum(BLOCKS[:b]), BLOCKS[b]) for b in range(len(BLOCKS))]
+    blocks = rows // BLOCK
     scale = 1.4426950408889634 / HD**0.5
     new = [start(nk_hbm, nk_ref, new_sems.at[0]), start(nv_hbm, nv_ref, new_sems.at[1])]
     loads = []
-    for b, here in enumerate(blocks):
+    for b in range(blocks):
+        here = pl.ds(b * BLOCK, BLOCK)
         pairs = ((q_hbm, q_ref), (k_hbm, k_ref), (v_hbm, v_ref))
         loads.append([start(a.at[here], z.at[here], in_sems.at[b, i]) for i, (a, z) in enumerate(pairs)])
-
-    cols = far_ref.shape[1]
-    weights = []
-    for side in range(2):
-        source = column_block(w_hbm, 2, 1, cols, side)
-        weights.append(start(source, w_ref.at[:, side_of(side, cols)], w_sems.at[side]))
 
     lens = len_ref[...].astype(F32)
     own = jnp.where(lax.shift_right_logical(iota((subs, rows), 1), 4) == iota((subs, rows), 0), lens, 0.0)
@@ -156,16 +152,16 @@
     ones = jnp.ones((WIDE, 128), BF16)
     wait(new)
     stores = []
-    for b, block in enumerate(blocks):
+    for b in range(blocks):
         wait(loads[b])
-        for sub in range(block.start, block.start + block.size, SUB):
-            here = pl.ds(sub, SUB)
+        for sub in range(BLOCK // SUB):
+            here = pl.ds(b * BLOCK + sub * SUB, SUB)
             q = jnp.concatenate([q_ref[here, h * HD : (h + 1) * HD] for h in range(GROUP)], axis=0)
             k = k_ref[here].reshape(WIDE, HD)
             v = v_ref[here].reshape(WIDE, HD)
             nk = nk_ref[here, :].astype(F32)
             nv = nv_ref[here, :].astype(F32)
-            live = live_ref[pl.ds(sub // SUB, 1), :]
+            live = live_ref[pl.ds(b * (BLOCK // SUB) + sub, 1), :]
             s = lax.dot_general(q, k, NT, preferred_element_type=F32) + diagonal + live
             own = jnp.sum(q.astype(F32) * jnp.concatenate([nk] * GROUP, axis=0), axis=1, keepdims=True)
             top = jnp.maximum(jnp.max(s, axis=1, keepdims=True), own)
@@ -176,47 +172,37 @@
             mixed = (mixed * (1.0 / (both[:, HD:] + e_own))).astype(BF16)
             for h in range(GROUP):
                 att_ref[here, h * HD : (h + 1) * HD] = mixed[h * SUB : (h + 1) * SUB, :]
-        stores.append(start(att_ref.at[block], att_hbm.at[block], att_sems.at[b]))
+        here = pl.ds(b * BLOCK, BLOCK)
+        stores.append(start(att_ref.at[here], att_hbm.at[here], att_sems.at[b]))
     stores += pack_all(plan_ref, att_ref, out_ref, out_hbm, out_sems)
-    for side in range(2):
-        weights[side].wait()
-        for n in range(side * (cols // 2), (side + 1) * (cols // 2), PIECE):
-            these = slice(n, n + PIECE)
-            far_ref[:, these] = dots(att_ref[...], w_ref, these).astype(BF16)
-        these = side_of(side, cols)
-        stores.append(start(far_ref.at[:, these], far_hbm.at[:, these], far_sems.at[side]))
     wait(stores)
 
 
-def attend(query, new_key, new_value, cache_keys, cache_values, weight, lengths, ids, cols):
+def attend(query, new_key, new_value, cache_keys, cache_values, lengths, ids):
     rows, width = query.shape
     slots = cache_keys.shape[1]
-    blocks = len(BLOCKS)
+    blocks = rows // BLOCK
     return call(
         attend_kernel,
         "attend",
-        [HBM] * 6 + [VMEM] * 2,
-        [shape(rows, width), shape(SENT, width), shape(rows, cols)],
+        [HBM] * 5 + [VMEM] * 2,
+        [shape(rows, width), shape(SENT, width)],
         [
             pltpu.VMEM((rows, width), BF16),
             pltpu.VMEM((rows, HD), BF16),
             pltpu.VMEM((rows, HD), BF16),
             pltpu.VMEM((rows, slots, HD), BF16),
             pltpu.VMEM((rows, slots, HD), BF16),
-            pltpu.VMEM((width, cols), BF16),
             pltpu.VMEM((rows // SUB, WIDE), F32),
             pltpu.VMEM((8, rows), jnp.int32),
             pltpu.VMEM((rows, width), BF16),
             pltpu.VMEM((SENT, width), BF16),
-            pltpu.VMEM((rows, cols), BF16),
             pltpu.SemaphoreType.DMA((blocks, 3)),
-            pltpu.SemaphoreType.DMA((2,)),
             pltpu.SemaphoreType.DMA((2,)),
             pltpu.SemaphoreType.DMA((blocks,)),
             pltpu.SemaphoreType.DMA((SENT // PACK,)),
-            pltpu.SemaphoreType.DMA((2,)),
-        ],
-    )(query, new_key, new_value, cache_keys, cache_values, weight, lengths, ids)
+        ],
+    )(query, new_key, new_value, cache_keys, cache_values, lengths, ids)
 
 
 def refill_kernel(turn_ref, ids_ref, att_ref, out_hbm, plan_ref, out_ref, sems):
@@ -297,6 +283,7 @@
             pltpu.SemaphoreType.DMA((2 + ADP * RANK // STEP,)),
             pltpu.SemaphoreType.DMA((3,)),
         ],
+        room=ROOM,
     )(arrived, down)
 
 
@@ -306,7 +293,10 @@
     cols = out_ref.shape[1]
     parts = [start(p, p_ref.at[i], in_sems.at[i]) for i, p in enumerate((p0_hbm, p1_hbm, p2_hbm, p3_hbm))]
     parts.append(start(name_hbm, name_ref, in_sems.at[4]))
-    up = start(b_hbm, b_ref, in_sems.at[5])
+    ups = []
+    for side in range(2):
+        these = side_of(side, cols)
+        ups.append(start(b_hbm.at[:, these], b_ref.at[:, these], in_sems.at[5 + side]))
     wait(parts)
     rank = (p_ref[0].astype(F32) + p_ref[1].astype(F32)) + (p_ref[2].astype(F32) + p_ref[3].astype(F32))
     rank = rank.astype(BF16).astype(F32)
@@ -320,9 +310,9 @@
         name = name_ref[here, :] - upper
         for t in range(ADP * RANK // 128):
             wide_ref[here, t * 128 : (t + 1) * 128] = jnp.where(name == 2 * t, own, 0.0).astype(BF16)
-        if half == 0:
-            up.wait()
         for side in range(2):
+            if half == 0:
+                ups[side].wait()
             for n in range(side * (cols // 2), (side + 1) * (cols // 2), PIECE):
                 these = slice(n, n + PIECE)
                 out_ref[here, these] = dots(wide_ref[here, :], b_ref, these).astype(BF16)
@@ -344,7 +334,7 @@
             pltpu.VMEM((depth, cols), BF16),
             pltpu.VMEM((SENT, depth), BF16),
             pltpu.VMEM((SENT, cols), BF16),
-            pltpu.SemaphoreType.DMA((6,)),
+            pltpu.SemaphoreType.DMA((7,)),
             pltpu.SemaphoreType.DMA((2, 2)),
         ],
     )(*parts, names, up)
@@ -512,24 +502,25 @@
     halves, refs = refs[:more], refs[more:]
     out_hbm, back_ref, base_ref, half_ref, out_ref, pick_ref, in_sems, more_sems, out_sems = refs
     rows, cols = out_ref.shape
-    loads = [[start(pick_hbm, pick_ref, in_sems.at[0, 0])], []]
-    for side in range(2):
-        these = side_of(side, cols)
+    loads = [[] for _ in range(SIDES)]
+    loads[0].append(start(pick_hbm, pick_ref, in_sems.at[0, 0]))
+    for side in range(SIDES):
+        these = pl.ds(side * (cols // SIDES), cols // SIDES)
         loads[side].append(start(back_hbm.at[:, these], back_ref.at[:, these], in_sems.at[side, 1]))
         loads[side].append(start(base_hbm.at[:, these], base_ref.at[:, these], in_sems.at[side, 2]))
         for i, x in enumerate(halves):
             loads[side].append(start(x.at[:, these], half_ref.at[i, :, these], more_sems.at[side, i]))
     stores = []
-    for side in range(2):
+    for side in range(SIDES):
         wait(loads[side])
-        for n in range(side * (cols // 2), (side + 1) * (cols // 2), PIECE):
+        for n in range(side * (cols // SIDES), (side + 1) * (cols // SIDES), PIECE):
             these = slice(n, n + PIECE)
             base = base_ref[:, these].astype(F32)
             if more:
                 base = base + half_ref[:, :, these].reshape(base.shape).astype(F32)
-            delta = dots(pick_ref[...], back_ref, these).astype(BF16).astype(F32)
+            delta = dots(pick_ref[...], back_ref, these)
             out_ref[:, these] = (base + delta).astype(BF16)
-        these = side_of(side, cols)
+        these = pl.ds(side * (cols // SIDES), cols // SIDES)
         stores.append(start(out_ref.at[:, these], out_hbm.at[:, these], out_sems.at[side]))
     wait(stores)
 
@@ -547,9 +538,9 @@
             pltpu.VMEM((2, rows // 2, cols), BF16),
             pltpu.VMEM((rows, cols), BF16),
             pltpu.VMEM((rows, SENT), BF16),
-            pltpu.SemaphoreType.DMA((2, 3)),
-            pltpu.SemaphoreType.DMA((2, 2)),
-            pltpu.SemaphoreType.DMA((2,)),
+            pltpu.SemaphoreType.DMA((SIDES, 3)),
+            pltpu.SemaphoreType.DMA((SIDES, 2)),
+            pltpu.SemaphoreType.DMA((SIDES,)),
         ],
     )(pick, back, base, *halves)
 
@@ -572,9 +563,7 @@
     lens = lengths.reshape(1, lengths.shape[0])
     down = jnp.transpose(adapter_a, (0, 2, 1)).reshape(ADP * RANK, adapter_a.shape[1])
     up = adapter_b.reshape(ADP * RANK, adapter_b.shape[2])
-    attended, outgoing, far = attend(
-        query, new_key, new_value, cache_keys, cache_values, out_weight, lens, ids, cols
-    )
+    attended, outgoing = attend(query, new_key, new_value, cache_keys, cache_values, lens, ids)
 
     def exchange(x):
         x = x.reshape(GROUPS, SLOTS, x.shape[1])
@@ -590,23 +579,25 @@
     arrived = exchange(outgoing)
 
     tie = lax.optimization_barrier
+    (far,) = theirs(attended, out_weight, (2,), cols)
     far = send(far, swap)
-    near = [send(x, swap) for x in theirs(attended, out_weight, (1, 3), cols)]
+    *near, home = [send(x, swap) for x in theirs(attended, out_weight, (1, 3, 0), cols)]
     far_top, far_bot = mine(attended, out_weight, (far,), (2,), cols, (2,))
     from_left, from_right = send(far_top, right), send(far_bot, left)
     right_top, right_bot, left_top, left_bot = mine(attended, out_weight, near, (1, 3), cols, (2, 2))
+    arrived, right_top, left_bot, right_bot, left_top = tie((arrived, right_top, left_bot, right_bot, left_top))
+    pair, names = pair_rank(arrived)
+    pair, right_top, left_bot, from_left, from_right = tie((pair, right_top, left_bot, from_left, from_right))
+    own_part, *others, last = all_ranks(pair)
+    last, right_bot, left_top = tie((last, right_bot, left_top))
     l_bot, r_top = send(right_bot, right), send(left_top, left)
-    arrived, right_top, left_bot = tie((arrived, right_top, left_bot))
-    pair, names = pair_rank(arrived)
-    pair, right_top, left_bot, from_left, from_right, l_bot, r_top = tie(
-        (pair, right_top, left_bot, from_left, from_right, l_bot, r_top)
+    parts, (right_top, left_bot) = tie(
+        ((own_part, *others, last), merge(right_top, from_left, left_bot, from_right))
     )
-    parts, (right_top, left_bot) = tie((all_ranks(pair), merge(right_top, from_left, left_bot, from_right)))
     delta, attended, ids = tie((deltas(parts, names, up), attended, ids))
     back = exchange(delta)
     l_top, r_bot = send(right_top, right), send(left_bot, left)
-    (home,) = theirs(attended, out_weight, (0,), cols)
-    (own,) = mine(attended, out_weight, (send(home, swap),), (0,), cols, (1,), halves=(r_top, l_bot))
+    (own,) = mine(attended, out_weight, (home,), (0,), cols, (1,), halves=(r_top, l_bot))
     pick = picks(jnp.zeros((1,), jnp.int32), ids)
     out = finish(pick, back, own, halves=(l_top, r_bot))
 

time: 107 us -> 105 us (0.981)
  starting transfers between devices: 30.9 us -> 27.2 us
  waiting for transfers between devices: 19.7 us -> 22.3 us
    ppermute x14, waiting for transfers between devices: 9.17 us -> 18.6 us  [per_device(): send = lambda x, perm: lax.ppermute(x, 'tensor', perm)]
    all_to_all x2, waiting for transfers between devices: 10.5 us -> 3.68 us  [exchange(): lax.all_to_all(x, 'dp', split_axis=0, concat_axis=0, tiled=True)]
    all_to_all x2, starting transfers between devices: 15.3 us -> 12.6 us  [exchange(): lax.all_to_all(x, 'dp', split_axis=0, concat_axis=0, tiled=True)]
    pallas_call x2, Pallas kernels: 9.1 us -> 10.6 us  [theirs(): call(functools.partial(theirs_kernel, offsets=offsets), 'theirs', [HBM] *...]
    pallas_call x1, Pallas kernels: 8.97 us -> 7.5 us  [attend(): call(attend_kernel, 'attend', [HBM] * 5 + [VMEM] * 2, [shape(rows, width)...]
  transfers between devices with their start and end apart: 16 -> 16, of which waited for: 8 -> 7; matrix products, arithmetic and copies ran while one was open for 3% -> 3% of each run, Pallas kernels for 32% -> 33%
where the time goes in v4:
time: 105 us
  Pallas kernels  51.2 us (49%)
  starting transfers between devices  27.2 us (26%)
  waiting for transfers between devices  22.3 us (21%)
  other arithmetic  2.96 us (3%)
    ppermute x14, waiting for transfers between devices, per_device(): send = lambda x, perm: lax.ppermute(x, 'tensor', perm)  18.6 us
    ppermute x14, starting transfers between devices, per_device(): send = lambda x, perm: lax.ppermute(x, 'tensor', perm)  14.6 us
    pallas_call x3, Pallas kernels, mine(): call(functools.partial(mine_kernel, offsets=offsets, parts=parts, more=le...  14.5 us
    all_to_all x2, starting transfers between devices, exchange(): lax.all_to_all(x, 'dp', split_axis=0, concat_axis=0, tiled=True)  12.6 us
    pallas_call x2, Pallas kernels, theirs(): call(functools.partial(theirs_kernel, offsets=offsets), 'theirs', [HBM] *...  10.6 us
    pallas_call x1, Pallas kernels, attend(): call(attend_kernel, 'attend', [HBM] * 5 + [VMEM] * 2, [shape(rows, width)...  7.5 us
    pallas_call x1, Pallas kernels, rank_parts(): call(rank_kernel, 'rank_parts', [HBM] * 2, [shape(HALF, 128), shape(SENT,...  5.21 us
    pallas_call x1, Pallas kernels, deltas(): call(delta_kernel, 'deltas', [HBM] * 6, shape(SENT, cols), [pltpu.VMEM((4...  4.76 us
  transfers between devices with their start and end apart: 16, of which 7 were waited for; matrix products, arithmetic and copies ran while one was open for 3% of the time, Pallas kernels for 33%

profile of v4, /device:TPU:0, one launch (start us, length us, event | category | flops | bytes accessed | tf_op | source)
XLA Modules:
  0.0 104.7 jit_solution(5950347451046973673)
XLA Ops:
  0.0 7.5 %attend.1 = (bf16[512,1024]{1,0:T(8,128)(2,1)}, bf16[896,1024]{1,0:T(8,128)(2,1)}) custom-call(bf16[512,1024]{1,0:T(8,128)(2,1)} %q_hbm.1, bf16[512,128]{1,0:T(8,128)(2,1)} %nk_hbm.1, bf16[512,128]{1,0:T(8,128)(2,1)} %nv_hbm.1, bf16[512,16,128]{2,1,0:T(8,128)(2,1)} %k_hbm.1, bf16[512,16,128]{2,1,0:T(8,128)(2,1)} %v_hbm.1, s32[1,512]{1,0:T(1,128)} %bitcast.38, ...), custom_call_target="tpu_custom_call" | custom-call | flops 1024 | bytes 1024 | tf_op jit(solution)/shard_map/attend/pallas_call | solution.py:185
  7.5 8.2 %all-to-all-start.2 = ((bf16[16,56,1024]{2,1,0:T(8,128)(2,1)}), bf16[16,56,1024]{2,1,0:T(8,128)(2,1)}, u32[]{:S(2)}, u32[]{:S(2)}) async-start(bf16[16,56,1024]{2,1,0:T(8,128)(2,1)} %bitcast.34), calls=%async_computation.2 | async-start | bytes 3670016 | tf_op jit(solution)/shard_map/all_to_all | solution.py:570
  15.7 3.9 %theirs.3 = bf16[512,1024]{1,0:T(8,128)(2,1)} custom-call(bf16[512,1024]{1,0:T(8,128)(2,1)} %get-tuple-element.186.att_hbm, bf16[1024,8192]{1,0:T(8,128)(2,1)} %w_hbm.9), custom_call_target="tpu_custom_call" | custom-call | flops 1024 | bytes 1024 | tf_op jit(solution)/shard_map/theirs/pallas_call | solution.py:381
  19.6 0.1 collective-permute-start.7
  19.7 6.7 %theirs.2 = (bf16[512,1024]{1,0:T(8,128)(2,1)}, bf16[512,1024]{1,0:T(8,128)(2,1)}, bf16[512,1024]{1,0:T(8,128)(2,1)}) custom-call(bf16[512,1024]{1,0:T(8,128)(2,1)} %get-tuple-element.186.att_hbm, bf16[1024,8192]{1,0:T(8,128)(2,1)} %w_hbm.9), custom_call_target="tpu_custom_call" | custom-call | flops 1024 | bytes 1024 | tf_op jit(solution)/shard_map/theirs/pallas_call | solution.py:381
  26.4 0.6 collective-permute-start.4
  27.0 0.1 collective-permute-start.5
  27.1 0.0 collective-permute-done.7.refs_0_
  27.1 4.0 %mine.4 = (bf16[256,1024]{1,0:T(8,128)(2,1)}, bf16[256,1024]{1,0:T(8,128)(2,1)}) custom-call(bf16[512,1024]{1,0:T(8,128)(2,1)} %get-tuple-element.186.att_hbm, bf16[1024,8192]{1,0:T(8,128)(2,1)} %w_hbm.9, bf16[512,1024]{1,0:T(8,128)(2,1)} %collective-permute-done.7.refs_0_), custom_call_target="tpu_custom_call" | custom-call | flops 1024 | bytes 1024 | tf_op jit(solution)/shard_map/mine/pallas_call | solution.py:437
  31.1 1.6 %collective-permute-start.8 = (bf16[256,1024]{1,0:T(8,128)(2,1)}, bf16[256,1024]{1,0:T(8,128)(2,1)}, u32[]{:S(2)}, u32[]{:S(2)}) collective-permute-start(bf16[256,1024]{1,0:T(8,128)(2,1)} %get-tuple-element.94), channel_id=1, source_target_pairs={{0,2},{1,3},{2,4},{3,5},{4,6},{5,7},{6,0},{7,1},{8,10},{9,11},{10,... | collective-permute-start | bytes 1572872 | tf_op jit(solution)/shard_map/ppermute | solution.py:560
  32.7 1.7 %collective-permute-start.9 = (bf16[256,1024]{1,0:T(8,128)(2,1)}, bf16[256,1024]{1,0:T(8,128)(2,1)}, u32[]{:S(2)}, u32[]{:S(2)}) collective-permute-start(bf16[256,1024]{1,0:T(8,128)(2,1)} %get-tuple-element.95), channel_id=1, source_target_pairs={{0,6},{1,7},{2,0},{3,1},{4,2},{5,3},{6,4},{7,5},{8,14},{9,15},{10,... | collective-permute-start | bytes 1572872 | tf_op jit(solution)/shard_map/ppermute | solution.py:560
  34.4 0.0 collective-permute-done.4.refs_0_
  34.4 0.0 collective-permute-done.5.refs_1_
  34.4 5.6 %mine.3 = (bf16[256,1024]{1,0:T(8,128)(2,1)}, bf16[256,1024]{1,0:T(8,128)(2,1)}, bf16[256,1024]{1,0:T(8,128)(2,1)}, bf16[256,1024]{1,0:T(8,128)(2,1)}) custom-call(bf16[512,1024]{1,0:T(8,128)(2,1)} %get-tuple-element.186.att_hbm, bf16[1024,8192]{1,0:T(8,128)(2,1)} %w_hbm.9, bf16[512,1024]{1,0:T(8,128)(2,1)} %collective-permute-done.4.refs_0_, ...), custom_call_target="tpu_custom_call" | custom-call | flops 1024 | bytes 1024 | tf_op jit(solution)/shard_map/mine/pallas_call | solution.py:437
  40.0 3.7 %all-to-all-done.2 = bf16[16,56,1024]{2,1,0:T(8,128)(2,1)} async-done(((bf16[16,56,1024]{2,1,0:T(8,128)(2,1)}), bf16[16,56,1024]{2,1,0:T(8,128)(2,1)}, u32[]{:S(2)}, u32[]{:S(2)}) %all-to-all-start.2) | async-done | bytes 1835040 | tf_op jit(solution)/shard_map/all_to_all | solution.py:570
  43.7 5.2 %rank_parts.2 = (bf16[448,128]{1,0:T(8,128)(2,1)}, s32[896,128]{1,0:T(8,128)}) custom-call(bf16[896,1024]{1,0:T(8,128)(2,1)} %bitcast.8.x_hbm, bf16[1024,1024]{1,0:T(8,128)(2,1)} %bitcast.31), custom_call_target="tpu_custom_call" | custom-call | flops 1024 | bytes 1024 | tf_op jit(solution)/shard_map/rank_parts/pallas_call | solution.py:273
  48.9 0.1 collective-permute-start.6
  49.0 1.5 %collective-permute-done.6 = bf16[448,128]{1,0:T(8,128)(2,1)S(1)} collective-permute-done((bf16[448,128]{1,0:T(8,128)(2,1)}, bf16[448,128]{1,0:T(8,128)(2,1)S(1)}, u32[]{:S(2)}, u32[]{:S(2)}) %collective-permute-start.6) | collective-permute-done | bytes 114720 | tf_op jit(solution)/shard_map/ppermute | solution.py:560
  50.5 1.6 %add_convert_fusion.1.p0_hbm = bf16[448,128]{1,0:T(8,128)(2,1)} fusion(bf16[448,128]{1,0:T(8,128)(2,1)S(1)} %collective-permute-done.6, bf16[448,128]{1,0:T(8,128)(2,1)} %get-tuple-element.91), kind=kLoop, calls=%fused_computation.1 | loop fusion | flops 229376 | bytes 344064 | tf_op jit(solution)/shard_map/convert_element_type | solution.py:549
  52.1 0.0 collective-permute-done.8.b_hbm
  52.1 0.0 collective-permute-done.9.d_hbm
  52.1 3.0 %collective-permute-start.12 = (bf16[448,128]{1,0:T(8,128)(2,1)}, bf16[448,128]{1,0:T(8,128)(2,1)}, u32[]{:S(2)}, u32[]{:S(2)}) collective-permute-start(bf16[448,128]{1,0:T(8,128)(2,1)} %add_convert_fusion.1.p0_hbm), channel_id=1, source_target_pairs={{0,4},{1,5},{2,6},{3,7},{4,0},{5,1},{6,2},{7,3},{8,12},{9,13},{10,... | collective-permute-start | bytes 344072 | tf_op jit(solution)/shard_map/ppermute | solution.py:560
  55.1 1.1 %collective-permute-start.11 = (bf16[448,128]{1,0:T(8,128)(2,1)}, bf16[448,128]{1,0:T(8,128)(2,1)}, u32[]{:S(2)}, u32[]{:S(2)}) collective-permute-start(bf16[448,128]{1,0:T(8,128)(2,1)} %add_convert_fusion.1.p0_hbm), channel_id=1, source_target_pairs={{0,6},{1,7},{2,0},{3,1},{4,2},{5,3},{6,4},{7,5},{8,14},{9,15},{10,... | collective-permute-start | bytes 344072 | tf_op jit(solution)/shard_map/ppermute | solution.py:560
  56.2 0.9 collective-permute-start.10
  57.1 2.5 %merge.1 = (bf16[256,1024]{1,0:T(8,128)(2,1)}, bf16[256,1024]{1,0:T(8,128)(2,1)}) custom-call(bf16[256,1024]{1,0:T(8,128)(2,1)} %get-tuple-element.100.a_hbm, bf16[256,1024]{1,0:T(8,128)(2,1)} %collective-permute-done.8.b_hbm, bf16[256,1024]{1,0:T(8,128)(2,1)} %get-tuple-element.102.c_hbm, bf16[256,1024]{1,0:T(8,128)(2,1)} %collective-permute-done.9.d_hbm), custom_call_target="tpu_custom_call" | custom-call | flops 1024 | bytes 1024 | tf_op jit(solution)/shard_map/merge/pallas_call | solution.py:467
  59.6 0.0 collective-permute-done.12.p3_hbm
  59.7 2.0 %collective-permute-done.11.p2_hbm = bf16[448,128]{1,0:T(8,128)(2,1)} collective-permute-done((bf16[448,128]{1,0:T(8,128)(2,1)}, bf16[448,128]{1,0:T(8,128)(2,1)}, u32[]{:S(2)}, u32[]{:S(2)}) %collective-permute-start.11) | collective-permute-done | bytes 114720 | tf_op jit(solution)/shard_map/ppermute | solution.py:560
  61.7 0.9 collective-permute-done.10.p1_hbm
  62.6 4.8 %deltas.2 = bf16[896,1024]{1,0:T(8,128)(2,1)} custom-call(bf16[448,128]{1,0:T(8,128)(2,1)} %add_convert_fusion.1.p0_hbm, bf16[448,128]{1,0:T(8,128)(2,1)} %collective-permute-done.10.p1_hbm, bf16[448,128]{1,0:T(8,128)(2,1)} %collective-permute-done.11.p2_hbm, bf16[448,128]{1,0:T(8,128)(2,1)} %collective-permute-done.12.p3_hbm, ...), custom_call_target="tpu_custom_call" | custom-call | flops 1024 | bytes 1024 | tf_op jit(solution)/shard_map/deltas/pallas_call | solution.py:326
  67.3 4.4 %all-to-all-start.3 = ((bf16[16,56,1024]{2,1,0:T(8,128)(2,1)}), bf16[16,56,1024]{2,1,0:T(8,128)(2,1)}, u32[]{:S(2)}, u32[]{:S(2)}) async-start(bf16[16,56,1024]{2,1,0:T(8,128)(2,1)} %bitcast.33), calls=%async_computation.3 | async-start | bytes 3670016 | tf_op jit(solution)/shard_map/all_to_all | solution.py:570
  71.8 0.1 collective-permute-start.13
  71.9 1.8 %collective-permute-start.14 = (bf16[256,1024]{1,0:T(8,128)(2,1)}, bf16[256,1024]{1,0:T(8,128)(2,1)}, u32[]{:S(2)}, u32[]{:S(2)}) collective-permute-start(bf16[256,1024]{1,0:T(8,128)(2,1)} %get-tuple-element.115), channel_id=1, source_target_pairs={{0,6},{1,7},{2,0},{3,1},{4,2},{5,3},{6,4},{7,5},{8,14},{9,15},{10,... | collective-permute-start | bytes 1572872 | tf_op jit(solution)/shard_map/ppermute | solution.py:560
  73.7 0.3 collective-permute-start.15
  74.0 0.5 collective-permute-start.16
  74.5 2.7 %collective-permute-start.17 = (bf16[256,1024]{1,0:T(8,128)(2,1)}, bf16[256,1024]{1,0:T(8,128)(2,1)}, u32[]{:S(2)}, u32[]{:S(2)}) collective-permute-start(bf16[256,1024]{1,0:T(8,128)(2,1)} %get-tuple-element.118), channel_id=1, source_target_pairs={{0,6},{1,7},{2,0},{3,1},{4,2},{5,3},{6,4},{7,5},{8,14},{9,15},{10,... | collective-permute-start | bytes 1572872 | tf_op jit(solution)/shard_map/ppermute | solution.py:560
  77.2 1.4 %slice_reduce_fusion = bf16[]{:T(256)} fusion(bf16[16,56,1024]{2,1,0:T(8,128)(2,1)} %bitcast.14), kind=kLoop, calls=%fused_computation.2 | loop fusion | flops 15 | bytes 34 | tf_op jit(solution)/shard_map/reduce_max | solution.py:604
  79.2 2.1 %picks.2.pick_hbm = bf16[512,896]{1,0:T(8,128)(2,1)} custom-call(s32[1]{0:T(128)} %constant.3.clone.1.turn_ref, s32[1,512]{1,0:T(1,128)} %bitcast.36), custom_call_target="tpu_custom_call" | custom-call | flops 1024 | bytes 1024 | tf_op jit(solution)/shard_map/picks/pallas_call | solution.py:492
  81.4 0.0 collective-permute-done.13.refs_0_
  81.4 5.6 %collective-permute-done.14.refs_1_ = bf16[256,1024]{1,0:T(8,128)(2,1)} collective-permute-done((bf16[256,1024]{1,0:T(8,128)(2,1)}, bf16[256,1024]{1,0:T(8,128)(2,1)}, u32[]{:S(2)}, u32[]{:S(2)}) %collective-permute-start.14) | collective-permute-done | bytes 524320 | tf_op jit(solution)/shard_map/ppermute | solution.py:560
  87.0 3.0 %collective-permute-done.15.refs_2_ = bf16[256,1024]{1,0:T(8,128)(2,1)} collective-permute-done((bf16[256,1024]{1,0:T(8,128)(2,1)}, bf16[256,1024]{1,0:T(8,128)(2,1)}, u32[]{:S(2)}, u32[]{:S(2)}) %collective-permute-start.15) | collective-permute-done | bytes 524320 | tf_op jit(solution)/shard_map/ppermute | solution.py:560
  90.0 4.9 %mine.5.base_hbm = bf16[512,1024]{1,0:T(8,128)(2,1)} custom-call(bf16[512,1024]{1,0:T(8,128)(2,1)} %get-tuple-element.186.att_hbm, bf16[1024,8192]{1,0:T(8,128)(2,1)} %w_hbm.9, bf16[512,1024]{1,0:T(8,128)(2,1)} %collective-permute-done.13.refs_0_, bf16[256,1024]{1,0:T(8,128)(2,1)} %collective-permute-done.14.refs_1_, ...), custom_call_target="tpu_custom_call" | custom-call | flops 1024 | bytes 1024 | tf_op jit(solution)/shard_map/mine/pallas_call | solution.py:437
  94.9 5.6 %collective-permute-done.16.refs_0_ = bf16[256,1024]{1,0:T(8,128)(2,1)} collective-permute-done((bf16[256,1024]{1,0:T(8,128)(2,1)}, bf16[256,1024]{1,0:T(8,128)(2,1)}, u32[]{:S(2)}, u32[]{:S(2)}) %collective-permute-start.16) | collective-permute-done | bytes 524320 | tf_op jit(solution)/shard_map/ppermute | solution.py:560
  100.5 0.0 collective-permute-done.17.refs_1_
  100.5 0.0 all-to-all-done.3
  100.5 4.1 %finish.2 = bf16[512,1024]{1,0:T(8,128)(2,1)} custom-call(bf16[512,896]{1,0:T(8,128)(2,1)} %picks.2.pick_hbm, bf16[896,1024]{1,0:T(8,128)(2,1)} %bitcast.13.back_hbm, bf16[512,1024]{1,0:T(8,128)(2,1)} %mine.5.base_hbm, bf16[256,1024]{1,0:T(8,128)(2,1)} %collective-permute-done.16.refs_0_, bf16[256,1024]{1,0:T(8,128)(2,1)} %collective-permute-done.17.refs_1_), custom_call_target="tpu_custom_call" | custom-call | flops 1024 | bytes 1024 | tf_op jit(solution)/shard_map/finish/pallas_call | solution.py:530
  (1 shorter events, 0.0 us)
Async XLA Ops:
  7.5 36.2 %all-to-all-start.2 = ((bf16[16,56,1024]{2,1,0:T(8,128)(2,1)}), bf16[16,56,1024]{2,1,0:T(8,128)(2,1)}, u32[]{:S(2)}, u32[]{:S(2)}) async-start(bf16[16,56,1024]{2,1,0:T(8,128)(2,1)} %bitcast.34), calls=%async_computation.2 | async-start | bytes 3670016 | tf_op jit(solution)/shard_map/all_to_all | solution.py:570
  19.6 7.5 %collective-permute-start.7 = (bf16[512,1024]{1,0:T(8,128)(2,1)}, bf16[512,1024]{1,0:T(8,128)(2,1)}, u32[]{:S(2)}, u32[]{:S(2)}) collective-permute-start(bf16[512,1024]{1,0:T(8,128)(2,1)} %theirs.3), channel_id=1, source_target_pairs={{0,1},{1,0},{2,3},{3,2},{4,5},{5,4},{6,7},{7,6},{8,9},{9,8},{10,11... | collective-permute-start | bytes 3145736 | tf_op jit(solution)/shard_map/ppermute | solution.py:560
  26.4 8.0 %collective-permute-start.4 = (bf16[512,1024]{1,0:T(8,128)(2,1)}, bf16[512,1024]{1,0:T(8,128)(2,1)}, u32[]{:S(2)}, u32[]{:S(2)}) collective-permute-start(bf16[512,1024]{1,0:T(8,128)(2,1)} %get-tuple-element.84), channel_id=1, source_target_pairs={{0,1},{1,0},{2,3},{3,2},{4,5},{5,4},{6,7},{7,6},{8,9},{9,8},{10,11... | collective-permute-start | bytes 3145736 | tf_op jit(solution)/shard_map/ppermute | solution.py:560
  27.0 7.4 %collective-permute-start.5 = (bf16[512,1024]{1,0:T(8,128)(2,1)}, bf16[512,1024]{1,0:T(8,128)(2,1)}, u32[]{:S(2)}, u32[]{:S(2)}) collective-permute-start(bf16[512,1024]{1,0:T(8,128)(2,1)} %get-tuple-element.85), channel_id=1, source_target_pairs={{0,1},{1,0},{2,3},{3,2},{4,5},{5,4},{6,7},{7,6},{8,9},{9,8},{10,11... | collective-permute-start | bytes 3145736 | tf_op jit(solution)/shard_map/ppermute | solution.py:560
  31.1 21.0 %collective-permute-start.8 = (bf16[256,1024]{1,0:T(8,128)(2,1)}, bf16[256,1024]{1,0:T(8,128)(2,1)}, u32[]{:S(2)}, u32[]{:S(2)}) collective-permute-start(bf16[256,1024]{1,0:T(8,128)(2,1)} %get-tuple-element.94), channel_id=1, source_target_pairs={{0,2},{1,3},{2,4},{3,5},{4,6},{5,7},{6,0},{7,1},{8,10},{9,11},{10,... | collective-permute-start | bytes 1572872 | tf_op jit(solution)/shard_map/ppermute | solution.py:560
  32.7 19.4 %collective-permute-start.9 = (bf16[256,1024]{1,0:T(8,128)(2,1)}, bf16[256,1024]{1,0:T(8,128)(2,1)}, u32[]{:S(2)}, u32[]{:S(2)}) collective-permute-start(bf16[256,1024]{1,0:T(8,128)(2,1)} %get-tuple-element.95), channel_id=1, source_target_pairs={{0,6},{1,7},{2,0},{3,1},{4,2},{5,3},{6,4},{7,5},{8,14},{9,15},{10,... | collective-permute-start | bytes 1572872 | tf_op jit(solution)/shard_map/ppermute | solution.py:560
  48.9 1.6 %collective-permute-start.6 = (bf16[448,128]{1,0:T(8,128)(2,1)}, bf16[448,128]{1,0:T(8,128)(2,1)S(1)}, u32[]{:S(2)}, u32[]{:S(2)}) collective-permute-start(bf16[448,128]{1,0:T(8,128)(2,1)} %get-tuple-element.91), channel_id=1, source_target_pairs={{0,1},{1,0},{2,3},{3,2},{4,5},{5,4},{6,7},{7,6},{8,9},{9,8},{10,11... | collective-permute-start | bytes 344072 | tf_op jit(solution)/shard_map/ppermute | solution.py:560
  52.1 7.6 %collective-permute-start.12 = (bf16[448,128]{1,0:T(8,128)(2,1)}, bf16[448,128]{1,0:T(8,128)(2,1)}, u32[]{:S(2)}, u32[]{:S(2)}) collective-permute-start(bf16[448,128]{1,0:T(8,128)(2,1)} %add_convert_fusion.1.p0_hbm), channel_id=1, source_target_pairs={{0,4},{1,5},{2,6},{3,7},{4,0},{5,1},{6,2},{7,3},{8,12},{9,13},{10,... | collective-permute-start | bytes 344072 | tf_op jit(solution)/shard_map/ppermute | solution.py:560
  55.1 6.5 %collective-permute-start.11 = (bf16[448,128]{1,0:T(8,128)(2,1)}, bf16[448,128]{1,0:T(8,128)(2,1)}, u32[]{:S(2)}, u32[]{:S(2)}) collective-permute-start(bf16[448,128]{1,0:T(8,128)(2,1)} %add_convert_fusion.1.p0_hbm), channel_id=1, source_target_pairs={{0,6},{1,7},{2,0},{3,1},{4,2},{5,3},{6,4},{7,5},{8,14},{9,15},{10,... | collective-permute-start | bytes 344072 | tf_op jit(solution)/shard_map/ppermute | solution.py:560
  56.2 6.3 %collective-permute-start.10 = (bf16[448,128]{1,0:T(8,128)(2,1)}, bf16[448,128]{1,0:T(8,128)(2,1)}, u32[]{:S(2)}, u32[]{:S(2)}) collective-permute-start(bf16[448,128]{1,0:T(8,128)(2,1)} %add_convert_fusion.1.p0_hbm), channel_id=1, source_target_pairs={{0,2},{1,3},{2,4},{3,5},{4,6},{5,7},{6,0},{7,1},{8,10},{9,11},{10,... | collective-permute-start | bytes 344072 | tf_op jit(solution)/shard_map/ppermute | solution.py:560
  67.3 33.1 %all-to-all-start.3 = ((bf16[16,56,1024]{2,1,0:T(8,128)(2,1)}), bf16[16,56,1024]{2,1,0:T(8,128)(2,1)}, u32[]{:S(2)}, u32[]{:S(2)}) async-start(bf16[16,56,1024]{2,1,0:T(8,128)(2,1)} %bitcast.33), calls=%async_computation.3 | async-start | bytes 3670016 | tf_op jit(solution)/shard_map/all_to_all | solution.py:570
  71.8 9.6 %collective-permute-start.13 = (bf16[512,1024]{1,0:T(8,128)(2,1)}, bf16[512,1024]{1,0:T(8,128)(2,1)}, u32[]{:S(2)}, u32[]{:S(2)}) collective-permute-start(bf16[512,1024]{1,0:T(8,128)(2,1)} %get-tuple-element.114), channel_id=1, source_target_pairs={{0,1},{1,0},{2,3},{3,2},{4,5},{5,4},{6,7},{7,6},{8,9},{9,8},{10,11... | collective-permute-start | bytes 3145736 | tf_op jit(solution)/shard_map/ppermute | solution.py:560
  71.9 15.1 %collective-permute-start.14 = (bf16[256,1024]{1,0:T(8,128)(2,1)}, bf16[256,1024]{1,0:T(8,128)(2,1)}, u32[]{:S(2)}, u32[]{:S(2)}) collective-permute-start(bf16[256,1024]{1,0:T(8,128)(2,1)} %get-tuple-element.115), channel_id=1, source_target_pairs={{0,6},{1,7},{2,0},{3,1},{4,2},{5,3},{6,4},{7,5},{8,14},{9,15},{10,... | collective-permute-start | bytes 1572872 | tf_op jit(solution)/shard_map/ppermute | solution.py:560
  73.7 16.3 %collective-permute-start.15 = (bf16[256,1024]{1,0:T(8,128)(2,1)}, bf16[256,1024]{1,0:T(8,128)(2,1)}, u32[]{:S(2)}, u32[]{:S(2)}) collective-permute-start(bf16[256,1024]{1,0:T(8,128)(2,1)} %get-tuple-element.116), channel_id=1, source_target_pairs={{0,2},{1,3},{2,4},{3,5},{4,6},{5,7},{6,0},{7,1},{8,10},{9,11},{10,... | collective-permute-start | bytes 1572872 | tf_op jit(solution)/shard_map/ppermute | solution.py:560
  74.0 26.5 %collective-permute-start.16 = (bf16[256,1024]{1,0:T(8,128)(2,1)}, bf16[256,1024]{1,0:T(8,128)(2,1)}, u32[]{:S(2)}, u32[]{:S(2)}) collective-permute-start(bf16[256,1024]{1,0:T(8,128)(2,1)} %get-tuple-element.117), channel_id=1, source_target_pairs={{0,2},{1,3},{2,4},{3,5},{4,6},{5,7},{6,0},{7,1},{8,10},{9,11},{10,... | collective-permute-start | bytes 1572872 | tf_op jit(solution)/shard_map/ppermute | solution.py:560
  74.5 26.0 %collective-permute-start.17 = (bf16[256,1024]{1,0:T(8,128)(2,1)}, bf16[256,1024]{1,0:T(8,128)(2,1)}, u32[]{:S(2)}, u32[]{:S(2)}) collective-permute-start(bf16[256,1024]{1,0:T(8,128)(2,1)} %get-tuple-element.118), channel_id=1, source_target_pairs={{0,6},{1,7},{2,0},{3,1},{4,2},{5,3},{6,4},{7,5},{8,14},{9,15},{10,... | collective-permute-start | bytes 1572872 | tf_op jit(solution)/shard_map/ppermute | solution.py:560

commit v5 on v4

--- a/solution.py
+++ b/solution.py
@@ -19,7 +19,7 @@
 SUB = 16
 WIDE = SUB * SUB
 PACK = 448
-PIECE = 256
+PIECE = 512
 BLOCK = 256
 STEP = 512
 F32 = jnp.float32

time: 105 us -> 105 us (level)
  no operation moved by 1% of the time
where the time goes in v5:
time: 105 us
  Pallas kernels  50.6 us (48%)
  starting transfers between devices  27.2 us (26%)
  waiting for transfers between devices  23 us (22%)
  other arithmetic  2.96 us (3%)
    ppermute x14, waiting for transfers between devices, per_device(): send = lambda x, perm: lax.ppermute(x, 'tensor', perm)  19.3 us
    ppermute x14, starting transfers between devices, per_device(): send = lambda x, perm: lax.ppermute(x, 'tensor', perm)  14.6 us
    pallas_call x3, Pallas kernels, mine(): call(functools.partial(mine_kernel, offsets=offsets, parts=parts, more=le...  13.8 us
    all_to_all x2, starting transfers between devices, exchange(): lax.all_to_all(x, 'dp', split_axis=0, concat_axis=0, tiled=True)  12.6 us
    pallas_call x2, Pallas kernels, theirs(): call(functools.partial(theirs_kernel, offsets=offsets), 'theirs', [HBM] *...  10.6 us
    pallas_call x1, Pallas kernels, attend(): call(attend_kernel, 'attend', [HBM] * 5 + [VMEM] * 2, [shape(rows, width)...  7.5 us
    pallas_call x1, Pallas kernels, rank_parts(): call(rank_kernel, 'rank_parts', [HBM] * 2, [shape(HALF, 128), shape(SENT,...  5.21 us
    pallas_call x1, Pallas kernels, deltas(): call(delta_kernel, 'deltas', [HBM] * 6, shape(SENT, cols), [pltpu.VMEM((4...  4.76 us
  transfers between devices with their start and end apart: 16, of which 7 were waited for; matrix products, arithmetic and copies ran while one was open for 3% of the time, Pallas kernels for 33%

profile of v5, /device:TPU:0, one launch (start us, length us, event | category | flops | bytes accessed | tf_op | source)
XLA Modules:
  0.0 104.7 jit_solution(4308449102753457553)
XLA Ops:
  0.0 7.5 %attend.1 = (bf16[512,1024]{1,0:T(8,128)(2,1)}, bf16[896,1024]{1,0:T(8,128)(2,1)}) custom-call(bf16[512,1024]{1,0:T(8,128)(2,1)} %q_hbm.1, bf16[512,128]{1,0:T(8,128)(2,1)} %nk_hbm.1, bf16[512,128]{1,0:T(8,128)(2,1)} %nv_hbm.1, bf16[512,16,128]{2,1,0:T(8,128)(2,1)} %k_hbm.1, bf16[512,16,128]{2,1,0:T(8,128)(2,1)} %v_hbm.1, s32[1,512]{1,0:T(1,128)} %bitcast.38, ...), custom_call_target="tpu_custom_call" | custom-call | flops 1024 | bytes 1024 | tf_op jit(solution)/shard_map/attend/pallas_call | solution.py:185
  7.5 8.2 %all-to-all-start.2 = ((bf16[16,56,1024]{2,1,0:T(8,128)(2,1)}), bf16[16,56,1024]{2,1,0:T(8,128)(2,1)}, u32[]{:S(2)}, u32[]{:S(2)}) async-start(bf16[16,56,1024]{2,1,0:T(8,128)(2,1)} %bitcast.34), calls=%async_computation.2 | async-start | bytes 3670016 | tf_op jit(solution)/shard_map/all_to_all | solution.py:570
  15.7 3.9 %theirs.3 = bf16[512,1024]{1,0:T(8,128)(2,1)} custom-call(bf16[512,1024]{1,0:T(8,128)(2,1)} %get-tuple-element.186.att_hbm, bf16[1024,8192]{1,0:T(8,128)(2,1)} %w_hbm.9), custom_call_target="tpu_custom_call" | custom-call | flops 1024 | bytes 1024 | tf_op jit(solution)/shard_map/theirs/pallas_call | solution.py:381
  19.6 0.1 collective-permute-start.7
  19.7 6.7 %theirs.2 = (bf16[512,1024]{1,0:T(8,128)(2,1)}, bf16[512,1024]{1,0:T(8,128)(2,1)}, bf16[512,1024]{1,0:T(8,128)(2,1)}) custom-call(bf16[512,1024]{1,0:T(8,128)(2,1)} %get-tuple-element.186.att_hbm, bf16[1024,8192]{1,0:T(8,128)(2,1)} %w_hbm.9), custom_call_target="tpu_custom_call" | custom-call | flops 1024 | bytes 1024 | tf_op jit(solution)/shard_map/theirs/pallas_call | solution.py:381
  26.4 0.6 collective-permute-start.4
  27.0 0.1 collective-permute-start.5
  27.1 0.0 collective-permute-done.7.refs_0_
  27.1 4.0 %mine.4 = (bf16[256,1024]{1,0:T(8,128)(2,1)}, bf16[256,1024]{1,0:T(8,128)(2,1)}) custom-call(bf16[512,1024]{1,0:T(8,128)(2,1)} %get-tuple-element.186.att_hbm, bf16[1024,8192]{1,0:T(8,128)(2,1)} %w_hbm.9, bf16[512,1024]{1,0:T(8,128)(2,1)} %collective-permute-done.7.refs_0_), custom_call_target="tpu_custom_call" | custom-call | flops 1024 | bytes 1024 | tf_op jit(solution)/shard_map/mine/pallas_call | solution.py:437
  31.1 1.6 %collective-permute-start.8 = (bf16[256,1024]{1,0:T(8,128)(2,1)}, bf16[256,1024]{1,0:T(8,128)(2,1)}, u32[]{:S(2)}, u32[]{:S(2)}) collective-permute-start(bf16[256,1024]{1,0:T(8,128)(2,1)} %get-tuple-element.94), channel_id=1, source_target_pairs={{0,2},{1,3},{2,4},{3,5},{4,6},{5,7},{6,0},{7,1},{8,10},{9,11},{10,... | collective-permute-start | bytes 1572872 | tf_op jit(solution)/shard_map/ppermute | solution.py:560
  32.7 1.7 %collective-permute-start.9 = (bf16[256,1024]{1,0:T(8,128)(2,1)}, bf16[256,1024]{1,0:T(8,128)(2,1)}, u32[]{:S(2)}, u32[]{:S(2)}) collective-permute-start(bf16[256,1024]{1,0:T(8,128)(2,1)} %get-tuple-element.95), channel_id=1, source_target_pairs={{0,6},{1,7},{2,0},{3,1},{4,2},{5,3},{6,4},{7,5},{8,14},{9,15},{10,... | collective-permute-start | bytes 1572872 | tf_op jit(solution)/shard_map/ppermute | solution.py:560
  34.4 0.0 collective-permute-done.4.refs_0_
  34.4 0.0 collective-permute-done.5.refs_1_
  34.4 5.6 %mine.3 = (bf16[256,1024]{1,0:T(8,128)(2,1)}, bf16[256,1024]{1,0:T(8,128)(2,1)}, bf16[256,1024]{1,0:T(8,128)(2,1)}, bf16[256,1024]{1,0:T(8,128)(2,1)}) custom-call(bf16[512,1024]{1,0:T(8,128)(2,1)} %get-tuple-element.186.att_hbm, bf16[1024,8192]{1,0:T(8,128)(2,1)} %w_hbm.9, bf16[512,1024]{1,0:T(8,128)(2,1)} %collective-permute-done.4.refs_0_, ...), custom_call_target="tpu_custom_call" | custom-call | flops 1024 | bytes 1024 | tf_op jit(solution)/shard_map/mine/pallas_call | solution.py:437
  40.0 3.7 %all-to-all-done.2 = bf16[16,56,1024]{2,1,0:T(8,128)(2,1)} async-done(((bf16[16,56,1024]{2,1,0:T(8,128)(2,1)}), bf16[16,56,1024]{2,1,0:T(8,128)(2,1)}, u32[]{:S(2)}, u32[]{:S(2)}) %all-to-all-start.2) | async-done | bytes 1835040 | tf_op jit(solution)/shard_map/all_to_all | solution.py:570
  43.7 5.2 %rank_parts.2 = (bf16[448,128]{1,0:T(8,128)(2,1)}, s32[896,128]{1,0:T(8,128)}) custom-call(bf16[896,1024]{1,0:T(8,128)(2,1)} %bitcast.8.x_hbm, bf16[1024,1024]{1,0:T(8,128)(2,1)} %bitcast.31), custom_call_target="tpu_custom_call" | custom-call | flops 1024 | bytes 1024 | tf_op jit(solution)/shard_map/rank_parts/pallas_call | solution.py:273
  48.9 0.1 collective-permute-start.6
  49.0 1.5 %collective-permute-done.6 = bf16[448,128]{1,0:T(8,128)(2,1)S(1)} collective-permute-done((bf16[448,128]{1,0:T(8,128)(2,1)}, bf16[448,128]{1,0:T(8,128)(2,1)S(1)}, u32[]{:S(2)}, u32[]{:S(2)}) %collective-permute-start.6) | collective-permute-done | bytes 114720 | tf_op jit(solution)/shard_map/ppermute | solution.py:560
  50.5 1.6 %add_convert_fusion.1.p0_hbm = bf16[448,128]{1,0:T(8,128)(2,1)} fusion(bf16[448,128]{1,0:T(8,128)(2,1)S(1)} %collective-permute-done.6, bf16[448,128]{1,0:T(8,128)(2,1)} %get-tuple-element.91), kind=kLoop, calls=%fused_computation.1 | loop fusion | flops 229376 | bytes 344064 | tf_op jit(solution)/shard_map/convert_element_type | solution.py:549
  52.1 0.0 collective-permute-done.8.b_hbm
  52.1 0.0 collective-permute-done.9.d_hbm
  52.1 3.0 %collective-permute-start.12 = (bf16[448,128]{1,0:T(8,128)(2,1)}, bf16[448,128]{1,0:T(8,128)(2,1)}, u32[]{:S(2)}, u32[]{:S(2)}) collective-permute-start(bf16[448,128]{1,0:T(8,128)(2,1)} %add_convert_fusion.1.p0_hbm), channel_id=1, source_target_pairs={{0,4},{1,5},{2,6},{3,7},{4,0},{5,1},{6,2},{7,3},{8,12},{9,13},{10,... | collective-permute-start | bytes 344072 | tf_op jit(solution)/shard_map/ppermute | solution.py:560
  55.1 1.1 %collective-permute-start.11 = (bf16[448,128]{1,0:T(8,128)(2,1)}, bf16[448,128]{1,0:T(8,128)(2,1)}, u32[]{:S(2)}, u32[]{:S(2)}) collective-permute-start(bf16[448,128]{1,0:T(8,128)(2,1)} %add_convert_fusion.1.p0_hbm), channel_id=1, source_target_pairs={{0,6},{1,7},{2,0},{3,1},{4,2},{5,3},{6,4},{7,5},{8,14},{9,15},{10,... | collective-permute-start | bytes 344072 | tf_op jit(solution)/shard_map/ppermute | solution.py:560
  56.2 0.9 collective-permute-start.10
  57.1 2.5 %merge.1 = (bf16[256,1024]{1,0:T(8,128)(2,1)}, bf16[256,1024]{1,0:T(8,128)(2,1)}) custom-call(bf16[256,1024]{1,0:T(8,128)(2,1)} %get-tuple-element.100.a_hbm, bf16[256,1024]{1,0:T(8,128)(2,1)} %collective-permute-done.8.b_hbm, bf16[256,1024]{1,0:T(8,128)(2,1)} %get-tuple-element.102.c_hbm, bf16[256,1024]{1,0:T(8,128)(2,1)} %collective-permute-done.9.d_hbm), custom_call_target="tpu_custom_call" | custom-call | flops 1024 | bytes 1024 | tf_op jit(solution)/shard_map/merge/pallas_call | solution.py:467
  59.6 0.0 collective-permute-done.12.p3_hbm
  59.7 2.0 %collective-permute-done.11.p2_hbm = bf16[448,128]{1,0:T(8,128)(2,1)} collective-permute-done((bf16[448,128]{1,0:T(8,128)(2,1)}, bf16[448,128]{1,0:T(8,128)(2,1)}, u32[]{:S(2)}, u32[]{:S(2)}) %collective-permute-start.11) | collective-permute-done | bytes 114720 | tf_op jit(solution)/shard_map/ppermute | solution.py:560
  61.7 0.9 collective-permute-done.10.p1_hbm
  62.6 4.8 %deltas.2 = bf16[896,1024]{1,0:T(8,128)(2,1)} custom-call(bf16[448,128]{1,0:T(8,128)(2,1)} %add_convert_fusion.1.p0_hbm, bf16[448,128]{1,0:T(8,128)(2,1)} %collective-permute-done.10.p1_hbm, bf16[448,128]{1,0:T(8,128)(2,1)} %collective-permute-done.11.p2_hbm, bf16[448,128]{1,0:T(8,128)(2,1)} %collective-permute-done.12.p3_hbm, ...), custom_call_target="tpu_custom_call" | custom-call | flops 1024 | bytes 1024 | tf_op jit(solution)/shard_map/deltas/pallas_call | solution.py:326
  67.3 4.4 %all-to-all-start.3 = ((bf16[16,56,1024]{2,1,0:T(8,128)(2,1)}), bf16[16,56,1024]{2,1,0:T(8,128)(2,1)}, u32[]{:S(2)}, u32[]{:S(2)}) async-start(bf16[16,56,1024]{2,1,0:T(8,128)(2,1)} %bitcast.33), calls=%async_computation.3 | async-start | bytes 3670016 | tf_op jit(solution)/shard_map/all_to_all | solution.py:570
  71.8 0.1 collective-permute-start.13
  71.9 1.8 %collective-permute-start.14 = (bf16[256,1024]{1,0:T(8,128)(2,1)}, bf16[256,1024]{1,0:T(8,128)(2,1)}, u32[]{:S(2)}, u32[]{:S(2)}) collective-permute-start(bf16[256,1024]{1,0:T(8,128)(2,1)} %get-tuple-element.115), channel_id=1, source_target_pairs={{0,6},{1,7},{2,0},{3,1},{4,2},{5,3},{6,4},{7,5},{8,14},{9,15},{10,... | collective-permute-start | bytes 1572872 | tf_op jit(solution)/shard_map/ppermute | solution.py:560
  73.7 0.3 collective-permute-start.15
  74.0 0.5 collective-permute-start.16
  74.5 2.7 %collective-permute-start.17 = (bf16[256,1024]{1,0:T(8,128)(2,1)}, bf16[256,1024]{1,0:T(8,128)(2,1)}, u32[]{:S(2)}, u32[]{:S(2)}) collective-permute-start(bf16[256,1024]{1,0:T(8,128)(2,1)} %get-tuple-element.118), channel_id=1, source_target_pairs={{0,6},{1,7},{2,0},{3,1},{4,2},{5,3},{6,4},{7,5},{8,14},{9,15},{10,... | collective-permute-start | bytes 1572872 | tf_op jit(solution)/shard_map/ppermute | solution.py:560
  77.2 1.4 %slice_reduce_fusion = bf16[]{:T(256)} fusion(bf16[16,56,1024]{2,1,0:T(8,128)(2,1)} %bitcast.14), kind=kLoop, calls=%fused_computation.2 | loop fusion | flops 15 | bytes 34 | tf_op jit(solution)/shard_map/reduce_max | solution.py:604
  79.2 2.1 %picks.2.pick_hbm = bf16[512,896]{1,0:T(8,128)(2,1)} custom-call(s32[1]{0:T(128)} %constant.3.clone.1.turn_ref, s32[1,512]{1,0:T(1,128)} %bitcast.36), custom_call_target="tpu_custom_call" | custom-call | flops 1024 | bytes 1024 | tf_op jit(solution)/shard_map/picks/pallas_call | solution.py:492
  81.4 0.0 collective-permute-done.13.refs_0_
  81.4 5.6 %collective-permute-done.14.refs_1_ = bf16[256,1024]{1,0:T(8,128)(2,1)} collective-permute-done((bf16[256,1024]{1,0:T(8,128)(2,1)}, bf16[256,1024]{1,0:T(8,128)(2,1)}, u32[]{:S(2)}, u32[]{:S(2)}) %collective-permute-start.14) | collective-permute-done | bytes 524320 | tf_op jit(solution)/shard_map/ppermute | solution.py:560
  87.0 3.0 %collective-permute-done.15.refs_2_ = bf16[256,1024]{1,0:T(8,128)(2,1)} collective-permute-done((bf16[256,1024]{1,0:T(8,128)(2,1)}, bf16[256,1024]{1,0:T(8,128)(2,1)}, u32[]{:S(2)}, u32[]{:S(2)}) %collective-permute-start.15) | collective-permute-done | bytes 524320 | tf_op jit(solution)/shard_map/ppermute | solution.py:560
  90.0 4.2 %mine.5.base_hbm = bf16[512,1024]{1,0:T(8,128)(2,1)} custom-call(bf16[512,1024]{1,0:T(8,128)(2,1)} %get-tuple-element.186.att_hbm, bf16[1024,8192]{1,0:T(8,128)(2,1)} %w_hbm.9, bf16[512,1024]{1,0:T(8,128)(2,1)} %collective-permute-done.13.refs_0_, bf16[256,1024]{1,0:T(8,128)(2,1)} %collective-permute-done.14.refs_1_, ...), custom_call_target="tpu_custom_call" | custom-call | flops 1024 | bytes 1024 | tf_op jit(solution)/shard_map/mine/pallas_call | solution.py:437
  94.2 6.2 %collective-permute-done.16.refs_0_ = bf16[256,1024]{1,0:T(8,128)(2,1)} collective-permute-done((bf16[256,1024]{1,0:T(8,128)(2,1)}, bf16[256,1024]{1,0:T(8,128)(2,1)}, u32[]{:S(2)}, u32[]{:S(2)}) %collective-permute-start.16) | collective-permute-done | bytes 524320 | tf_op jit(solution)/shard_map/ppermute | solution.py:560
  100.5 0.0 collective-permute-done.17.refs_1_
  100.5 0.0 all-to-all-done.3
  100.5 4.1 %finish.2 = bf16[512,1024]{1,0:T(8,128)(2,1)} custom-call(bf16[512,896]{1,0:T(8,128)(2,1)} %picks.2.pick_hbm, bf16[896,1024]{1,0:T(8,128)(2,1)} %bitcast.13.back_hbm, bf16[512,1024]{1,0:T(8,128)(2,1)} %mine.5.base_hbm, bf16[256,1024]{1,0:T(8,128)(2,1)} %collective-permute-done.16.refs_0_, bf16[256,1024]{1,0:T(8,128)(2,1)} %collective-permute-done.17.refs_1_), custom_call_target="tpu_custom_call" | custom-call | flops 1024 | bytes 1024 | tf_op jit(solution)/shard_map/finish/pallas_call | solution.py:530
  (1 shorter events, 0.0 us)
Async XLA Ops:
  7.5 36.2 %all-to-all-start.2 = ((bf16[16,56,1024]{2,1,0:T(8,128)(2,1)}), bf16[16,56,1024]{2,1,0:T(8,128)(2,1)}, u32[]{:S(2)}, u32[]{:S(2)}) async-start(bf16[16,56,1024]{2,1,0:T(8,128)(2,1)} %bitcast.34), calls=%async_computation.2 | async-start | bytes 3670016 | tf_op jit(solution)/shard_map/all_to_all | solution.py:570
  19.6 7.5 %collective-permute-start.7 = (bf16[512,1024]{1,0:T(8,128)(2,1)}, bf16[512,1024]{1,0:T(8,128)(2,1)}, u32[]{:S(2)}, u32[]{:S(2)}) collective-permute-start(bf16[512,1024]{1,0:T(8,128)(2,1)} %theirs.3), channel_id=1, source_target_pairs={{0,1},{1,0},{2,3},{3,2},{4,5},{5,4},{6,7},{7,6},{8,9},{9,8},{10,11... | collective-permute-start | bytes 3145736 | tf_op jit(solution)/shard_map/ppermute | solution.py:560
  26.4 8.0 %collective-permute-start.4 = (bf16[512,1024]{1,0:T(8,128)(2,1)}, bf16[512,1024]{1,0:T(8,128)(2,1)}, u32[]{:S(2)}, u32[]{:S(2)}) collective-permute-start(bf16[512,1024]{1,0:T(8,128)(2,1)} %get-tuple-element.84), channel_id=1, source_target_pairs={{0,1},{1,0},{2,3},{3,2},{4,5},{5,4},{6,7},{7,6},{8,9},{9,8},{10,11... | collective-permute-start | bytes 3145736 | tf_op jit(solution)/shard_map/ppermute | solution.py:560
  27.0 7.4 %collective-permute-start.5 = (bf16[512,1024]{1,0:T(8,128)(2,1)}, bf16[512,1024]{1,0:T(8,128)(2,1)}, u32[]{:S(2)}, u32[]{:S(2)}) collective-permute-start(bf16[512,1024]{1,0:T(8,128)(2,1)} %get-tuple-element.85), channel_id=1, source_target_pairs={{0,1},{1,0},{2,3},{3,2},{4,5},{5,4},{6,7},{7,6},{8,9},{9,8},{10,11... | collective-permute-start | bytes 3145736 | tf_op jit(solution)/shard_map/ppermute | solution.py:560
  31.1 21.0 %collective-permute-start.8 = (bf16[256,1024]{1,0:T(8,128)(2,1)}, bf16[256,1024]{1,0:T(8,128)(2,1)}, u32[]{:S(2)}, u32[]{:S(2)}) collective-permute-start(bf16[256,1024]{1,0:T(8,128)(2,1)} %get-tuple-element.94), channel_id=1, source_target_pairs={{0,2},{1,3},{2,4},{3,5},{4,6},{5,7},{6,0},{7,1},{8,10},{9,11},{10,... | collective-permute-start | bytes 1572872 | tf_op jit(solution)/shard_map/ppermute | solution.py:560
  32.7 19.4 %collective-permute-start.9 = (bf16[256,1024]{1,0:T(8,128)(2,1)}, bf16[256,1024]{1,0:T(8,128)(2,1)}, u32[]{:S(2)}, u32[]{:S(2)}) collective-permute-start(bf16[256,1024]{1,0:T(8,128)(2,1)} %get-tuple-element.95), channel_id=1, source_target_pairs={{0,6},{1,7},{2,0},{3,1},{4,2},{5,3},{6,4},{7,5},{8,14},{9,15},{10,... | collective-permute-start | bytes 1572872 | tf_op jit(solution)/shard_map/ppermute | solution.py:560
  48.9 1.6 %collective-permute-start.6 = (bf16[448,128]{1,0:T(8,128)(2,1)}, bf16[448,128]{1,0:T(8,128)(2,1)S(1)}, u32[]{:S(2)}, u32[]{:S(2)}) collective-permute-start(bf16[448,128]{1,0:T(8,128)(2,1)} %get-tuple-element.91), channel_id=1, source_target_pairs={{0,1},{1,0},{2,3},{3,2},{4,5},{5,4},{6,7},{7,6},{8,9},{9,8},{10,11... | collective-permute-start | bytes 344072 | tf_op jit(solution)/shard_map/ppermute | solution.py:560
  52.1 7.6 %collective-permute-start.12 = (bf16[448,128]{1,0:T(8,128)(2,1)}, bf16[448,128]{1,0:T(8,128)(2,1)}, u32[]{:S(2)}, u32[]{:S(2)}) collective-permute-start(bf16[448,128]{1,0:T(8,128)(2,1)} %add_convert_fusion.1.p0_hbm), channel_id=1, source_target_pairs={{0,4},{1,5},{2,6},{3,7},{4,0},{5,1},{6,2},{7,3},{8,12},{9,13},{10,... | collective-permute-start | bytes 344072 | tf_op jit(solution)/shard_map/ppermute | solution.py:560
  55.1 6.5 %collective-permute-start.11 = (bf16[448,128]{1,0:T(8,128)(2,1)}, bf16[448,128]{1,0:T(8,128)(2,1)}, u32[]{:S(2)}, u32[]{:S(2)}) collective-permute-start(bf16[448,128]{1,0:T(8,128)(2,1)} %add_convert_fusion.1.p0_hbm), channel_id=1, source_target_pairs={{0,6},{1,7},{2,0},{3,1},{4,2},{5,3},{6,4},{7,5},{8,14},{9,15},{10,... | collective-permute-start | bytes 344072 | tf_op jit(solution)/shard_map/ppermute | solution.py:560
  56.2 6.3 %collective-permute-start.10 = (bf16[448,128]{1,0:T(8,128)(2,1)}, bf16[448,128]{1,0:T(8,128)(2,1)}, u32[]{:S(2)}, u32[]{:S(2)}) collective-permute-start(bf16[448,128]{1,0:T(8,128)(2,1)} %add_convert_fusion.1.p0_hbm), channel_id=1, source_target_pairs={{0,2},{1,3},{2,4},{3,5},{4,6},{5,7},{6,0},{7,1},{8,10},{9,11},{10,... | collective-permute-start | bytes 344072 | tf_op jit(solution)/shard_map/ppermute | solution.py:560
  67.3 33.1 %all-to-all-start.3 = ((bf16[16,56,1024]{2,1,0:T(8,128)(2,1)}), bf16[16,56,1024]{2,1,0:T(8,128)(2,1)}, u32[]{:S(2)}, u32[]{:S(2)}) async-start(bf16[16,56,1024]{2,1,0:T(8,128)(2,1)} %bitcast.33), calls=%async_computation.3 | async-start | bytes 3670016 | tf_op jit(solution)/shard_map/all_to_all | solution.py:570
  71.8 9.6 %collective-permute-start.13 = (bf16[512,1024]{1,0:T(8,128)(2,1)}, bf16[512,1024]{1,0:T(8,128)(2,1)}, u32[]{:S(2)}, u32[]{:S(2)}) collective-permute-start(bf16[512,1024]{1,0:T(8,128)(2,1)} %get-tuple-element.114), channel_id=1, source_target_pairs={{0,1},{1,0},{2,3},{3,2},{4,5},{5,4},{6,7},{7,6},{8,9},{9,8},{10,11... | collective-permute-start | bytes 3145736 | tf_op jit(solution)/shard_map/ppermute | solution.py:560
  71.9 15.1 %collective-permute-start.14 = (bf16[256,1024]{1,0:T(8,128)(2,1)}, bf16[256,1024]{1,0:T(8,128)(2,1)}, u32[]{:S(2)}, u32[]{:S(2)}) collective-permute-start(bf16[256,1024]{1,0:T(8,128)(2,1)} %get-tuple-element.115), channel_id=1, source_target_pairs={{0,6},{1,7},{2,0},{3,1},{4,2},{5,3},{6,4},{7,5},{8,14},{9,15},{10,... | collective-permute-start | bytes 1572872 | tf_op jit(solution)/shard_map/ppermute | solution.py:560
  73.7 16.3 %collective-permute-start.15 = (bf16[256,1024]{1,0:T(8,128)(2,1)}, bf16[256,1024]{1,0:T(8,128)(2,1)}, u32[]{:S(2)}, u32[]{:S(2)}) collective-permute-start(bf16[256,1024]{1,0:T(8,128)(2,1)} %get-tuple-element.116), channel_id=1, source_target_pairs={{0,2},{1,3},{2,4},{3,5},{4,6},{5,7},{6,0},{7,1},{8,10},{9,11},{10,... | collective-permute-start | bytes 1572872 | tf_op jit(solution)/shard_map/ppermute | solution.py:560
  74.0 26.5 %collective-permute-start.16 = (bf16[256,1024]{1,0:T(8,128)(2,1)}, bf16[256,1024]{1,0:T(8,128)(2,1)}, u32[]{:S(2)}, u32[]{:S(2)}) collective-permute-start(bf16[256,1024]{1,0:T(8,128)(2,1)} %get-tuple-element.117), channel_id=1, source_target_pairs={{0,2},{1,3},{2,4},{3,5},{4,6},{5,7},{6,0},{7,1},{8,10},{9,11},{10,... | collective-permute-start | bytes 1572872 | tf_op jit(solution)/shard_map/ppermute | solution.py:560
  74.5 26.0 %collective-permute-start.17 = (bf16[256,1024]{1,0:T(8,128)(2,1)}, bf16[256,1024]{1,0:T(8,128)(2,1)}, u32[]{:S(2)}, u32[]{:S(2)}) collective-permute-start(bf16[256,1024]{1,0:T(8,128)(2,1)} %get-tuple-element.118), channel_id=1, source_target_pairs={{0,6},{1,7},{2,0},{3,1},{4,2},{5,3},{6,4},{7,5},{8,14},{9,15},{10,... | collective-permute-start | bytes 1572872 | tf_op jit(solution)/shard_map/ppermute | solution.py:560
